TPU v7x, 128 devices: a whole 4x4x4 slice. The times are simulated.
128 devices in a mesh: row: 8 (over y_lo, z), col: 16 (over x, y_hi, core).
Axes of the slice: x: 4, y: 4 (y_hi: 2, y_lo: 2; y = y_hi * 2 + y_lo), z: 4, core: 2. Of those that a mesh axis runs over, the one named last changes fastest.
Arguments:
- pair: bfloat16 [768, 768, 128], P(('row', 'col')), may hold values from -1000 to 1000
- residue_mask: int32 [768], replicated, may hold values from 0 to 1, as said below
- ln_gain: float32 [128], replicated, may hold values from 0.1 to 1.9
- ln_shift: float32 [128], replicated, may hold values from -3 to 3
- w_query: bfloat16 [128, 128], replicated, may hold values from -0.5 to 0.5
- w_key: bfloat16 [128, 128], replicated, may hold values from -0.5 to 0.5
- w_value: bfloat16 [128, 128], replicated, may hold values from -0.5 to 0.5
- w_gate: bfloat16 [128, 128], replicated, may hold values from -0.5 to 0.5
- gate_shift: float32 [128], replicated, may hold values from -4 to 4
- w_bias: bfloat16 [128, 4], replicated, may hold values from -40 to 40
- w_out: bfloat16 [128, 128], replicated, may hold values from -0.5 to 0.5
- out_shift: float32 [128], replicated, may hold values from -3 to 3
Outputs:
- update: bfloat16 [768, 768, 128], P(('row', 'col'))
Inputs may be any that keep to these rules, and one draw needn't show every extreme that they name: `residue_mask`: 1 on a leading run of residues and 0 on the remaining 768//16 to 192 residues.
All inputs are finite; a program needn't handle non-finite values.
Results may differ from a plain program's by a relative error of at most 0.035.
The roundings to bfloat16 on the way count: a program that leaves them out, or rounds other values in their place, can miss the bound.
Values may be sent and summed in bfloat16 or wider, within the bound.
No kernel may reach another device: no remote copies, remote signals or barrier semaphores. Data moves between devices by JAX's collectives and lax.ppermute only.
A program may use at most 64 MiB of HBM per device.

v0:
```python
import jax
import jax.numpy as jnp
from jax import lax
from jax.sharding import PartitionSpec as P


def normalize(pair, ln_gain, ln_shift):
    values_f = pair.astype(jnp.float32)
    center = jnp.mean(values_f, axis=-1, keepdims=True)
    centered = values_f - center
    spread = jnp.mean(centered * centered, axis=-1, keepdims=True)
    scaled = centered * lax.rsqrt(spread + 1e-05) * ln_gain + ln_shift
    return scaled.astype(jnp.bfloat16)


def project(normed, w_query, w_key, w_value, w_gate, gate_shift):
    queries = jnp.einsum(
        "...c,cd->...d", normed, w_query, preferred_element_type=jnp.float32
    ).astype(jnp.bfloat16)
    keys_all = jnp.einsum(
        "...c,cd->...d", normed, w_key, preferred_element_type=jnp.float32
    ).astype(jnp.bfloat16)
    values_all = jnp.einsum(
        "...c,cd->...d", normed, w_value, preferred_element_type=jnp.float32
    ).astype(jnp.bfloat16)
    gate_lin = jnp.einsum("...c,cd->...d", normed, w_gate, preferred_element_type=jnp.float32)
    gate = jax.nn.sigmoid(gate_lin + gate_shift).astype(jnp.bfloat16)
    return (queries, keys_all, values_all, gate)


def to_columns(local):
    return lax.all_to_all(local, ("row", "col"), split_axis=1, concat_axis=0, tiled=True)


def to_rows(local):
    return lax.all_to_all(local, ("row", "col"), split_axis=0, concat_axis=1, tiled=True)


def attend(
    queries, keys_all, values_all, gate, residue_mask, bias_sel, head_count, head_dim, device
):
    length, own_rows, channels = queries.shape
    width = head_count * head_dim
    blocks = max(1, length // 512)
    block = length // blocks
    scale = head_dim ** (-0.5)

    def one_column(column, gathered):
        flag = lax.dynamic_index_in_dim(residue_mask, device * own_rows + column, 0, keepdims=False)
        valid = (residue_mask * flag > 0)[None, :, None]
        query_col = lax.dynamic_index_in_dim(queries, column, 1, keepdims=False).reshape(
            length, head_count, head_dim
        )
        key_col = lax.dynamic_index_in_dim(keys_all, column, 1, keepdims=False).reshape(
            length, head_count, head_dim
        )
        value_col = lax.dynamic_index_in_dim(values_all, column, 1, keepdims=False).reshape(
            length, head_count, head_dim
        )
        gate_col = lax.dynamic_index_in_dim(gate, column, 1, keepdims=False)
        scores = jnp.einsum("ihd,khd->hki", query_col, key_col, preferred_element_type=jnp.float32)
        scores = scores * scale + bias_sel.astype(jnp.float32)
        scores = jnp.where(valid, scores, -1000000000.0)
        highest = jnp.max(scores, axis=1, keepdims=True)
        exponent = jnp.exp(scores - highest)
        weights = (exponent / jnp.sum(exponent, axis=1, keepdims=True)).astype(jnp.bfloat16)
        attended = jnp.einsum(
            "hki,khd->ihd", weights, value_col, preferred_element_type=jnp.float32
        ).reshape(block, width)
        pieces = [(gate_col.astype(jnp.float32) * attended).astype(jnp.bfloat16)]
        gated_col = jnp.concatenate(pieces, axis=0)
        return lax.dynamic_update_index_in_dim(gathered, gated_col, column, 1)

    return lax.fori_loop(
        0, own_rows, one_column, jnp.zeros((length, own_rows, width), jnp.bfloat16)
    )


def on_device(
    pair,
    residue_mask,
    ln_gain,
    ln_shift,
    w_query,
    w_key,
    w_value,
    w_gate,
    gate_shift,
    w_bias,
    w_out,
    out_shift,
):
    own_rows, length, channels = pair.shape
    head_count = w_bias.shape[1]
    head_dim = channels // head_count
    normed = normalize(pair, ln_gain, ln_shift)
    bias_local = jnp.einsum(
        "jnc,ch->hjn", normed, w_bias, preferred_element_type=jnp.float32
    ).astype(jnp.bfloat16)
    moved = to_columns(normed)
    queries, keys_all, values_all, gate = project(
        moved, w_query, w_key, w_value, w_gate, gate_shift
    )
    device = lax.axis_index("row") * lax.axis_size("col") + lax.axis_index("col")
    bias_all = lax.all_gather(bias_local, ("row", "col"), axis=1, tiled=True)
    gated = attend(
        queries, keys_all, values_all, gate, residue_mask, bias_all, head_count, head_dim, device
    )
    update = jnp.einsum("ijc,cd->ijd", gated, w_out, preferred_element_type=jnp.float32) + out_shift
    return to_rows(update.astype(jnp.bfloat16))


def solution(mesh):
    placed = (P(("row", "col"), None, None), P(), P(), P(), P(), P(), P(), P(), P(), P(), P(), P())
    return jax.shard_map(
        on_device,
        mesh=mesh,
        in_specs=placed,
        out_specs=P(("row", "col"), None, None),
        check_vma=False,
    )
```

profile of v0, /device:TPU:0, one launch (start us, length us, event | category | flops | bytes accessed | tf_op | source)
XLA Modules:
  0.0 448.7 jit_solution(3485207723200173787)
XLA Ops:
  8.9 8.1 %fusion.8 = f32[6,768]{0,1:T(8,128)S(1)} fusion(bf16[6,768,128]{2,1,0:T(8,128)(2,1)S(1)} %copy-done.1, f32[6,768]{0,1:T(8,128)S(1)} %broadcast_multiply_fusion), kind=kLoop, calls=%fused_computation.20 | loop fusion | flops 2354688 | bytes 1216512 | tf_op jit(solution)/shard_map/reduce_sum | solution.py:11
  17.1 8.7 %fusion.11 = bf16[6,768,128]{2,0,1:T(8,128)(2,1)} fusion(bf16[6,768,128]{2,1,0:T(8,128)(2,1)S(1)} %copy-done.1, f32[128]{0:T(128)S(1)} %copy-done.6, f32[128]{0:T(128)S(1)} %copy-done.7, f32[6,768]{0,1:T(8,128)S(1)} %add_rsqrt_fusion, f32[6,768]{0,1:T(8,128)S(1)} %broadcast_multiply_fusion), kind=kLoop, calls=%fused_computation.23 | loop fusion | flops 3538944 | bytes 2397184 | tf_op jit(solution)/shard_map/convert_element_type | solution.py:13
  28.3 11.3 %all-to-all-start = ((bf16[6,768,128]{2,0,1:T(8,128)(2,1)}), bf16[6,768,128]{2,0,1:T(8,128)(2,1)S(1)}, u32[]{:S(2)}, u32[]{:S(2)}) async-start(bf16[6,768,128]{2,0,1:T(8,128)(2,1)} %fusion.11), calls=%async_computation | async-start | bytes 3145728 | tf_op jit(solution)/shard_map/all_to_all | solution.py:32
  39.7 23.6 %all-to-all-done = bf16[6,768,128]{2,0,1:T(8,128)(2,1)S(1)} async-done(((bf16[6,768,128]{2,0,1:T(8,128)(2,1)}), bf16[6,768,128]{2,0,1:T(8,128)(2,1)S(1)}, u32[]{:S(2)}, u32[]{:S(2)}) %all-to-all-start) | async-done | bytes 1179680 | tf_op jit(solution)/shard_map/all_to_all | solution.py:32
  69.4 171.6 %all-gather.2.cloned.1.call-done = bf16[4,768,768]{2,0,1:T(4,128)(2,1)} async-done(((bf16[4,6,768]{2,0,1:T(4,128)(2,1)}), bf16[4,768,768]{2,0,1:T(4,128)(2,1)}) %all-gather.2.cloned.1.call-update) | async-done | bytes 4718608 | tf_op jit(solution)/shard_map/all_gather | solution.py:105
  246.1 159.9 %while.15 = (s32[]{:T(128)}, bf16[768,6,128]{0,2,1:T(8,128)(2,1)}, bf16[768,6,128]{2,0,1:T(8,128)(2,1)}, bf16[768,6,128]{2,0,1:T(8,128)(2,1)}, s32[]{:T(128)}, /...) while((s32[]{:T(128)}, bf16[768,6,128]{0,2,1:T(8,128)(2,1)}, ...), condition=%wide.region_5.6_spmd, body=%wide.region_2.5_spmd.sunk | while | flops 483956736 | bytes 33650616 | solution.py:74
  248.5 8.1 %add_select_fusion.2 = f32[4,768,768]{2,1,0:T(8,128)} fusion(bf16[4,768,768]{2,1,0:T(8,128)(2,1)} %get-tuple-element.344, pred[768]{0:T(1024)(128)(4,1)S(1)} %multiply_compare_fusion.2, bf16[768,4,32]{0,2,1:T(8,128)(2,1)S(1)} %bitcast.71, bf16[768,4,32]{0,2,1:T(8,128)(2,1)S(1)} %bitcast.73), kind=kOutput, calls=%fused_computation.3.clone.2 | convolution fusion | flops 160432128 | bytes 14549760 | tf_op jit(solution)/shard_map/while/body/eval_jaxpr/ihd,khd->hki/dot_general | solution.py:61
  256.6 5.5 %fusion.52 = f32[4,768]{1,0:T(4,128)S(1)} fusion(bf16[4,768,768]{2,1,0:T(8,128)(2,1)} %get-tuple-element.344, pred[768]{0:T(1024)(128)(4,1)S(1)} %multiply_compare_fusion.2, bf16[768,4,32]{0,2,1:T(8,128)(2,1)S(1)} %bitcast.72, bf16[768,4,32]{0,2,1:T(8,128)(2,1)S(1)} %bitcast.74), kind=kOutput, calls=%fused_computation.41.clone.1 | convolution fusion | flops 165151488 | bytes 5124864 | tf_op jit(solution)/shard_map/while/body/eval_jaxpr/sub | solution.py:65
  263.4 8.5 %fusion.53 = f32[4,32,768]{2,1,0:T(8,128)S(1)} fusion(bf16[768,4,32]{0,2,1:T(8,128)(2,1)S(1)} %bitcast.77, f32[4,768]{1,0:T(4,128)S(1)} %fusion.52, f32[4,768,768]{2,1,0:T(8,128)} %add_select_fusion.2), kind=kOutput, calls=%fused_computation.4.clone.1 | convolution fusion | flops 158076672 | bytes 10039296 | tf_op jit(solution)/shard_map/while/body/eval_jaxpr/hki,khd->ihd/dot_general | solution.py:67
  275.2 8.1 %add_select_fusion.2 = f32[4,768,768]{2,1,0:T(8,128)} fusion(bf16[4,768,768]{2,1,0:T(8,128)(2,1)} %get-tuple-element.344, pred[768]{0:T(1024)(128)(4,1)S(1)} %multiply_compare_fusion.2, bf16[768,4,32]{0,2,1:T(8,128)(2,1)S(1)} %bitcast.71, bf16[768,4,32]{0,2,1:T(8,128)(2,1)S(1)} %bitcast.73), kind=kOutput, calls=%fused_computation.3.clone.2 | convolution fusion | flops 160432128 | bytes 14549760 | tf_op jit(solution)/shard_map/while/body/eval_jaxpr/ihd,khd->hki/dot_general | solution.py:61
  283.3 5.5 %fusion.52 = f32[4,768]{1,0:T(4,128)S(1)} fusion(bf16[4,768,768]{2,1,0:T(8,128)(2,1)} %get-tuple-element.344, pred[768]{0:T(1024)(128)(4,1)S(1)} %multiply_compare_fusion.2, bf16[768,4,32]{0,2,1:T(8,128)(2,1)S(1)} %bitcast.72, bf16[768,4,32]{0,2,1:T(8,128)(2,1)S(1)} %bitcast.74), kind=kOutput, calls=%fused_computation.41.clone.1 | convolution fusion | flops 165151488 | bytes 5124864 | tf_op jit(solution)/shard_map/while/body/eval_jaxpr/sub | solution.py:65
  290.0 8.5 %fusion.53 = f32[4,32,768]{2,1,0:T(8,128)S(1)} fusion(bf16[768,4,32]{0,2,1:T(8,128)(2,1)S(1)} %bitcast.77, f32[4,768]{1,0:T(4,128)S(1)} %fusion.52, f32[4,768,768]{2,1,0:T(8,128)} %add_select_fusion.2), kind=kOutput, calls=%fused_computation.4.clone.1 | convolution fusion | flops 158076672 | bytes 10039296 | tf_op jit(solution)/shard_map/while/body/eval_jaxpr/hki,khd->ihd/dot_general | solution.py:67
  301.8 8.1 %add_select_fusion.2 = f32[4,768,768]{2,1,0:T(8,128)} fusion(bf16[4,768,768]{2,1,0:T(8,128)(2,1)} %get-tuple-element.344, pred[768]{0:T(1024)(128)(4,1)S(1)} %multiply_compare_fusion.2, bf16[768,4,32]{0,2,1:T(8,128)(2,1)S(1)} %bitcast.71, bf16[768,4,32]{0,2,1:T(8,128)(2,1)S(1)} %bitcast.73), kind=kOutput, calls=%fused_computation.3.clone.2 | convolution fusion | flops 160432128 | bytes 14549760 | tf_op jit(solution)/shard_map/while/body/eval_jaxpr/ihd,khd->hki/dot_general | solution.py:61
  309.9 5.5 %fusion.52 = f32[4,768]{1,0:T(4,128)S(1)} fusion(bf16[4,768,768]{2,1,0:T(8,128)(2,1)} %get-tuple-element.344, pred[768]{0:T(1024)(128)(4,1)S(1)} %multiply_compare_fusion.2, bf16[768,4,32]{0,2,1:T(8,128)(2,1)S(1)} %bitcast.72, bf16[768,4,32]{0,2,1:T(8,128)(2,1)S(1)} %bitcast.74), kind=kOutput, calls=%fused_computation.41.clone.1 | convolution fusion | flops 165151488 | bytes 5124864 | tf_op jit(solution)/shard_map/while/body/eval_jaxpr/sub | solution.py:65
  316.7 8.5 %fusion.53 = f32[4,32,768]{2,1,0:T(8,128)S(1)} fusion(bf16[768,4,32]{0,2,1:T(8,128)(2,1)S(1)} %bitcast.77, f32[4,768]{1,0:T(4,128)S(1)} %fusion.52, f32[4,768,768]{2,1,0:T(8,128)} %add_select_fusion.2), kind=kOutput, calls=%fused_computation.4.clone.1 | convolution fusion | flops 158076672 | bytes 10039296 | tf_op jit(solution)/shard_map/while/body/eval_jaxpr/hki,khd->ihd/dot_general | solution.py:67
  328.5 8.1 %add_select_fusion.2 = f32[4,768,768]{2,1,0:T(8,128)} fusion(bf16[4,768,768]{2,1,0:T(8,128)(2,1)} %get-tuple-element.344, pred[768]{0:T(1024)(128)(4,1)S(1)} %multiply_compare_fusion.2, bf16[768,4,32]{0,2,1:T(8,128)(2,1)S(1)} %bitcast.71, bf16[768,4,32]{0,2,1:T(8,128)(2,1)S(1)} %bitcast.73), kind=kOutput, calls=%fused_computation.3.clone.2 | convolution fusion | flops 160432128 | bytes 14549760 | tf_op jit(solution)/shard_map/while/body/eval_jaxpr/ihd,khd->hki/dot_general | solution.py:61
  343.3 8.5 %fusion.53 = f32[4,32,768]{2,1,0:T(8,128)S(1)} fusion(bf16[768,4,32]{0,2,1:T(8,128)(2,1)S(1)} %bitcast.77, f32[4,768]{1,0:T(4,128)S(1)} %fusion.52, f32[4,768,768]{2,1,0:T(8,128)} %add_select_fusion.2), kind=kOutput, calls=%fused_computation.4.clone.1 | convolution fusion | flops 158076672 | bytes 10039296 | tf_op jit(solution)/shard_map/while/body/eval_jaxpr/hki,khd->ihd/dot_general | solution.py:67
  355.1 8.1 %add_select_fusion.2 = f32[4,768,768]{2,1,0:T(8,128)} fusion(bf16[4,768,768]{2,1,0:T(8,128)(2,1)} %get-tuple-element.344, pred[768]{0:T(1024)(128)(4,1)S(1)} %multiply_compare_fusion.2, bf16[768,4,32]{0,2,1:T(8,128)(2,1)S(1)} %bitcast.71, bf16[768,4,32]{0,2,1:T(8,128)(2,1)S(1)} %bitcast.73), kind=kOutput, calls=%fused_computation.3.clone.2 | convolution fusion | flops 160432128 | bytes 14549760 | tf_op jit(solution)/shard_map/while/body/eval_jaxpr/ihd,khd->hki/dot_general | solution.py:61
  363.2 5.5 %fusion.52 = f32[4,768]{1,0:T(4,128)S(1)} fusion(bf16[4,768,768]{2,1,0:T(8,128)(2,1)} %get-tuple-element.344, pred[768]{0:T(1024)(128)(4,1)S(1)} %multiply_compare_fusion.2, bf16[768,4,32]{0,2,1:T(8,128)(2,1)S(1)} %bitcast.72, bf16[768,4,32]{0,2,1:T(8,128)(2,1)S(1)} %bitcast.74), kind=kOutput, calls=%fused_computation.41.clone.1 | convolution fusion | flops 165151488 | bytes 5124864 | tf_op jit(solution)/shard_map/while/body/eval_jaxpr/sub | solution.py:65
  370.0 8.5 %fusion.53 = f32[4,32,768]{2,1,0:T(8,128)S(1)} fusion(bf16[768,4,32]{0,2,1:T(8,128)(2,1)S(1)} %bitcast.77, f32[4,768]{1,0:T(4,128)S(1)} %fusion.52, f32[4,768,768]{2,1,0:T(8,128)} %add_select_fusion.2), kind=kOutput, calls=%fused_computation.4.clone.1 | convolution fusion | flops 158076672 | bytes 10039296 | tf_op jit(solution)/shard_map/while/body/eval_jaxpr/hki,khd->ihd/dot_general | solution.py:67
  381.8 8.1 %add_select_fusion.2 = f32[4,768,768]{2,1,0:T(8,128)} fusion(bf16[4,768,768]{2,1,0:T(8,128)(2,1)} %get-tuple-element.344, pred[768]{0:T(1024)(128)(4,1)S(1)} %multiply_compare_fusion.2, bf16[768,4,32]{0,2,1:T(8,128)(2,1)S(1)} %bitcast.71, bf16[768,4,32]{0,2,1:T(8,128)(2,1)S(1)} %bitcast.73), kind=kOutput, calls=%fused_computation.3.clone.2 | convolution fusion | flops 160432128 | bytes 14549760 | tf_op jit(solution)/shard_map/while/body/eval_jaxpr/ihd,khd->hki/dot_general | solution.py:61
  389.9 5.5 %fusion.52 = f32[4,768]{1,0:T(4,128)S(1)} fusion(bf16[4,768,768]{2,1,0:T(8,128)(2,1)} %get-tuple-element.344, pred[768]{0:T(1024)(128)(4,1)S(1)} %multiply_compare_fusion.2, bf16[768,4,32]{0,2,1:T(8,128)(2,1)S(1)} %bitcast.72, bf16[768,4,32]{0,2,1:T(8,128)(2,1)S(1)} %bitcast.74), kind=kOutput, calls=%fused_computation.41.clone.1 | convolution fusion | flops 165151488 | bytes 5124864 | tf_op jit(solution)/shard_map/while/body/eval_jaxpr/sub | solution.py:65
  396.6 8.5 %fusion.53 = f32[4,32,768]{2,1,0:T(8,128)S(1)} fusion(bf16[768,4,32]{0,2,1:T(8,128)(2,1)S(1)} %bitcast.77, f32[4,768]{1,0:T(4,128)S(1)} %fusion.52, f32[4,768,768]{2,1,0:T(8,128)} %add_select_fusion.2), kind=kOutput, calls=%fused_computation.4.clone.1 | convolution fusion | flops 158076672 | bytes 10039296 | tf_op jit(solution)/shard_map/while/body/eval_jaxpr/hki,khd->ihd/dot_general | solution.py:67
  408.6 31.7 %all_to_all.36 = bf16[768,6,128]{2,1,0:T(8,128)(2,1)S(1)} all-to-all(bf16[768,6,128]{2,1,0:T(8,128)(2,1)S(1)} %copy.28), channel_id=1, replica_groups=mesh['row'=8,'col'=16] {'row','col'}, dimensions={0} | all-to-all | bytes 2359296 | tf_op jit(solution)/shard_map/all_to_all | solution.py:36
  (97 shorter events, 52.5 us)
Async XLA Ops:
  6.5 57.5 %copy-start = (bf16[128,128]{1,0:T(8,128)(2,1)S(1)}, bf16[128,128]{1,0:T(8,128)(2,1)}, u32[]{:S(2)}) copy-start(bf16[128,128]{1,0:T(8,128)(2,1)} %param.18) | copy-start | bytes 98308
  6.5 2.4 copy-start.1
  6.5 10.6 %copy-start.7 = (f32[128]{0:T(128)S(1)}, f32[128]{0:T(128)}, u32[]{:S(2)}) copy-start(f32[128]{0:T(128)} %param.16) | copy-start | bytes 1540
  6.5 10.6 %copy-start.6 = (f32[128]{0:T(128)S(1)}, f32[128]{0:T(128)}, u32[]{:S(2)}) copy-start(f32[128]{0:T(128)} %param.17) | copy-start | bytes 1540
  6.5 234.4 %all-gather.2.cloned.1.call-start = ((), (), s32[]{:S(2)}) async-start(), calls=%async_computation.2 | async-start | bytes 4755456 | tf_op jit(solution)/shard_map/all_gather | solution.py:105
  17.0 8.8 %copy-start.10 = (bf16[128,4]{0,1:T(4,128)(2,1)S(1)}, bf16[128,4]{0,1:T(4,128)(2,1)}, u32[]{:S(2)}) copy-start(bf16[128,4]{0,1:T(4,128)(2,1)} %param.23) | copy-start | bytes 3076
  28.3 35.0 %all-to-all-start = ((bf16[6,768,128]{2,0,1:T(8,128)(2,1)}), bf16[6,768,128]{2,0,1:T(8,128)(2,1)S(1)}, u32[]{:S(2)}, u32[]{:S(2)}) async-start(bf16[6,768,128]{2,0,1:T(8,128)(2,1)} %fusion.11), calls=%async_computation | async-start | bytes 3145728 | tf_op jit(solution)/shard_map/all_to_all | solution.py:32
  63.6 1.0 copy-start.3
  64.1 2.0 copy-start.4
  64.6 3.0 copy-start.9
  64.6 3.0 copy-start.11
  69.4 176.7 %copy-start.2 = (s32[768]{0:T(1024)S(1)}, s32[768]{0:T(1024)}, u32[]{:S(2)}) copy-start(s32[768]{0:T(1024)} %param.15) | copy-start | bytes 9220
  246.1 159.9 %copy-start.5 = (bf16[128,128]{1,0:T(8,128)(2,1)S(1)}, bf16[128,128]{1,0:T(8,128)(2,1)}, u32[]{:S(2)}) copy-start(bf16[128,128]{1,0:T(8,128)(2,1)} %param.24) | copy-start | bytes 98308
  246.1 159.9 %copy-start.8 = (f32[128]{0:T(128)S(1)}, f32[128]{0:T(128)}, u32[]{:S(2)}) copy-start(f32[128]{0:T(128)} %param.25) | copy-start | bytes 1540
Sparse Core Ops, SparseCore 0:
  28.5 212.4 all-gather.1
where the time goes:
time: 451 us; the launch traced here: 449 us
  waiting for transfers between devices  195 us (43%)
  matrix products  142 us (31%)
  blocking collectives  31.7 us (7%)
  local copies, waits for them, and re-layouts  27.4 us (6%)
  other arithmetic  26.9 us (6%)
  between operations  13.6 us (3%)
  starting transfers between devices  11.4 us (3%)
    all_gather x1, waiting for transfers between devices, on_device(): bias_all = lax.all_gather(bias_local, ('row', 'col'), axis=1, tiled=True)  172 us
    dot_general x6, matrix products, one_column(): jnp.einsum('hki,khd->ihd', weights, value_col, preferred_element_type=jnp...  51.2 us
    dot_general x6, matrix products, one_column(): jnp.einsum('ihd,khd->hki', query_col, key_col, preferred_element_type=jnp...  48.6 us
    sub x6, matrix products, one_column(): exponent = jnp.exp(scores - highest)  33.2 us
    all_to_all x1, blocking collectives, to_rows(): lax.all_to_all(local, ('row', 'col'), split_axis=0, concat_axis=1, tiled=...  31.7 us
    all_to_all x1, waiting for transfers between devices, to_columns(): lax.all_to_all(local, ('row', 'col'), split_axis=1, concat_axis=0, tiled=...  23.6 us
    all_to_all x1, starting transfers between devices, to_columns(): lax.all_to_all(local, ('row', 'col'), split_axis=1, concat_axis=0, tiled=...  11.3 us
  transfers between devices with their start and end apart: 2, of which 2 were waited for; matrix products, arithmetic and copies ran while one was open for 1% of the time, Pallas kernels for 0%

commit v1 on v0

v1 whole, which is shorter than its diff:
```python
import math

import jax
import jax.numpy as jnp
from jax import lax
from jax.experimental import pallas as pl
from jax.experimental.pallas import tpu as pltpu
from jax.sharding import Mesh, PartitionSpec as P

BF = jnp.bfloat16
F32 = jnp.float32
CHIPS = ("row", "chip")
PLACES = ("row", "chip", "core")
HEADS = 4
DIM = 32
LOG2E = math.log2(math.e)
VMEM_BYTES = 56 * 1024 * 1024

NT = (((1,), (1,)), ((), ()))
TN = (((0,), (0,)), ((), ()))


def layer_norm(x, gain, shift):
    center = jnp.mean(x, axis=-1, keepdims=True)
    centered = x - center
    spread = jnp.mean(centered * centered, axis=-1, keepdims=True)
    return centered * lax.rsqrt(spread + 1e-05) * gain + shift


def bias_kernel(where_ref, pair_ref, gain_ref, shift_ref, wb_ref, own_ref, send_ref, norm_ref, rows_ref):
    own_rows, length, _ = pair_ref.shape
    chips = length // (2 * own_rows)
    core = where_ref[0]
    gain, shift, wb = gain_ref[...], shift_ref[...], wb_ref[...]
    part = length // 4
    for r in range(own_rows):
        for p in range(4):
            x = pair_ref[r, p * part : (p + 1) * part, :].astype(F32)
            norm_ref[r, p * part : (p + 1) * part, :] = layer_norm(x, gain, shift)
    for side, out_ref in ((0, own_ref), (1, send_ref)):
        half = core if side == 0 else 1 - core
        for r in range(own_rows):
            piece = [
                norm_ref[r, pl.ds(half * own_rows + q, chips, stride=2 * own_rows), :]
                for q in range(own_rows)
            ]
            cols = jnp.concatenate(piece, axis=0).astype(BF)
            rows_ref[r * HEADS : (r + 1) * HEADS, :] = lax.dot_general(
                wb, cols, NT, preferred_element_type=F32
            )
        out_ref[...] = rows_ref[...].astype(BF)


def bias_call(where, pair, gain, shift, wb):
    own_rows, length, channels = pair.shape
    half = length // 2
    shape = jax.ShapeDtypeStruct((own_rows * HEADS, half), BF)
    vm = pl.BlockSpec(memory_space=pltpu.VMEM)
    return pl.pallas_call(
        bias_kernel,
        out_shape=(shape, shape),
        in_specs=[pl.BlockSpec(memory_space=pltpu.SMEM), vm, vm, vm, vm],
        out_specs=(vm, vm),
        scratch_shapes=[
            pltpu.VMEM((own_rows, length, channels), F32),
            pltpu.VMEM((own_rows * HEADS, half), F32),
        ],
        compiler_params=pltpu.CompilerParams(vmem_limit_bytes=VMEM_BYTES),
        name="bias_rows",
    )(where, pair, gain, shift, wb)


def columns_kernel(got_ref, gain_ref, shift_ref, wq_ref, wk_ref, wv_ref, wg_ref, gs_ref,
                   cols_ref, qhi_ref, qlo_ref, key_ref, val_ref, gate_ref, norm_ref):
    total = got_ref.shape[0]
    columns, half, channels = cols_ref.shape
    rows = half // 64
    group = columns * rows
    gain, shift = gain_ref[...], shift_ref[...]
    step = 256

    def norm(i, _):
        at = pl.ds(pl.multiple_of(i * step, step), step)
        norm_ref[at, :] = layer_norm(got_ref[at, :].astype(F32), gain, shift)
        return 0

    lax.fori_loop(0, total // step, norm, 0, unroll=2)
    scale = LOG2E * DIM ** (-0.5)

    def column(t, _):
        piece = [norm_ref[pl.ds(r * columns + t, 64, stride=group), :] for r in range(rows)]
        cols = jnp.concatenate(piece, axis=0).astype(BF)
        cols_ref[t] = cols
        query = lax.dot_general(wq_ref[...], cols, NT, preferred_element_type=F32)
        query = query.astype(BF).astype(F32) * scale
        high = query.astype(BF)
        qhi_ref[t] = high
        qlo_ref[t] = (query - high.astype(F32)).astype(BF)
        key_ref[t] = jnp.dot(cols, wk_ref[...], preferred_element_type=F32).astype(BF)
        val_ref[t] = lax.dot_general(wv_ref[...], cols, NT, preferred_element_type=F32).astype(BF)
        lin = lax.dot_general(wg_ref[...], cols, NT, preferred_element_type=F32) + gs_ref[...]
        gate_ref[t] = jax.nn.sigmoid(lin).astype(BF)
        return 0

    lax.fori_loop(0, columns, column, 0)


def columns_call(got, gain, shift, wq, wk, wv, wg, gs, columns):
    total, channels = got.shape
    half = total // columns
    vm = pl.BlockSpec(memory_space=pltpu.VMEM)
    by_row = jax.ShapeDtypeStruct((columns, half, channels), BF)
    by_channel = jax.ShapeDtypeStruct((columns, channels, half), BF)
    key = jax.ShapeDtypeStruct((columns, half, 2 * channels), BF)
    return pl.pallas_call(
        columns_kernel,
        out_shape=(by_row, by_channel, by_channel, key, by_channel, by_channel),
        in_specs=[vm] * 8,
        out_specs=(vm,) * 6,
        scratch_shapes=[pltpu.VMEM((total, channels), F32)],
        compiler_params=pltpu.CompilerParams(vmem_limit_bytes=VMEM_BYTES),
        name="own_columns",
    )(got, gain, shift, wq, wk, wv, wg, gs)


def other_kernel(cols_ref, wk_ref, wv_ref, key_ref, val_ref):
    def column(t, _):
        cols = cols_ref[t]
        key_ref[t] = jnp.dot(cols, wk_ref[...], preferred_element_type=F32).astype(BF)
        val_ref[t] = lax.dot_general(wv_ref[...], cols, NT, preferred_element_type=F32).astype(BF)
        return 0

    lax.fori_loop(0, cols_ref.shape[0], column, 0)


def other_call(cols, wk, wv):
    columns, half, channels = cols.shape
    vm = pl.BlockSpec(memory_space=pltpu.VMEM)
    return pl.pallas_call(
        other_kernel,
        out_shape=(
            jax.ShapeDtypeStruct((columns, half, 2 * channels), BF),
            jax.ShapeDtypeStruct((columns, channels, half), BF),
        ),
        in_specs=[vm] * 3,
        out_specs=(vm,) * 2,
        compiler_params=pltpu.CompilerParams(vmem_limit_bytes=VMEM_BYTES),
        name="other_columns",
    )(cols, wk, wv)


def attend_kernel(where_ref, bias_ref, qhi_ref, qlo_ref, key0_ref, key1_ref, val0_ref, val1_ref, gate_ref,
                  wo_ref, os_ref, out_ref, raw_ref, add_ref, q_ref, s_ref, e_ref, att_ref, upd_ref):
    t = pl.program_id(0)
    columns = pl.num_programs(0)
    core, chip, count = where_ref[0], where_ref[1], where_ref[2]
    channels, half = gate_ref.shape[1:]
    rows = half // 64
    length = 2 * half
    sources = length // (2 * rows)
    packed = 2 * rows * HEADS

    @pl.when(t == 0)
    def _():
        def widen(i, _):
            at = pl.ds(pl.multiple_of(i * 64, 64), 64)
            wide = bias_ref[at, :].astype(F32) * LOG2E
            for n in range(half // 128):
                raw_ref[n, at, :] = wide[:, n * 128 : (n + 1) * 128]
            return 0

        lax.fori_loop(0, bias_ref.shape[0] // 64, widen, 0)

        def arrange(i, _):
            side, r = i // rows, i % rows
            place = lax.broadcasted_iota(jnp.int32, (64, 128), 0)
            real_side = jnp.where(side == 0, core, 1 - core)
            valid = place * (2 * rows) + (real_side * rows + r) < count
            at = pl.ds(pl.multiple_of(i * 64, 64), 64)
            for h in range(HEADS):
                for n in range(half // 128):
                    rows_in = raw_ref[n, pl.ds(i * HEADS + h, 64, stride=packed), :]
                    add_ref[h, at, n * 128 : (n + 1) * 128] = jnp.where(valid, rows_in, -1e9)
            return 0

        lax.fori_loop(0, 2 * rows, arrange, 0)
        q_ref[...] = jnp.zeros_like(q_ref)

    real = t * sources + chip < count

    @pl.when(real)
    def _():
        for h in range(HEADS):
            mine = slice(h * DIM, (h + 1) * DIM)
            q_ref[h, mine, :] = qhi_ref[0, mine, :]
            q_ref[h, channels + h * DIM : channels + (h + 1) * DIM, :] = qlo_ref[0, mine, :]
        for h in range(HEADS):
            mine = slice(h * DIM, (h + 1) * DIM)
            s0 = jnp.dot(key0_ref[0], q_ref[h], preferred_element_type=F32) + add_ref[h, :half, :]
            s1 = jnp.dot(key1_ref[0], q_ref[h], preferred_element_type=F32) + add_ref[h, half:, :]
            top = jnp.maximum(jnp.max(s0, axis=0, keepdims=True), jnp.max(s1, axis=0, keepdims=True))
            e0 = jnp.exp2(s0 - top)
            e1 = jnp.exp2(s1 - top)
            total = jnp.sum(e0, axis=0, keepdims=True) + jnp.sum(e1, axis=0, keepdims=True)
            got = jnp.dot(val0_ref[0, mine, :], e0.astype(BF), preferred_element_type=F32)
            got += jnp.dot(val1_ref[0, mine, :], e1.astype(BF), preferred_element_type=F32)
            att_ref[mine, :] = got / total

    @pl.when(jnp.logical_not(real))
    def _():
        weight = F32(1.0 / length).astype(BF).astype(F32)
        both = jnp.sum(val0_ref[0].astype(F32), axis=1, keepdims=True)
        both += jnp.sum(val1_ref[0].astype(F32), axis=1, keepdims=True)
        att_ref[...] = jnp.broadcast_to(both * weight, att_ref.shape)

    gated = (gate_ref[0].astype(F32) * att_ref[...]).astype(BF)
    update = lax.dot_general(gated, wo_ref[...], TN, preferred_element_type=F32) + os_ref[...]
    for r in range(rows):
        upd_ref[pl.ds(r * columns + t, 64, stride=rows * columns), :] = update[r * 64 : (r + 1) * 64, :]

    @pl.when(t == columns - 1)
    def _():
        def narrow(i, _):
            at = pl.ds(pl.multiple_of(i * 256, 256), 256)
            out_ref[at, :] = upd_ref[at, :].astype(BF)
            return 0

        lax.fori_loop(0, out_ref.shape[0] // 256, narrow, 0)


def attend_call(where, bias, qhi, qlo, key0, key1, val0, val1, gate, wo, os):
    columns, channels, half = gate.shape
    whole = lambda a: pl.BlockSpec(a.shape, lambda t: (0,) * a.ndim)
    one = lambda a: pl.BlockSpec((1,) + a.shape[1:], lambda t: (t, 0, 0))
    out_rows = columns * half
    return pl.pallas_call(
        attend_kernel,
        grid=(columns,),
        out_shape=jax.ShapeDtypeStruct((out_rows, channels), BF),
        in_specs=[pl.BlockSpec(memory_space=pltpu.SMEM), whole(bias), one(qhi), one(qlo), one(key0), one(key1),
                  one(val0), one(val1), one(gate), whole(wo), whole(os)],
        out_specs=pl.BlockSpec((out_rows, channels), lambda t: (0, 0)),
        scratch_shapes=[
            pltpu.VMEM((half // 128, bias.shape[0], 128), F32),
            pltpu.VMEM((HEADS, 2 * half, half), F32),
            pltpu.VMEM((HEADS, 2 * channels, half), BF),
            pltpu.VMEM((8, half), F32),
            pltpu.VMEM((8, half), F32),
            pltpu.VMEM((channels, half), F32),
            pltpu.VMEM((out_rows, channels), F32),
        ],
        compiler_params=pltpu.CompilerParams(vmem_limit_bytes=VMEM_BYTES),
        name="attend",
    )(where, bias, qhi, qlo, key0, key1, val0, val1, gate, wo, os)


def on_device(pair, residue_mask, ln_gain, ln_shift, w_query, w_key, w_value, w_gate, gate_shift,
              w_bias, w_out, out_shift):
    own_rows, length, channels = pair.shape
    half = length // 2
    chips = length // (2 * own_rows)
    columns = length // chips
    core = lax.axis_index("core")
    chip = lax.axis_index("row") * lax.axis_size("chip") + lax.axis_index("chip")
    where = jnp.stack([core, chip, jnp.sum(residue_mask)]).astype(jnp.int32)
    gain, shift = ln_gain.reshape(1, channels), ln_shift.reshape(1, channels)
    swap = [(0, 1), (1, 0)]

    sent = pair.reshape(own_rows * columns, chips, channels).transpose(1, 0, 2)
    got = lax.all_to_all(sent, CHIPS, split_axis=0, concat_axis=0, tiled=True)
    bias_own, bias_send = bias_call(where, pair, gain, shift, w_bias.T)
    bias_other = lax.ppermute(bias_send, "core", swap)
    message = jnp.concatenate([bias_own, bias_other], axis=0)
    copies = jnp.broadcast_to(message[None], (chips,) + message.shape)
    bias = lax.all_to_all(copies, CHIPS, split_axis=0, concat_axis=0, tiled=True)
    bias = bias.reshape(-1, half)

    wk2 = jnp.concatenate([w_key, w_key], axis=1)
    wv = w_value.T
    cols, qhi, qlo, key0, val0, gate = columns_call(
        got.reshape(-1, channels), gain, shift, w_query.T, wk2, wv, w_gate.T,
        gate_shift.reshape(channels, 1), columns)
    other = lax.ppermute(cols, "core", swap)
    key1, val1 = other_call(other, wk2, wv)
    out = attend_call(where, bias, qhi, qlo, key0, key1, val0, val1, gate, w_out, out_shift.reshape(1, channels))
    back = lax.all_to_all(out.reshape(chips, own_rows * columns, channels), CHIPS, split_axis=0, concat_axis=0, tiled=True)
    return back.transpose(1, 0, 2).reshape(own_rows, length, channels)


def solution(mesh):
    rows, cols = mesh.devices.shape
    fine = Mesh(mesh.devices.reshape(rows, cols // 2, 2), PLACES)
    placed = (P(PLACES, None, None),) + (P(),) * 11
    return jax.shard_map(
        on_device,
        mesh=fine,
        in_specs=placed,
        out_specs=P(PLACES, None, None),
        check_vma=False,
    )
```

time: 451 us -> 134 us (0.30)
  waiting for transfers between devices: 195 us -> 21.9 us
  matrix products: 142 us -> 0 us
  Pallas kernels: 0 us -> 55.3 us
  other arithmetic: 26.9 us -> 2.68 us
  local copies, waits for them, and re-layouts: 27.4 us -> 12.2 us
  between operations: 13.6 us -> 0.09 us
  blocking collectives: 31.7 us -> 24.1 us
  starting transfers between devices: 11.4 us -> 17 us
    all_gather x1 -> x0, waiting for transfers between devices: 172 us -> none  [on_device(): bias_all = lax.all_gather(bias_local, ('row', 'col'), axis=1, tiled=True)]
    dot_general x18 -> x0, matrix products: 109 us -> none  [the longest x6 51.2 us: one_column(): jnp.einsum('hki,khd->ihd', weights, value_col, preferred_element_type=jnp...]
    pallas_call x0 -> x4, Pallas kernels: none -> 55.3 us  [the longest x1 34.6 us: attend_call(): pl.pallas_call(attend_kernel, grid=(columns,), out_shape=jax.ShapeDtypeSt...]
    sub x6 -> x0, matrix products: 33.2 us -> none  [one_column(): exponent = jnp.exp(scores - highest)]
    dynamic_slice x42 -> x0, local copies, waits for them, and re-layouts: 19.1 us -> none  [the longest x12 7.2 us: one_column(): lax.dynamic_index_in_dim(values_all, column, 1, keepdims=False)]
    reduce_sum x2 -> x1, other arithmetic: 10.4 us -> 0.65 us  [on_device(): where = jnp.stack([core, chip, jnp.sum(residue_mask)]).astype(jnp.int32)]
    convert_element_type x1 -> x0, other arithmetic: 8.71 us -> none  [normalize(): return scaled.astype(jnp.bfloat16)]
    all_to_all x1, blocking collectives: 31.7 us -> 24.1 us  [on_device(): lax.all_to_all(out.reshape(chips, own_rows * columns, channels), CHIPS, s...]
  transfers between devices with their start and end apart: 2 -> 4, of which waited for: 2 -> 4; matrix products, arithmetic and copies ran while one was open for 1% -> 4% of each run, Pallas kernels for 0% -> 16%
where the time goes in v1:
time: 134 us; the launch traced here: 133 us
  Pallas kernels  55.3 us (41%)
  blocking collectives  24.1 us (18%)
  waiting for transfers between devices  21.9 us (16%)
  starting transfers between devices  17 us (13%)
  local copies, waits for them, and re-layouts  12.2 us (9%)
  other arithmetic  2.68 us (2%)
    pallas_call x1, Pallas kernels, attend_call(): pl.pallas_call(attend_kernel, grid=(columns,), out_shape=jax.ShapeDtypeSt...  34.6 us
    all_to_all x1, blocking collectives, on_device(): lax.all_to_all(out.reshape(chips, own_rows * columns, channels), CHIPS, s...  24.1 us
    all_to_all x1, starting transfers between devices, on_device(): got = lax.all_to_all(sent, CHIPS, split_axis=0, concat_axis=0, tiled=True)  11.6 us
    all_to_all x1, waiting for transfers between devices, on_device(): got = lax.all_to_all(sent, CHIPS, split_axis=0, concat_axis=0, tiled=True)  11.3 us
    pallas_call x1, Pallas kernels, columns_call(): pl.pallas_call(columns_kernel, out_shape=(by_row, by_channel, by_channel,...  10.4 us
    all_to_all x1, waiting for transfers between devices, on_device(): lax.all_to_all(copies, CHIPS, split_axis=0, concat_axis=0, tiled=True)  6.16 us
    pallas_call x1, Pallas kernels, other_call(): pl.pallas_call(other_kernel, out_shape=(jax.ShapeDtypeStruct((columns, ha...  6 us
    all_to_all x1, starting transfers between devices, on_device(): lax.all_to_all(copies, CHIPS, split_axis=0, concat_axis=0, tiled=True)  5.37 us
  transfers between devices with their start and end apart: 4, of which 4 were waited for; matrix products, arithmetic and copies ran while one was open for 4% of the time, Pallas kernels for 16%

profile of v1, /device:TPU:0, one launch (start us, length us, event | category | flops | bytes accessed | tf_op | source)
XLA Modules:
  0.0 133.2 jit_solution(9279440941387392170)
XLA Ops:
  0.0 3.0 %copy.20 = bf16[72,64,128]{2,0,1:T(8,128)(2,1)} copy(bf16[72,64,128]{2,1,0:T(8,128)(2,1)} %bitcast.22) | data formatting | bytes 2359296 | tf_op jit(solution)/shard_map/reshape | solution.py:269
  3.0 11.6 %all-to-all-start.1 = ((bf16[64,72,128]{2,1,0:T(8,128)(2,1)}), bf16[64,72,128]{2,1,0:T(8,128)(2,1)S(1)}, u32[]{:S(2)}, u32[]{:S(2)}) async-start(bf16[64,72,128]{2,1,0:T(8,128)(2,1)} %bitcast.19), calls=%async_computation.1 | async-start | bytes 2359296 | tf_op jit(solution)/shard_map/all_to_all | solution.py:270
  14.7 0.7 reduce_sum.9
  15.4 1.3 pad_add_fusion.where_ref
  16.7 4.3 %bias_rows.1 = (bf16[24,384]{1,0:T(8,128)(2,1)}, bf16[24,384]{1,0:T(8,128)(2,1)}) custom-call(s32[3]{0:T(128)} %pad_add_fusion.where_ref, bf16[6,768,128]{2,1,0:T(8,128)(2,1)} %pair_ref.1, f32[1,128]{1,0:T(1,128)} %bitcast.29, f32[1,128]{1,0:T(1,128)} %bitcast.31, bf16[4,128]{1,0:T(4,128)(2,1)} %bitcast.33), custom_call_target="tpu_custom_call" | custom-call | tf_op jit(solution)/shard_map/bias_rows/pallas_call | solution.py:59
  21.0 1.4 %collective-permute-done = bf16[24,384]{1,0:T(8,128)(2,1)S(1)} collective-permute-done((bf16[24,384]{1,0:T(8,128)(2,1)}, bf16[24,384]{1,0:T(8,128)(2,1)S(1)}, u32[]{:S(2)}, u32[]{:S(2)}) %collective-permute-start) | collective-permute-done | bytes 18464 | tf_op jit(solution)/shard_map/ppermute | solution.py:272
  22.4 0.7 pad_maximum_fusion
  23.1 11.3 %all-to-all-done.1 = bf16[64,72,128]{2,1,0:T(8,128)(2,1)S(1)} async-done(((bf16[64,72,128]{2,1,0:T(8,128)(2,1)}), bf16[64,72,128]{2,1,0:T(8,128)(2,1)S(1)}, u32[]{:S(2)}, u32[]{:S(2)}) %all-to-all-start.1) | async-done | bytes 1179680 | tf_op jit(solution)/shard_map/all_to_all | solution.py:270
  34.4 1.8 %broadcast_in_dim.2 = bf16[64,48,384]{2,1,0:T(8,128)(2,1)} broadcast(bf16[48,384]{1,0:T(8,128)(2,1)S(1)} %pad_maximum_fusion), dimensions={1,2} | broadcast | bytes 2396160 | tf_op jit(solution)/shard_map/broadcast_in_dim | solution.py:274
  36.2 5.4 %all-to-all-start = ((bf16[64,48,384]{2,1,0:T(8,128)(2,1)}), bf16[64,48,384]{2,1,0:T(8,128)(2,1)S(1)}, u32[]{:S(2)}, u32[]{:S(2)}) async-start(bf16[64,48,384]{2,1,0:T(8,128)(2,1)} %broadcast_in_dim.2), calls=%async_computation | async-start | bytes 4718592 | tf_op jit(solution)/shard_map/all_to_all | solution.py:275
  41.6 0.7 copy.14
  42.3 0.7 copy.15
  43.1 0.7 copy.16
  43.8 0.7 copy.17.gs_ref
  44.6 0.6 copy-done.3
  45.2 10.4 %own_columns.1 = (bf16[12,384,128]{2,1,0:T(8,128)(2,1)}, bf16[12,128,384]{2,1,0:T(8,128)(2,1)}, bf16[12,128,384]{2,1,0:T(8,128)(2,1)}, bf16[12,384,256]{2,1,0:T(...) custom-call(bf16[4608,128]{1,0:T(8,128)(2,1)} %bitcast.23, f32[1,128]{1,0:T(1,128)} %bitcast.30, ...), custom_call_target="tpu_custom_call" | custom-call | tf_op jit(solution)/shard_map/own_columns/pallas_call | solution.py:115
  55.6 3.1 %collective-permute-done.1.cols_ref = bf16[12,384,128]{2,1,0:T(8,128)(2,1)S(1)} collective-permute-done((bf16[12,384,128]{2,1,0:T(8,128)(2,1)}, bf16[12,384,128]{2,1,0:T(8,128)(2,1)S(1)}, u32[]{:S(2)}, u32[]{:S(2)}) %collective-permute-start.1) | collective-permute-done | bytes 1179680 | tf_op jit(solution)/shard_map/ppermute | solution.py:283
  58.7 1.0 copy-done.2
  59.7 6.0 %other_columns.1 = (bf16[12,384,256]{2,1,0:T(8,128)(2,1)}, bf16[12,128,384]{2,1,0:T(8,128)(2,1)}) custom-call(bf16[12,384,128]{2,1,0:T(8,128)(2,1)} %copy-done.2, bf16[128,256]{1,0:T(8,128)(2,1)} %copy-done.3, bf16[128,128]{1,0:T(8,128)(2,1)} %bitcast.26), custom_call_target="tpu_custom_call" | custom-call | tf_op jit(solution)/shard_map/other_columns/pallas_call | solution.py:139
  65.7 6.2 %all-to-all-done = bf16[64,48,384]{2,1,0:T(8,128)(2,1)S(1)} async-done(((bf16[64,48,384]{2,1,0:T(8,128)(2,1)}), bf16[64,48,384]{2,1,0:T(8,128)(2,1)S(1)}, u32[]{:S(2)}, u32[]{:S(2)}) %all-to-all-start) | async-done | bytes 2359328 | tf_op jit(solution)/shard_map/all_to_all | solution.py:275
  71.8 1.4 %copy-done = bf16[64,48,384]{2,1,0:T(8,128)(2,1)} copy-done((bf16[64,48,384]{2,1,0:T(8,128)(2,1)}, bf16[64,48,384]{2,1,0:T(8,128)(2,1)S(1)}, u32[]{:S(2)}) %copy-start) | copy-done | bytes 2359320
  73.3 34.6 %attend.1 = bf16[4608,128]{1,0:T(8,128)(2,1)} custom-call(s32[3]{0:T(128)} %pad_add_fusion.where_ref, bf16[3072,384]{1,0:T(8,128)(2,1)} %bitcast.20, bf16[12,128,384]{2,1,0:T(8,128)(2,1)} %get-tuple-element.17.qhi_ref, bf16[12,128,384]{2,1,0:T(8,128)(2,1)} %get-tuple-element.18.qlo_ref, bf16[12,384,256]{2,1,0:T(8,128)(2,1)} %get-tuple-element.19.key0_ref, ...), custom_call_target="tpu_custom_call" | custom-call | tf_op jit(solution)/shard_map/attend/pallas_call | solution.py:236
  107.8 24.1 %all_to_all.15 = bf16[64,72,128]{2,1,0:T(8,128)(2,1)S(1)} all-to-all(bf16[64,72,128]{2,1,0:T(8,128)(2,1)} %bitcast.21), channel_id=1, replica_groups=mesh['row'=8,'chip'=8,'core'=2] {'row','chip'}, dimensions={0} | all-to-all | bytes 2359296 | tf_op jit(solution)/shard_map/all_to_all | solution.py:286
  131.9 1.3 copy.18
  (21 shorter events, 0.1 us)
Async XLA Ops:
  3.0 11.6 %copy-start.8 = (s32[768]{0:T(1024)S(1)}, s32[768]{0:T(1024)}, u32[]{:S(2)}) copy-start(s32[768]{0:T(1024)} %param.13) | copy-start | bytes 9220
  3.0 31.4 %all-to-all-start.1 = ((bf16[64,72,128]{2,1,0:T(8,128)(2,1)}), bf16[64,72,128]{2,1,0:T(8,128)(2,1)S(1)}, u32[]{:S(2)}, u32[]{:S(2)}) async-start(bf16[64,72,128]{2,1,0:T(8,128)(2,1)} %bitcast.19), calls=%async_computation.1 | async-start | bytes 2359296 | tf_op jit(solution)/shard_map/all_to_all | solution.py:270
  21.0 1.4 %collective-permute-start = (bf16[24,384]{1,0:T(8,128)(2,1)}, bf16[24,384]{1,0:T(8,128)(2,1)S(1)}, u32[]{:S(2)}, u32[]{:S(2)}) collective-permute-start(bf16[24,384]{1,0:T(8,128)(2,1)} %get-tuple-element.16), channel_id=1, source_target_pairs={{0,1},{1,0},{2,3},{3,2},{4,5},{5,4},{6,7},{7,6},{8,9},{9,8},{10,11... | collective-permute-start | bytes 55304 | tf_op jit(solution)/shard_map/ppermute | solution.py:272
  34.4 1.8 %copy-start.1 = (bf16[64,72,128]{2,1,0:T(8,128)(2,1)}, bf16[64,72,128]{2,1,0:T(8,128)(2,1)S(1)}, u32[]{:S(2)}) copy-start(bf16[64,72,128]{2,1,0:T(8,128)(2,1)S(1)} %all-to-all-done.1) | copy-start | bytes 3538948
  36.2 5.4 %copy-start.5 = (bf16[128,128]{1,0:T(8,128)(2,1)S(1)}, bf16[128,128]{1,0:T(8,128)(2,1)}, u32[]{:S(2)}) copy-start(bf16[128,128]{1,0:T(8,128)(2,1)} %param.16) | copy-start | bytes 98308
  36.2 6.1 %copy-start.6 = (bf16[128,128]{1,0:T(8,128)(2,1)S(1)}, bf16[128,128]{1,0:T(8,128)(2,1)}, u32[]{:S(2)}) copy-start(bf16[128,128]{1,0:T(8,128)(2,1)} %param.18) | copy-start | bytes 98308
  36.2 6.9 %copy-start.7 = (bf16[128,128]{1,0:T(8,128)(2,1)S(1)}, bf16[128,128]{1,0:T(8,128)(2,1)}, u32[]{:S(2)}) copy-start(bf16[128,128]{1,0:T(8,128)(2,1)} %param.19) | copy-start | bytes 98308
  36.2 7.6 %copy-start.9 = (f32[128]{0:T(128)S(1)}, f32[128]{0:T(128)}, u32[]{:S(2)}) copy-start(f32[128]{0:T(128)} %param.20) | copy-start | bytes 1540
  36.2 8.3 %copy-start.4 = (bf16[128,128]{1,0:T(8,128)(2,1)S(1)}, bf16[128,128]{1,0:T(8,128)(2,1)}, u32[]{:S(2)}) copy-start(bf16[128,128]{1,0:T(8,128)(2,1)} %param.17) | copy-start | bytes 98308
  36.2 35.6 %all-to-all-start = ((bf16[64,48,384]{2,1,0:T(8,128)(2,1)}), bf16[64,48,384]{2,1,0:T(8,128)(2,1)S(1)}, u32[]{:S(2)}, u32[]{:S(2)}) async-start(bf16[64,48,384]{2,1,0:T(8,128)(2,1)} %broadcast_in_dim.2), calls=%async_computation | async-start | bytes 4718592 | tf_op jit(solution)/shard_map/all_to_all | solution.py:275
  44.5 0.6 copy-start.3
  55.6 3.1 %collective-permute-start.1 = (bf16[12,384,128]{2,1,0:T(8,128)(2,1)}, bf16[12,384,128]{2,1,0:T(8,128)(2,1)S(1)}, u32[]{:S(2)}, u32[]{:S(2)}) collective-permute-start(bf16[12,384,128]{2,1,0:T(8,128)(2,1)} %get-tuple-element.20), channel_id=1, source_target_pairs={{0,1},{1,0},{2,3},{3,2},{4,5},{5,4},{6,7},{7,6},{8,9},{9,8},{10,11... | collective-permute-start | bytes 3538952 | tf_op jit(solution)/shard_map/ppermute | solution.py:283
  58.7 1.0 copy-start.2
  71.8 1.4 %copy-start = (bf16[64,48,384]{2,1,0:T(8,128)(2,1)}, bf16[64,48,384]{2,1,0:T(8,128)(2,1)S(1)}, u32[]{:S(2)}) copy-start(bf16[64,48,384]{2,1,0:T(8,128)(2,1)S(1)} %all-to-all-done) | copy-start | bytes 7077892

commit v2 on v0

v2 whole, which is shorter than its diff:
```python
import math

import jax
import jax.numpy as jnp
from jax import lax
from jax.experimental import pallas as pl
from jax.experimental.pallas import tpu as pltpu
from jax.sharding import Mesh, PartitionSpec as P

BF = jnp.bfloat16
F32 = jnp.float32
CHIPS = ("ylo", "z", "x", "yhi")
PLACES = CHIPS + ("core",)
RING = 4
HEADS = 4
DIM = 32
LANES = 128
LOG2E = math.log2(math.e)

NT = (((1,), (1,)), ((), ()))
TN = (((0,), (0,)), ((), ()))
VM = pl.BlockSpec(memory_space=pltpu.VMEM)
ANY = pl.BlockSpec(memory_space=pl.ANY)


def room(mib):
    return pltpu.CompilerParams(vmem_limit_bytes=mib * 1024 * 1024)


def held(a):
    return pltpu.with_memory_space_constraint(a, pltpu.VMEM)


def away(a):
    return pltpu.with_memory_space_constraint(a, pltpu.HBM)


def in_vmem(shape):
    return pltpu.VMEM(shape, BF)


def layer_norm(x, gain, shift):
    center = jnp.mean(x, axis=-1, keepdims=True)
    centered = x - center
    spread = jnp.mean(centered * centered, axis=-1, keepdims=True)
    return centered * lax.rsqrt(spread + 1e-05) * gain + shift


def bias_kernel(pair_ref, gain_ref, shift_ref, wb_ref, own_ref, send_ref, norm_ref, cols_ref, rows_ref):
    own_rows, length, channels = pair_ref.shape
    chips = length // (2 * own_rows)
    core = lax.axis_index("core")
    gain, shift, wb = gain_ref[...], shift_ref[...], wb_ref[...]
    step = 256
    for r in range(own_rows):
        for p in range(length // step):
            x = pair_ref[r, p * step : (p + 1) * step, :].astype(F32)
            norm_ref[r * length + p * step : r * length + (p + 1) * step, :] = layer_norm(x, gain, shift)

    for side, out_ref in ((0, own_ref), (1, send_ref)):
        half = core if side == 0 else 1 - core
        rows_ref[...] = jnp.zeros_like(rows_ref)
        for r in range(own_rows):
            for q in range(own_rows):
                cols_ref[r % 2, pl.ds(q, chips, stride=own_rows), :] = norm_ref[
                    pl.ds(r * length + half * own_rows + q, chips, stride=2 * own_rows), :
                ]
            row = lax.dot_general(wb, cols_ref[r % 2].astype(BF), NT, preferred_element_type=F32)
            at = r * 2 * HEADS + side * HEADS
            for n in range(row.shape[1] // LANES):
                rows_ref[n, at : at + HEADS, :] = row[:, n * LANES : (n + 1) * LANES]
        out_ref[...] = rows_ref[...].astype(BF)


def bias_call(pair, gain, shift, wb):
    own_rows, length, channels = pair.shape
    half = length // 2
    rows = 2 * own_rows * HEADS
    piece = jax.ShapeDtypeStruct((half // LANES, rows, LANES), BF)
    return pl.pallas_call(
        bias_kernel,
        out_shape=(piece, piece),
        in_specs=[VM] * 4,
        out_specs=(VM,) * 2,
        scratch_shapes=[
            pltpu.VMEM((own_rows * length, channels), F32),
            pltpu.VMEM((2, half, channels), F32),
            pltpu.VMEM((half // LANES, rows, LANES), F32),
        ],
        compiler_params=room(10),
        name="bias_rows",
    )(pair, gain, shift, wb)


def copies_kernel(own_ref, other_ref, out_ref):
    thirds, rows, _ = own_ref.shape
    for n in range(thirds):
        block = own_ref[n] + other_ref[n]

        def fill(c, _):
            out_ref[c, n * rows : (n + 1) * rows, :] = block
            return 0

        lax.fori_loop(0, out_ref.shape[0], fill, 0, unroll=4)


def copies_call(own, other, chips):
    thirds, rows, _ = own.shape
    return pl.pallas_call(
        copies_kernel,
        out_shape=jax.ShapeDtypeStruct((chips, thirds * rows, LANES), BF),
        in_specs=[VM, VM],
        out_specs=VM,
        compiler_params=room(8),
        name="copies",
    )(own, other)


def columns_kernel(got_ref, gain_ref, shift_ref, by_source_ref, wide_ref):
    sources, width, channels = got_ref.shape
    columns, half, _ = by_source_ref.shape
    gain, shift = gain_ref[...], shift_ref[...]
    step = 4

    def norm(i, _):
        for s in range(step):
            at = pl.ds(pl.multiple_of((i * step + s) * width, 8), width)
            wide_ref[at, :] = layer_norm(got_ref[i * step + s].astype(F32), gain, shift)
        return 0

    lax.fori_loop(0, sources // step, norm, 0)

    def column(t, _):
        by_source_ref[t] = wide_ref[pl.ds(t, half, stride=columns), :].astype(BF)
        return 0

    lax.fori_loop(0, columns, column, 0, unroll=2)


def columns_call(got, gain, shift, columns):
    sources, width, channels = got.shape
    half = sources * width // columns
    return pl.pallas_call(
        columns_kernel,
        out_shape=in_vmem((columns, half, channels)),
        in_specs=[VM] * 3,
        out_specs=VM,
        scratch_shapes=[pltpu.VMEM((columns * half, channels), F32)],
        compiler_params=room(10),
        name="columns",
    )(got, gain, shift)


def keys_values(cols, wk, wv, key_ref, val_ref, t):
    key_ref[t] = jnp.dot(cols, wk, preferred_element_type=F32).astype(BF)
    value = lax.dot_general(wv, cols, NT, preferred_element_type=F32).astype(BF)
    pairs = val_ref.shape[1]
    step = 2 * DIM
    for p in range(pairs):
        val_ref[t, p, :step, :] = value[p * step : (p + 1) * step, :]
        val_ref[t, p, step:, :] = jnp.ones((val_ref.shape[2] - step, value.shape[1]), BF)


def turned(w_ref):
    return w_ref[...].astype(F32).T.astype(BF)


def own_kernel(cols_ref, wq_ref, wk_ref, wv_ref, wg_ref, gs_ref, qhi_ref, qlo_ref, key_ref, val_ref, gate_ref, gs_wide_ref):
    scale = LOG2E * DIM ** (-0.5)
    wq, wv, wg, wk = turned(wq_ref), turned(wv_ref), turned(wg_ref), wk_ref[...]
    channels, half = gate_ref.shape[1:]
    across = jnp.broadcast_to(gs_ref[...], (channels, channels)).T
    for n in range(half // LANES):
        gs_wide_ref[:, n * LANES : (n + 1) * LANES] = across[:, :LANES]

    def column(t, _):
        cols = cols_ref[t]
        keys_values(cols, wk, wv, key_ref, val_ref, t)
        query = lax.dot_general(wq, cols, NT, preferred_element_type=F32)
        query = query.astype(BF).astype(F32) * scale
        high = query.astype(BF)
        qhi_ref[t] = high
        qlo_ref[t] = (query - high.astype(F32)).astype(BF)
        lin = lax.dot_general(wg, cols, NT, preferred_element_type=F32) + gs_wide_ref[...]
        gate_ref[t] = jax.nn.sigmoid(lin).astype(BF)
        return 0

    lax.fori_loop(0, cols_ref.shape[0], column, 0, unroll=4)


def value_shape(columns, half):
    return jax.ShapeDtypeStruct((columns, HEADS // 2, 2 * DIM + 16, half), BF)


def own_call(cols, wq, wk, wv, wg, gs):
    columns, half, channels = cols.shape
    by_channel = jax.ShapeDtypeStruct((columns, channels, half), BF)
    key = jax.ShapeDtypeStruct((columns, half, channels), BF)
    return pl.pallas_call(
        own_kernel,
        out_shape=(by_channel, by_channel, key, value_shape(columns, half), by_channel),
        in_specs=[VM] * 6,
        out_specs=(VM,) * 5,
        scratch_shapes=[pltpu.VMEM((channels, half), F32)],
        compiler_params=room(14),
        name="own",
    )(cols, wq, wk, wv, wg, gs)


def other_kernel(cols_ref, wk_ref, wv_ref, key_ref, val_ref):
    wk, wv = wk_ref[...], turned(wv_ref)

    def column(t, _):
        keys_values(cols_ref[t], wk, wv, key_ref, val_ref, t)
        return 0

    lax.fori_loop(0, cols_ref.shape[0], column, 0, unroll=4)


def other_call(cols, wk, wv):
    columns, half, channels = cols.shape
    return pl.pallas_call(
        other_kernel,
        out_shape=(jax.ShapeDtypeStruct((columns, half, channels), BF), value_shape(columns, half)),
        in_specs=[VM] * 3,
        out_specs=(VM,) * 2,
        compiler_params=room(12),
        name="other",
    )(cols, wk, wv)


def attend_kernel(mask_ref, bias_ref, *refs):
    far, refs = refs[:8], refs[8:]
    os_ref, out_ref, raw_ref, add_ref, q_ref, score_ref, att_ref, upd_ref = refs[:8]
    here, sems = refs[8:16], refs[16]
    qhi_ref, qlo_ref, key0_ref, key1_ref, val0_ref, val1_ref, gate_ref, wo_ref = here
    copies = [
        pltpu.make_async_copy(there, ref, sems.at[i]) for i, (there, ref) in enumerate(zip(far, here))
    ]
    for copy in copies:
        copy.start()
    core = lax.axis_index("core")
    chip = lax.axis_index(CHIPS)
    columns, channels, half = gate_ref.shape
    parts = half // LANES
    length = 2 * half
    sources = bias_ref.shape[0]
    rows = half // sources
    packed = 2 * rows * HEADS
    pairs = HEADS // 2
    count = jnp.sum(mask_ref[...])

    for n in range(parts):
        def widen(s, _):
            at = pl.ds(pl.multiple_of(s * packed, 8), packed)
            raw_ref[n % 2, at, :] = bias_ref[s, n * packed : (n + 1) * packed, :].astype(F32) * LOG2E
            return 0

        lax.fori_loop(0, sources, widen, 0, unroll=4)
        place = lax.broadcasted_iota(jnp.int32, (half, LANES), 0)
        for side in range(2):
            real = core if side == 0 else 1 - core
            valid = place + (place // rows) * rows + real * rows < count
            for h in range(HEADS):
                got = raw_ref[n % 2, pl.ds(side * HEADS + h, half, stride=2 * HEADS), :]
                add_ref[n, h // 2, side * half : (side + 1) * half, (h % 2) * LANES : (h % 2 + 1) * LANES] = (
                    jnp.where(valid, got, -1e9)
                )
    q_ref[...] = jnp.zeros_like(q_ref)
    units = [(n, p) for n in range(parts) for p in range(pairs)]

    def load_queries(t, slot):
        for n in range(parts):
            at = slice(n * LANES, (n + 1) * LANES)
            for h in range(HEADS):
                mine = slice(h * DIM, (h + 1) * DIM)
                to = slice((h % 2) * LANES, (h % 2 + 1) * LANES)
                q_ref[slot, n, h // 2, mine, to] = qhi_ref[t, mine, at]
                q_ref[slot, n, h // 2, channels + h * DIM : channels + (h + 1) * DIM, to] = qlo_ref[t, mine, at]

    def score(t, slot, i):
        n, p = units[i]
        key = jnp.concatenate([key0_ref[t], key1_ref[t]], axis=0)
        key = jnp.concatenate([key, key], axis=1)
        scores = jnp.dot(key, q_ref[slot, n, p], preferred_element_type=F32) + add_ref[n, p]
        score_ref[i % 2] = scores
        return jnp.max(scores, axis=0, keepdims=True)

    def combine(t, i, top):
        n, p = units[i]
        weights = jnp.exp2(score_ref[i % 2] - top).astype(BF)
        value = jnp.concatenate([val0_ref[t, p], val1_ref[t, p]], axis=1)
        got = jnp.dot(value, weights, preferred_element_type=F32)
        for k in range(2):
            to = slice(k * LANES, (k + 1) * LANES)
            h = 2 * p + k
            att_ref[h * DIM : (h + 1) * DIM, n * LANES : (n + 1) * LANES] = (
                got[k * DIM : (k + 1) * DIM, to] / got[2 * DIM : 2 * DIM + 1, to]
            )

    def finish(t):
        gated = (gate_ref[t].astype(F32) * att_ref[...]).astype(BF)
        update = lax.dot_general(gated, wo_ref[...], TN, preferred_element_type=F32) + os_ref[...]
        upd_ref[pl.ds(t, half, stride=columns), :] = update

    def column(t, top):
        slot = t % 2
        after = jnp.minimum(t + 1, columns - 1)
        load_queries(after, 1 - slot)
        for i in range(len(units)):
            if i + 1 < len(units):
                later = score(t, slot, i + 1)
            else:
                later = score(after, 1 - slot, 0)
            combine(t, i, top)
            top = later
        finish(t)
        return top

    for copy in copies:
        copy.wait()
    real = (count - chip + sources - 1) // sources
    load_queries(0, 0)
    lax.fori_loop(0, real, column, score(0, 0, 0))

    def padding(t, _):
        weight = F32(1.0 / length).astype(BF).astype(F32)
        for p in range(pairs):
            part = jnp.sum(val0_ref[t, p, : 2 * DIM, :].astype(F32), axis=1, keepdims=True)
            part += jnp.sum(val1_ref[t, p, : 2 * DIM, :].astype(F32), axis=1, keepdims=True)
            att_ref[p * 2 * DIM : (p + 1) * 2 * DIM, :] = jnp.broadcast_to(part * weight, (2 * DIM, half))
        finish(t)
        return 0

    lax.fori_loop(real, columns, padding, 0)
    tall = rows * columns

    def narrow(s, _):
        out_ref[s] = upd_ref[pl.ds(pl.multiple_of(s * tall, 8), tall), :].astype(BF)
        return 0

    lax.fori_loop(0, sources, narrow, 0, unroll=4)


def attend_call(mask, bias, qhi, qlo, key0, key1, val0, val1, gate, wo, os):
    columns, channels, half = gate.shape
    sources = bias.shape[0]
    rows = half // sources
    parts = half // LANES
    far = (qhi, qlo, key0, key1, val0, val1, gate, wo)
    return pl.pallas_call(
        attend_kernel,
        out_shape=in_vmem((sources, rows * columns, channels)),
        in_specs=[VM, VM] + [pl.BlockSpec(memory_space=pltpu.HBM)] * len(far) + [VM],
        out_specs=VM,
        scratch_shapes=[
            pltpu.VMEM((2, sources * 2 * rows * HEADS, LANES), F32),
            pltpu.VMEM((parts, HEADS // 2, 2 * half, 2 * LANES), F32),
            pltpu.VMEM((2, parts, HEADS // 2, 2 * channels, 2 * LANES), BF),
            pltpu.VMEM((2, 2 * half, 2 * LANES), F32),
            pltpu.VMEM((channels, half), F32),
            pltpu.VMEM((columns * half, channels), F32),
        ]
        + [pltpu.VMEM(a.shape, a.dtype) for a in far]
        + [pltpu.SemaphoreType.DMA((len(far),))],
        compiler_params=room(30),
        name="attend",
    )(mask, held(bias), *map(away, far), os)


def on_device(pair, residue_mask, ln_gain, ln_shift, w_query, w_key, w_value, w_gate, gate_shift,
              w_bias, w_out, out_shift):
    own_rows, length, channels = pair.shape
    chips = length // (2 * own_rows)
    columns = length // chips
    gain, shift = ln_gain.reshape(1, channels), ln_shift.reshape(1, channels)
    mask = residue_mask.reshape(length // LANES, LANES)
    swap = [(0, 1), (1, 0)]
    trade = lambda a: lax.all_to_all(a, CHIPS, split_axis=0, concat_axis=0, tiled=True)

    got = trade(pair.reshape(own_rows * columns, chips, channels).transpose(1, 0, 2))
    bias_own, bias_send = bias_call(pair, gain, shift, w_bias.T)
    bias = trade(copies_call(bias_own, held(lax.ppermute(bias_send, "core", swap)), chips))

    cols = columns_call(held(got), gain, shift, columns)
    other = lax.ppermute(cols, "core", swap)
    qhi, qlo, key0, val0, gate = own_call(held(cols), w_query, w_key, w_value, w_gate, gate_shift.reshape(1, channels))
    key1, val1 = other_call(held(other), w_key, w_value)
    out = attend_call(mask, bias, qhi, qlo, key0, key1, val0, val1, gate, w_out, out_shift.reshape(1, channels))
    back = trade(out)
    return back.transpose(1, 0, 2).reshape(own_rows, length, channels)


def solution(mesh):
    fine = Mesh(mesh.devices.reshape(2, RING, RING, 2, 2), PLACES)
    placed = (P(PLACES, None, None),) + (P(),) * 11
    return jax.shard_map(
        on_device,
        mesh=fine,
        in_specs=placed,
        out_specs=P(PLACES, None, None),
        check_vma=False,
    )
```

time: 451 us -> 119 us (0.26)
  waiting for transfers between devices: 195 us -> 31 us
  matrix products: 142 us -> 0 us
  Pallas kernels: 0 us -> 36.3 us
  other arithmetic: 26.9 us -> 0 us
  local copies, waits for them, and re-layouts: 27.4 us -> 11.8 us
  between operations: 13.6 us -> 0.22 us
  blocking collectives: 31.7 us -> 22.5 us
  starting transfers between devices: 11.4 us -> 17 us
    all_gather x1 -> x0, waiting for transfers between devices: 172 us -> none  [on_device(): bias_all = lax.all_gather(bias_local, ('row', 'col'), axis=1, tiled=True)]
    dot_general x18 -> x0, matrix products: 109 us -> none  [the longest x6 51.2 us: one_column(): jnp.einsum('hki,khd->ihd', weights, value_col, preferred_element_type=jnp...]
    pallas_call x0 -> x6, Pallas kernels: none -> 36.3 us  [the longest x1 25.1 us: attend_call(): pl.pallas_call(attend_kernel, out_shape=in_vmem((sources, rows * columns,...]
    sub x6 -> x0, matrix products: 33.2 us -> none  [one_column(): exponent = jnp.exp(scores - highest)]
    dynamic_slice x42 -> x0, local copies, waits for them, and re-layouts: 19.1 us -> none  [the longest x12 7.2 us: one_column(): lax.dynamic_index_in_dim(values_all, column, 1, keepdims=False)]
    reduce_sum x2 -> x0, other arithmetic: 10.4 us -> none  [the longest x1 8.13 us: normalize(): spread = jnp.mean(centered * centered, axis=-1, keepdims=True)]
    all_to_all x1, blocking collectives: 31.7 us -> 22.5 us  [on_device(): lax.all_to_all(a, CHIPS, split_axis=0, concat_axis=0, tiled=True)]
    convert_element_type x1 -> x0, other arithmetic: 8.71 us -> none  [normalize(): return scaled.astype(jnp.bfloat16)]
  transfers between devices with their start and end apart: 2 -> 4, of which waited for: 2 -> 3; matrix products, arithmetic and copies ran while one was open for 1% -> 0% of each run, Pallas kernels for 0% -> 9%
where the time goes in v2:
time: 119 us
  Pallas kernels  36.3 us (31%)
  waiting for transfers between devices  31 us (26%)
  blocking collectives  22.5 us (19%)
  starting transfers between devices  17 us (14%)
  local copies, waits for them, and re-layouts  11.8 us (10%)
    all_to_all x2, waiting for transfers between devices, on_device(): lax.all_to_all(a, CHIPS, split_axis=0, concat_axis=0, tiled=True)  29.8 us
    pallas_call x1, Pallas kernels, attend_call(): pl.pallas_call(attend_kernel, out_shape=in_vmem((sources, rows * columns,...  25.1 us
    all_to_all x1, blocking collectives, on_device(): lax.all_to_all(a, CHIPS, split_axis=0, concat_axis=0, tiled=True)  22.5 us
    all_to_all x2, starting transfers between devices, on_device(): lax.all_to_all(a, CHIPS, split_axis=0, concat_axis=0, tiled=True)  16.9 us
    unnamed x36, local copies, waits for them, and re-layouts  7.46 us
    pallas_call x1, Pallas kernels, columns_call(): pl.pallas_call(columns_kernel, out_shape=in_vmem((columns, half, channels...  3.46 us
    reshape x1, local copies, waits for them, and re-layouts, on_device(): pair.reshape(own_rows * columns, chips, channels).transpose(1, 0, 2)  3.05 us
    pallas_call x1, Pallas kernels, bias_call(): pl.pallas_call(bias_kernel, out_shape=(piece, piece), in_specs=[VM] * 4,...  2.43 us
  transfers between devices with their start and end apart: 4, of which 3 were waited for; matrix products, arithmetic and copies ran while one was open for 0% of the time, Pallas kernels for 9%

profile of v2, /device:TPU:0, one launch (start us, length us, event | category | flops | bytes accessed | tf_op | source)
XLA Modules:
  0.0 118.8 jit_solution(3130891792530457108)
XLA Ops:
  0.0 3.0 %copy.16 = bf16[72,64,128]{2,0,1:T(8,128)(2,1)} copy(bf16[72,64,128]{2,1,0:T(8,128)(2,1)} %bitcast.12) | data formatting | bytes 2359296 | tf_op jit(solution)/shard_map/reshape | solution.py:381
  3.1 11.6 %all-to-all-start.1 = ((bf16[64,72,128]{2,1,0:T(8,128)(2,1)}), bf16[64,72,128]{2,1,0:T(8,128)(2,1)S(1)}, u32[]{:S(2)}, u32[]{:S(2)}) async-start(bf16[64,72,128]{2,1,0:T(8,128)(2,1)} %bitcast.21), calls=%async_computation.1 | async-start | bytes 2359296 | tf_op jit(solution)/shard_map/all_to_all | solution.py:379
  14.7 2.4 %bias_rows.1 = (bf16[3,48,128]{2,1,0:T(8,128)(2,1)S(1)}, bf16[3,48,128]{2,1,0:T(8,128)(2,1)S(1)}) custom-call(bf16[6,768,128]{2,1,0:T(8,128)(2,1)S(1)} %copy-done, f32[1,128]{1,0:T(1,128)S(1)} %bitcast.14, f32[1,128]{1,0:T(1,128)S(1)} %bitcast.16, bf16[4,128]{1,0:T(4,128)(2,1)S(1)} %bitcast.18), custom_call_target="tpu_custom_call" | custom-call | tf_op jit(solution)/shard_map/bias_rows/pallas_call | solution.py:80
  17.2 0.1 collective-permute-start
  17.3 1.2 %collective-permute-done.other_ref = bf16[3,48,128]{2,1,0:T(8,128)(2,1)S(1)} collective-permute-done((bf16[3,48,128]{2,1,0:T(8,128)(2,1)S(1)}, bf16[3,48,128]{2,1,0:T(8,128)(2,1)S(1)}, u32[]{:S(2)}, u32[]{:S(2)}) %collective-permute-start) | collective-permute-done | bytes 36896 | tf_op jit(solution)/shard_map/ppermute | solution.py:383
  18.5 1.7 %copies.1 = bf16[64,144,128]{2,1,0:T(8,128)(2,1)} custom-call(bf16[3,48,128]{2,1,0:T(8,128)(2,1)S(1)} %get-tuple-element.14.own_ref, bf16[3,48,128]{2,1,0:T(8,128)(2,1)S(1)} %collective-permute-done.other_ref), custom_call_target="tpu_custom_call" | custom-call | tf_op jit(solution)/shard_map/copies/pallas_call | solution.py:109
  20.2 14.2 %all-to-all-done.1.got_ref = bf16[64,72,128]{2,1,0:T(8,128)(2,1)S(1)} async-done(((bf16[64,72,128]{2,1,0:T(8,128)(2,1)}), bf16[64,72,128]{2,1,0:T(8,128)(2,1)S(1)}, u32[]{:S(2)}, u32[]{:S(2)}) %all-to-all-start.1) | async-done | bytes 1179680 | tf_op jit(solution)/shard_map/all_to_all | solution.py:379
  34.4 5.2 %all-to-all-start = ((bf16[64,144,128]{2,1,0:T(8,128)(2,1)}), bf16[64,144,128]{2,1,0:T(8,128)(2,1)S(1)}, u32[]{:S(2)}, u32[]{:S(2)}) async-start(bf16[64,144,128]{2,1,0:T(8,128)(2,1)} %copies.1), calls=%async_computation | async-start | bytes 4718592 | tf_op jit(solution)/shard_map/all_to_all | solution.py:379
  39.7 0.0 copy-start.10
  39.7 3.5 %columns.1.cols_ref = bf16[12,384,128]{2,1,0:T(8,128)(2,1)S(1)} custom-call(bf16[64,72,128]{2,1,0:T(8,128)(2,1)S(1)} %all-to-all-done.1.got_ref, f32[1,128]{1,0:T(1,128)S(1)} %bitcast.15, f32[1,128]{1,0:T(1,128)S(1)} %bitcast.17), custom_call_target="tpu_custom_call" | custom-call | tf_op jit(solution)/shard_map/columns/pallas_call | solution.py:143
  43.2 0.1 collective-permute-start.1
  43.4 2.3 %own.1 = (bf16[12,128,384]{2,1,0:T(8,128)(2,1)S(1)}, bf16[12,128,384]{2,1,0:T(8,128)(2,1)S(1)}, bf16[12,384,128]{2,1,0:T(8,128)(2,1)S(1)}, bf16[12,2,80,384]{3,2,1,0:T(8,128)(2,1)S(1)}, bf16[12,128,384]{2,1,0:T(8,128)(2,1)S(1)}) custom-call(bf16[12,384,128]{2,1,0:T(8,128)(2,1)S(1)} %columns.1.cols_ref, bf16[128,128]{1,0:T(8,128)(2,1)S(1)} %copy-done.10, ...), custom_call_target="tpu_custom_call" | custom-call | tf_op jit(solution)/shard_map/own/pallas_call | solution.py:199
  45.7 1.1 copy-done.1
  46.8 1.0 copy-done.3
  47.8 1.0 copy-done.4
  48.8 1.0 copy-done.5
  49.9 1.0 copy-done.6
  50.9 1.3 %other.1 = (bf16[12,384,128]{2,1,0:T(8,128)(2,1)S(1)}, bf16[12,2,80,384]{3,2,1,0:T(8,128)(2,1)S(1)}) custom-call(bf16[12,384,128]{2,1,0:T(8,128)(2,1)S(1)} %collective-permute-done.1.cols_ref, bf16[128,128]{1,0:T(8,128)(2,1)S(1)} %copy-done.8, bf16[128,128]{1,0:T(8,128)(2,1)S(1)} %copy-done.9), custom_call_target="tpu_custom_call" | custom-call | tf_op jit(solution)/shard_map/other/pallas_call | solution.py:222
  52.2 1.1 copy-done.2
  53.3 1.1 copy-done.7
  54.4 15.5 %all-to-all-done.bias_ref = bf16[64,144,128]{2,1,0:T(8,128)(2,1)S(1)} async-done(((bf16[64,144,128]{2,1,0:T(8,128)(2,1)}), bf16[64,144,128]{2,1,0:T(8,128)(2,1)S(1)}, u32[]{:S(2)}, u32[]{:S(2)}) %all-to-all-start) | async-done | bytes 2359328 | tf_op jit(solution)/shard_map/all_to_all | solution.py:379
  69.9 25.1 %attend.1 = bf16[64,72,128]{2,1,0:T(8,128)(2,1)S(1)} custom-call(s32[6,128]{1,0:T(8,128)S(1)} %bitcast.13, bf16[64,144,128]{2,1,0:T(8,128)(2,1)S(1)} %all-to-all-done.bias_ref, bf16[12,128,384]{2,1,0:T(8,128)(2,1)} %copy-done.3, bf16[12,128,384]{2,1,0:T(8,128)(2,1)} %copy-done.4, bf16[12,384,128]{2,1,0:T(8,128)(2,1)} %copy-done.5, ...), custom_call_target="tpu_custom_call" | custom-call | tf_op jit(solution)/shard_map/attend/pallas_call | solution.py:351
  95.0 22.5 %all_to_all.15 = bf16[64,72,128]{2,1,0:T(8,128)(2,1)S(1)} all-to-all(bf16[64,72,128]{2,1,0:T(8,128)(2,1)S(1)} %attend.1), channel_id=1, replica_groups=mesh['ylo'=2,'z'=4,'x'=4,'yhi'=2,'core'=2] {'ylo','z','x','yhi'}, dimensions={0} | all-to-all | bytes 2359296 | tf_op jit(solution)/shard_map/all_to_all | solution.py:379
  117.5 1.3 %copy.14 = bf16[72,64,128]{2,1,0:T(8,128)(2,1)} copy(bf16[72,64,128]{2,0,1:T(8,128)(2,1)S(1)} %bitcast.22) | data formatting | bytes 2359296 | tf_op jit(solution)/shard_map/transpose | solution.py:391
  (29 shorter events, 0.1 us)
Async XLA Ops:
  3.0 11.7 %copy-start = (bf16[6,768,128]{2,1,0:T(8,128)(2,1)S(1)}, bf16[6,768,128]{2,1,0:T(8,128)(2,1)}, u32[]{:S(2)}) copy-start(bf16[6,768,128]{2,1,0:T(8,128)(2,1)} %pair_ref.1) | copy-start | bytes 3538948
  3.0 11.7 %copy-start.13 = (f32[128]{0:T(128)S(1)}, f32[128]{0:T(128)}, u32[]{:S(2)}) copy-start(f32[128]{0:T(128)} %param.14) | copy-start | bytes 1540
  3.1 11.7 %copy-start.14 = (f32[128]{0:T(128)S(1)}, f32[128]{0:T(128)}, u32[]{:S(2)}) copy-start(f32[128]{0:T(128)} %param.15) | copy-start | bytes 1540
  3.1 11.7 %copy-start.15 = (bf16[128,4]{0,1:T(4,128)(2,1)S(1)}, bf16[128,4]{0,1:T(4,128)(2,1)}, u32[]{:S(2)}) copy-start(bf16[128,4]{0,1:T(4,128)(2,1)} %param.21) | copy-start | bytes 3076
  3.1 31.4 %all-to-all-start.1 = ((bf16[64,72,128]{2,1,0:T(8,128)(2,1)}), bf16[64,72,128]{2,1,0:T(8,128)(2,1)S(1)}, u32[]{:S(2)}, u32[]{:S(2)}) async-start(bf16[64,72,128]{2,1,0:T(8,128)(2,1)} %bitcast.21), calls=%async_computation.1 | async-start | bytes 2359296 | tf_op jit(solution)/shard_map/all_to_all | solution.py:379
  17.2 1.3 %collective-permute-start = (bf16[3,48,128]{2,1,0:T(8,128)(2,1)S(1)}, bf16[3,48,128]{2,1,0:T(8,128)(2,1)S(1)}, u32[]{:S(2)}, u32[]{:S(2)}) collective-permute-start(bf16[3,48,128]{2,1,0:T(8,128)(2,1)S(1)} %get-tuple-element.15), channel_id=1, source_target_pairs={{0,1},{1,0},{2,3},{3,2},{4,5},{5,4},{6,7},{7,6},{8,9},{9,8},{10,11... | collective-permute-start | bytes 110600 | tf_op jit(solution)/shard_map/ppermute | solution.py:383
  34.4 35.5 %all-to-all-start = ((bf16[64,144,128]{2,1,0:T(8,128)(2,1)}), bf16[64,144,128]{2,1,0:T(8,128)(2,1)S(1)}, u32[]{:S(2)}, u32[]{:S(2)}) async-start(bf16[64,144,128]{2,1,0:T(8,128)(2,1)} %copies.1), calls=%async_computation | async-start | bytes 4718592 | tf_op jit(solution)/shard_map/all_to_all | solution.py:379
  39.7 3.6 %copy-start.8 = (bf16[128,128]{1,0:T(8,128)(2,1)S(1)}, bf16[128,128]{1,0:T(8,128)(2,1)}, u32[]{:S(2)}) copy-start(bf16[128,128]{1,0:T(8,128)(2,1)} %wk_ref.3) | copy-start | bytes 98308
  39.7 3.6 %copy-start.9 = (bf16[128,128]{1,0:T(8,128)(2,1)S(1)}, bf16[128,128]{1,0:T(8,128)(2,1)}, u32[]{:S(2)}) copy-start(bf16[128,128]{1,0:T(8,128)(2,1)} %wv_ref.3) | copy-start | bytes 98308
  39.7 3.6 %copy-start.10 = (bf16[128,128]{1,0:T(8,128)(2,1)S(1)}, bf16[128,128]{1,0:T(8,128)(2,1)}, u32[]{:S(2)}) copy-start(bf16[128,128]{1,0:T(8,128)(2,1)} %wq_ref.1) | copy-start | bytes 98308
  39.7 3.6 %copy-start.11 = (bf16[128,128]{1,0:T(8,128)(2,1)S(1)}, bf16[128,128]{1,0:T(8,128)(2,1)}, u32[]{:S(2)}) copy-start(bf16[128,128]{1,0:T(8,128)(2,1)} %wg_ref.1) | copy-start | bytes 98308
  39.7 3.6 %copy-start.16 = (f32[128]{0:T(128)S(1)}, f32[128]{0:T(128)}, u32[]{:S(2)}) copy-start(f32[128]{0:T(128)} %param.20) | copy-start | bytes 1540
  43.2 7.7 %collective-permute-start.1 = (bf16[12,384,128]{2,1,0:T(8,128)(2,1)S(1)}, bf16[12,384,128]{2,1,0:T(8,128)(2,1)S(1)}, u32[]{:S(2)}, u32[]{:S(2)}) collective-permute-start(bf16[12,384,128]{2,1,0:T(8,128)(2,1)S(1)} %columns.1.cols_ref), channel_id=1, source_target_pairs={{0,1},{1,0},{2,3},{3,2},{4,5},{5,4},{6,7},{7,6},{8,9},{9,8},{10,11... | collective-permute-start | bytes 3538952 | tf_op jit(solution)/shard_map/ppermute | solution.py:386
  43.3 26.6 %copy-start.12 = (s32[768]{0:T(1024)S(1)}, s32[768]{0:T(1024)}, u32[]{:S(2)}) copy-start(s32[768]{0:T(1024)} %param.13) | copy-start | bytes 9220
  43.3 26.6 %copy-start.17 = (f32[128]{0:T(128)S(1)}, f32[128]{0:T(128)}, u32[]{:S(2)}) copy-start(f32[128]{0:T(128)} %param.23) | copy-start | bytes 1540
  45.7 1.1 copy-start.1
  46.8 1.0 copy-start.3
  47.8 1.0 copy-start.4
  48.8 1.0 copy-start.5
  49.9 1.0 copy-start.6
  52.2 1.1 copy-start.2
  53.3 1.1 copy-start.7

commit v3 on v2

--- a/solution.py
+++ b/solution.py
@@ -1,3 +1,4 @@
+import functools
 import math
 
 import jax
@@ -227,6 +228,10 @@
         compiler_params=room(12),
         name="other",
     )(cols, wk, wv)
+
+
+def takes(half):
+    return (half * 19 // 24, half * 21 // 24, half * 23 // 24)
 
 
 def attend_kernel(mask_ref, bias_ref, *refs):
@@ -278,19 +283,22 @@
                 q_ref[slot, n, h // 2, mine, to] = qhi_ref[t, mine, at]
                 q_ref[slot, n, h // 2, channels + h * DIM : channels + (h + 1) * DIM, to] = qlo_ref[t, mine, at]
 
-    def score(t, slot, i):
+    def score(t, slot, i, take):
         n, p = units[i]
-        key = jnp.concatenate([key0_ref[t], key1_ref[t]], axis=0)
+        key = jnp.concatenate([key0_ref[t, :take], key1_ref[t, :take]], axis=0)
         key = jnp.concatenate([key, key], axis=1)
-        scores = jnp.dot(key, q_ref[slot, n, p], preferred_element_type=F32) + add_ref[n, p]
-        score_ref[i % 2] = scores
-        return jnp.max(scores, axis=0, keepdims=True)
-
-    def combine(t, i, top):
+        scores = jnp.dot(key, q_ref[slot, n, p], preferred_element_type=F32)
+        own = scores[:take] + add_ref[n, p, :take]
+        other = scores[take:] + add_ref[n, p, half : half + take]
+        score_ref[i % 3, :take] = own
+        score_ref[i % 3, take : 2 * take] = other
+        return jnp.maximum(jnp.max(own, axis=0, keepdims=True), jnp.max(other, axis=0, keepdims=True))
+
+    def combine(t, i, take, top):
         n, p = units[i]
-        weights = jnp.exp2(score_ref[i % 2] - top).astype(BF)
-        value = jnp.concatenate([val0_ref[t, p], val1_ref[t, p]], axis=1)
-        got = jnp.dot(value, weights, preferred_element_type=F32)
+        weights = jnp.exp2(score_ref[i % 3, : 2 * take] - top).astype(BF)
+        got = jnp.dot(val0_ref[t, p, :, :take], weights[:take], preferred_element_type=F32)
+        got += jnp.dot(val1_ref[t, p, :, :take], weights[take:], preferred_element_type=F32)
         for k in range(2):
             to = slice(k * LANES, (k + 1) * LANES)
             h = 2 * p + k
@@ -303,25 +311,35 @@
         update = lax.dot_general(gated, wo_ref[...], TN, preferred_element_type=F32) + os_ref[...]
         upd_ref[pl.ds(t, half, stride=columns), :] = update
 
-    def column(t, top):
+    def column(take, t, tops):
         slot = t % 2
         after = jnp.minimum(t + 1, columns - 1)
         load_queries(after, 1 - slot)
         for i in range(len(units)):
-            if i + 1 < len(units):
-                later = score(t, slot, i + 1)
+            ahead = i + 2
+            if ahead < len(units):
+                later = score(t, slot, ahead, take)
             else:
-                later = score(after, 1 - slot, 0)
-            combine(t, i, top)
-            top = later
+                later = score(after, 1 - slot, ahead - len(units), take)
+            combine(t, i, take, tops[0])
+            tops = (tops[1], later)
         finish(t)
-        return top
+        return tops
 
     for copy in copies:
         copy.wait()
     real = (count - chip + sources - 1) // sources
     load_queries(0, 0)
-    lax.fori_loop(0, real, column, score(0, 0, 0))
+
+    def valid_columns(take):
+        tops = (score(0, 0, 0, take), score(0, 0, 1, take))
+        lax.fori_loop(0, real, functools.partial(column, take), tops)
+
+    need = (count + 2 * rows - 1) // (2 * rows) * rows
+    below = -1
+    for take in takes(half):
+        pl.when(jnp.logical_and(need > below, need <= take))(functools.partial(valid_columns, take))
+        below = take
 
     def padding(t, _):
         weight = F32(1.0 / length).astype(BF).astype(F32)
@@ -357,7 +375,7 @@
             pltpu.VMEM((2, sources * 2 * rows * HEADS, LANES), F32),
             pltpu.VMEM((parts, HEADS // 2, 2 * half, 2 * LANES), F32),
             pltpu.VMEM((2, parts, HEADS // 2, 2 * channels, 2 * LANES), BF),
-            pltpu.VMEM((2, 2 * half, 2 * LANES), F32),
+            pltpu.VMEM((3, 2 * half, 2 * LANES), F32),
             pltpu.VMEM((channels, half), F32),
             pltpu.VMEM((columns * half, channels), F32),
         ]

time: 119 us -> 113 us (0.950)
  Pallas kernels: 36.3 us -> 29 us
    pallas_call x1, Pallas kernels: 25.1 us -> 17.9 us  [attend_call(): pl.pallas_call(attend_kernel, out_shape=in_vmem((sources, rows * columns,...]
  transfers between devices with their start and end apart: 4 -> 4, of which waited for: 3 -> 3; matrix products, arithmetic and copies ran while one was open for 0% -> 0% of each run, Pallas kernels for 9% -> 10%
where the time goes in v3:
time: 113 us; the launch traced here: 112 us
  waiting for transfers between devices  31 us (27%)
  Pallas kernels  29 us (26%)
  blocking collectives  22.6 us (20%)
  starting transfers between devices  17 us (15%)
  local copies, waits for them, and re-layouts  11.8 us (10%)
    all_to_all x2, waiting for transfers between devices, on_device(): lax.all_to_all(a, CHIPS, split_axis=0, concat_axis=0, tiled=True)  29.8 us
    all_to_all x1, blocking collectives, on_device(): lax.all_to_all(a, CHIPS, split_axis=0, concat_axis=0, tiled=True)  22.6 us
    pallas_call x1, Pallas kernels, attend_call(): pl.pallas_call(attend_kernel, out_shape=in_vmem((sources, rows * columns,...  17.9 us
    all_to_all x2, starting transfers between devices, on_device(): lax.all_to_all(a, CHIPS, split_axis=0, concat_axis=0, tiled=True)  16.9 us
    unnamed x36, local copies, waits for them, and re-layouts  7.46 us
    pallas_call x1, Pallas kernels, columns_call(): pl.pallas_call(columns_kernel, out_shape=in_vmem((columns, half, channels...  3.46 us
    reshape x1, local copies, waits for them, and re-layouts, on_device(): pair.reshape(own_rows * columns, chips, channels).transpose(1, 0, 2)  3.05 us
    pallas_call x1, Pallas kernels, bias_call(): pl.pallas_call(bias_kernel, out_shape=(piece, piece), in_specs=[VM] * 4,...  2.43 us
  transfers between devices with their start and end apart: 4, of which 3 were waited for; matrix products, arithmetic and copies ran while one was open for 0% of the time, Pallas kernels for 10%

profile of v3, /device:TPU:0, one launch (start us, length us, event | category | flops | bytes accessed | tf_op | source)
XLA Modules:
  0.0 111.6 jit_solution(18179652639326947473)
XLA Ops:
  0.0 3.0 %copy.16 = bf16[72,64,128]{2,0,1:T(8,128)(2,1)} copy(bf16[72,64,128]{2,1,0:T(8,128)(2,1)} %bitcast.12) | data formatting | bytes 2359296 | tf_op jit(solution)/shard_map/reshape | solution.py:399
  3.1 11.6 %all-to-all-start.1 = ((bf16[64,72,128]{2,1,0:T(8,128)(2,1)}), bf16[64,72,128]{2,1,0:T(8,128)(2,1)S(1)}, u32[]{:S(2)}, u32[]{:S(2)}) async-start(bf16[64,72,128]{2,1,0:T(8,128)(2,1)} %bitcast.21), calls=%async_computation.1 | async-start | bytes 2359296 | tf_op jit(solution)/shard_map/all_to_all | solution.py:397
  14.7 2.4 %bias_rows.1 = (bf16[3,48,128]{2,1,0:T(8,128)(2,1)S(1)}, bf16[3,48,128]{2,1,0:T(8,128)(2,1)S(1)}) custom-call(bf16[6,768,128]{2,1,0:T(8,128)(2,1)S(1)} %copy-done, f32[1,128]{1,0:T(1,128)S(1)} %bitcast.14, f32[1,128]{1,0:T(1,128)S(1)} %bitcast.16, bf16[4,128]{1,0:T(4,128)(2,1)S(1)} %bitcast.18), custom_call_target="tpu_custom_call" | custom-call | tf_op jit(solution)/shard_map/bias_rows/pallas_call | solution.py:81
  17.2 0.1 collective-permute-start
  17.3 1.2 %collective-permute-done.other_ref = bf16[3,48,128]{2,1,0:T(8,128)(2,1)S(1)} collective-permute-done((bf16[3,48,128]{2,1,0:T(8,128)(2,1)S(1)}, bf16[3,48,128]{2,1,0:T(8,128)(2,1)S(1)}, u32[]{:S(2)}, u32[]{:S(2)}) %collective-permute-start) | collective-permute-done | bytes 36896 | tf_op jit(solution)/shard_map/ppermute | solution.py:401
  18.5 1.7 %copies.1 = bf16[64,144,128]{2,1,0:T(8,128)(2,1)} custom-call(bf16[3,48,128]{2,1,0:T(8,128)(2,1)S(1)} %get-tuple-element.14.own_ref, bf16[3,48,128]{2,1,0:T(8,128)(2,1)S(1)} %collective-permute-done.other_ref), custom_call_target="tpu_custom_call" | custom-call | tf_op jit(solution)/shard_map/copies/pallas_call | solution.py:110
  20.2 14.2 %all-to-all-done.1.got_ref = bf16[64,72,128]{2,1,0:T(8,128)(2,1)S(1)} async-done(((bf16[64,72,128]{2,1,0:T(8,128)(2,1)}), bf16[64,72,128]{2,1,0:T(8,128)(2,1)S(1)}, u32[]{:S(2)}, u32[]{:S(2)}) %all-to-all-start.1) | async-done | bytes 1179680 | tf_op jit(solution)/shard_map/all_to_all | solution.py:397
  34.4 5.2 %all-to-all-start = ((bf16[64,144,128]{2,1,0:T(8,128)(2,1)}), bf16[64,144,128]{2,1,0:T(8,128)(2,1)S(1)}, u32[]{:S(2)}, u32[]{:S(2)}) async-start(bf16[64,144,128]{2,1,0:T(8,128)(2,1)} %copies.1), calls=%async_computation | async-start | bytes 4718592 | tf_op jit(solution)/shard_map/all_to_all | solution.py:397
  39.7 0.0 copy-start.10
  39.7 3.5 %columns.1.cols_ref = bf16[12,384,128]{2,1,0:T(8,128)(2,1)S(1)} custom-call(bf16[64,72,128]{2,1,0:T(8,128)(2,1)S(1)} %all-to-all-done.1.got_ref, f32[1,128]{1,0:T(1,128)S(1)} %bitcast.15, f32[1,128]{1,0:T(1,128)S(1)} %bitcast.17), custom_call_target="tpu_custom_call" | custom-call | tf_op jit(solution)/shard_map/columns/pallas_call | solution.py:144
  43.2 0.1 collective-permute-start.1
  43.4 2.3 %own.1 = (bf16[12,128,384]{2,1,0:T(8,128)(2,1)S(1)}, bf16[12,128,384]{2,1,0:T(8,128)(2,1)S(1)}, bf16[12,384,128]{2,1,0:T(8,128)(2,1)S(1)}, bf16[12,2,80,384]{3,2,1,0:T(8,128)(2,1)S(1)}, bf16[12,128,384]{2,1,0:T(8,128)(2,1)S(1)}) custom-call(bf16[12,384,128]{2,1,0:T(8,128)(2,1)S(1)} %columns.1.cols_ref, bf16[128,128]{1,0:T(8,128)(2,1)S(1)} %copy-done.10, ...), custom_call_target="tpu_custom_call" | custom-call | tf_op jit(solution)/shard_map/own/pallas_call | solution.py:200
  45.7 1.1 copy-done.1
  46.8 1.0 copy-done.3
  47.8 1.0 copy-done.4
  48.8 1.0 copy-done.5
  49.9 1.0 copy-done.6
  50.9 1.3 %other.1 = (bf16[12,384,128]{2,1,0:T(8,128)(2,1)S(1)}, bf16[12,2,80,384]{3,2,1,0:T(8,128)(2,1)S(1)}) custom-call(bf16[12,384,128]{2,1,0:T(8,128)(2,1)S(1)} %collective-permute-done.1.cols_ref, bf16[128,128]{1,0:T(8,128)(2,1)S(1)} %copy-done.8, bf16[128,128]{1,0:T(8,128)(2,1)S(1)} %copy-done.9), custom_call_target="tpu_custom_call" | custom-call | tf_op jit(solution)/shard_map/other/pallas_call | solution.py:223
  52.2 1.1 %copy-done.2 = bf16[12,2,80,384]{3,2,1,0:T(8,128)(2,1)} copy-done((bf16[12,2,80,384]{3,2,1,0:T(8,128)(2,1)}, bf16[12,2,80,384]{3,2,1,0:T(8,128)(2,1)S(1)}, u32[]{:S(2)}) %copy-start.2) | copy-done | bytes 1474584
  53.3 1.1 copy-done.7
  54.4 15.5 %all-to-all-done.bias_ref = bf16[64,144,128]{2,1,0:T(8,128)(2,1)S(1)} async-done(((bf16[64,144,128]{2,1,0:T(8,128)(2,1)}), bf16[64,144,128]{2,1,0:T(8,128)(2,1)S(1)}, u32[]{:S(2)}, u32[]{:S(2)}) %all-to-all-start) | async-done | bytes 2359328 | tf_op jit(solution)/shard_map/all_to_all | solution.py:397
  69.9 17.9 %attend.1 = bf16[64,72,128]{2,1,0:T(8,128)(2,1)S(1)} custom-call(s32[6,128]{1,0:T(8,128)S(1)} %bitcast.13, bf16[64,144,128]{2,1,0:T(8,128)(2,1)S(1)} %all-to-all-done.bias_ref, bf16[12,128,384]{2,1,0:T(8,128)(2,1)} %copy-done.3, bf16[12,128,384]{2,1,0:T(8,128)(2,1)} %copy-done.4, bf16[12,384,128]{2,1,0:T(8,128)(2,1)} %copy-done.5, ...), custom_call_target="tpu_custom_call" | custom-call | tf_op jit(solution)/shard_map/attend/pallas_call | solution.py:369
  87.8 22.6 %all_to_all.15 = bf16[64,72,128]{2,1,0:T(8,128)(2,1)S(1)} all-to-all(bf16[64,72,128]{2,1,0:T(8,128)(2,1)S(1)} %attend.1), channel_id=1, replica_groups=mesh['ylo'=2,'z'=4,'x'=4,'yhi'=2,'core'=2] {'ylo','z','x','yhi'}, dimensions={0} | all-to-all | bytes 2359296 | tf_op jit(solution)/shard_map/all_to_all | solution.py:397
  110.3 1.3 %copy.14 = bf16[72,64,128]{2,1,0:T(8,128)(2,1)} copy(bf16[72,64,128]{2,0,1:T(8,128)(2,1)S(1)} %bitcast.22) | data formatting | bytes 2359296 | tf_op jit(solution)/shard_map/transpose | solution.py:409
  (29 shorter events, 0.1 us)
Async XLA Ops:
  3.0 11.7 %copy-start = (bf16[6,768,128]{2,1,0:T(8,128)(2,1)S(1)}, bf16[6,768,128]{2,1,0:T(8,128)(2,1)}, u32[]{:S(2)}) copy-start(bf16[6,768,128]{2,1,0:T(8,128)(2,1)} %pair_ref.1) | copy-start | bytes 3538948
  3.0 11.7 %copy-start.13 = (f32[128]{0:T(128)S(1)}, f32[128]{0:T(128)}, u32[]{:S(2)}) copy-start(f32[128]{0:T(128)} %param.14) | copy-start | bytes 1540
  3.1 11.7 %copy-start.14 = (f32[128]{0:T(128)S(1)}, f32[128]{0:T(128)}, u32[]{:S(2)}) copy-start(f32[128]{0:T(128)} %param.15) | copy-start | bytes 1540
  3.1 11.7 %copy-start.15 = (bf16[128,4]{0,1:T(4,128)(2,1)S(1)}, bf16[128,4]{0,1:T(4,128)(2,1)}, u32[]{:S(2)}) copy-start(bf16[128,4]{0,1:T(4,128)(2,1)} %param.21) | copy-start | bytes 3076
  3.1 31.4 %all-to-all-start.1 = ((bf16[64,72,128]{2,1,0:T(8,128)(2,1)}), bf16[64,72,128]{2,1,0:T(8,128)(2,1)S(1)}, u32[]{:S(2)}, u32[]{:S(2)}) async-start(bf16[64,72,128]{2,1,0:T(8,128)(2,1)} %bitcast.21), calls=%async_computation.1 | async-start | bytes 2359296 | tf_op jit(solution)/shard_map/all_to_all | solution.py:397
  17.2 1.3 %collective-permute-start = (bf16[3,48,128]{2,1,0:T(8,128)(2,1)S(1)}, bf16[3,48,128]{2,1,0:T(8,128)(2,1)S(1)}, u32[]{:S(2)}, u32[]{:S(2)}) collective-permute-start(bf16[3,48,128]{2,1,0:T(8,128)(2,1)S(1)} %get-tuple-element.15), channel_id=1, source_target_pairs={{0,1},{1,0},{2,3},{3,2},{4,5},{5,4},{6,7},{7,6},{8,9},{9,8},{10,11... | collective-permute-start | bytes 110600 | tf_op jit(solution)/shard_map/ppermute | solution.py:401
  34.4 35.5 %all-to-all-start = ((bf16[64,144,128]{2,1,0:T(8,128)(2,1)}), bf16[64,144,128]{2,1,0:T(8,128)(2,1)S(1)}, u32[]{:S(2)}, u32[]{:S(2)}) async-start(bf16[64,144,128]{2,1,0:T(8,128)(2,1)} %copies.1), calls=%async_computation | async-start | bytes 4718592 | tf_op jit(solution)/shard_map/all_to_all | solution.py:397
  39.7 3.6 %copy-start.8 = (bf16[128,128]{1,0:T(8,128)(2,1)S(1)}, bf16[128,128]{1,0:T(8,128)(2,1)}, u32[]{:S(2)}) copy-start(bf16[128,128]{1,0:T(8,128)(2,1)} %wk_ref.3) | copy-start | bytes 98308
  39.7 3.6 %copy-start.9 = (bf16[128,128]{1,0:T(8,128)(2,1)S(1)}, bf16[128,128]{1,0:T(8,128)(2,1)}, u32[]{:S(2)}) copy-start(bf16[128,128]{1,0:T(8,128)(2,1)} %wv_ref.3) | copy-start | bytes 98308
  39.7 3.6 %copy-start.10 = (bf16[128,128]{1,0:T(8,128)(2,1)S(1)}, bf16[128,128]{1,0:T(8,128)(2,1)}, u32[]{:S(2)}) copy-start(bf16[128,128]{1,0:T(8,128)(2,1)} %wq_ref.1) | copy-start | bytes 98308
  39.7 3.6 %copy-start.11 = (bf16[128,128]{1,0:T(8,128)(2,1)S(1)}, bf16[128,128]{1,0:T(8,128)(2,1)}, u32[]{:S(2)}) copy-start(bf16[128,128]{1,0:T(8,128)(2,1)} %wg_ref.1) | copy-start | bytes 98308
  39.7 3.6 %copy-start.16 = (f32[128]{0:T(128)S(1)}, f32[128]{0:T(128)}, u32[]{:S(2)}) copy-start(f32[128]{0:T(128)} %param.20) | copy-start | bytes 1540
  43.2 7.7 %collective-permute-start.1 = (bf16[12,384,128]{2,1,0:T(8,128)(2,1)S(1)}, bf16[12,384,128]{2,1,0:T(8,128)(2,1)S(1)}, u32[]{:S(2)}, u32[]{:S(2)}) collective-permute-start(bf16[12,384,128]{2,1,0:T(8,128)(2,1)S(1)} %columns.1.cols_ref), channel_id=1, source_target_pairs={{0,1},{1,0},{2,3},{3,2},{4,5},{5,4},{6,7},{7,6},{8,9},{9,8},{10,11... | collective-permute-start | bytes 3538952 | tf_op jit(solution)/shard_map/ppermute | solution.py:404
  43.3 26.6 %copy-start.12 = (s32[768]{0:T(1024)S(1)}, s32[768]{0:T(1024)}, u32[]{:S(2)}) copy-start(s32[768]{0:T(1024)} %param.13) | copy-start | bytes 9220
  43.3 26.6 %copy-start.17 = (f32[128]{0:T(128)S(1)}, f32[128]{0:T(128)}, u32[]{:S(2)}) copy-start(f32[128]{0:T(128)} %param.23) | copy-start | bytes 1540
  45.7 1.1 copy-start.1
  46.8 1.0 copy-start.3
  47.8 1.0 copy-start.4
  48.8 1.0 copy-start.5
  49.9 1.0 copy-start.6
  52.2 1.1 %copy-start.2 = (bf16[12,2,80,384]{3,2,1,0:T(8,128)(2,1)}, bf16[12,2,80,384]{3,2,1,0:T(8,128)(2,1)S(1)}, u32[]{:S(2)}) copy-start(bf16[12,2,80,384]{3,2,1,0:T(8,128)(2,1)S(1)} %get-tuple-element.21.refs_5_) | copy-start | bytes 4423684
  53.3 1.1 copy-start.7

commit v4 on v3

--- a/solution.py
+++ b/solution.py
@@ -1,4 +1,5 @@
 import functools
+import itertools
 import math
 
 import jax
@@ -30,10 +31,6 @@
 
 def held(a):
     return pltpu.with_memory_space_constraint(a, pltpu.VMEM)
-
-
-def away(a):
-    return pltpu.with_memory_space_constraint(a, pltpu.HBM)
 
 
 def in_vmem(shape):
@@ -93,30 +90,6 @@
     )(pair, gain, shift, wb)
 
 
-def copies_kernel(own_ref, other_ref, out_ref):
-    thirds, rows, _ = own_ref.shape
-    for n in range(thirds):
-        block = own_ref[n] + other_ref[n]
-
-        def fill(c, _):
-            out_ref[c, n * rows : (n + 1) * rows, :] = block
-            return 0
-
-        lax.fori_loop(0, out_ref.shape[0], fill, 0, unroll=4)
-
-
-def copies_call(own, other, chips):
-    thirds, rows, _ = own.shape
-    return pl.pallas_call(
-        copies_kernel,
-        out_shape=jax.ShapeDtypeStruct((chips, thirds * rows, LANES), BF),
-        in_specs=[VM, VM],
-        out_specs=VM,
-        compiler_params=room(8),
-        name="copies",
-    )(own, other)
-
-
 def columns_kernel(got_ref, gain_ref, shift_ref, by_source_ref, wide_ref):
     sources, width, channels = got_ref.shape
     columns, half, _ = by_source_ref.shape
@@ -234,34 +207,35 @@
     return (half * 19 // 24, half * 21 // 24, half * 23 // 24)
 
 
-def attend_kernel(mask_ref, bias_ref, *refs):
-    far, refs = refs[:8], refs[8:]
-    os_ref, out_ref, raw_ref, add_ref, q_ref, score_ref, att_ref, upd_ref = refs[:8]
-    here, sems = refs[8:16], refs[16]
-    qhi_ref, qlo_ref, key0_ref, key1_ref, val0_ref, val1_ref, gate_ref, wo_ref = here
-    copies = [
-        pltpu.make_async_copy(there, ref, sems.at[i]) for i, (there, ref) in enumerate(zip(far, here))
-    ]
-    for copy in copies:
-        copy.start()
+def attend_kernel(mask_ref, *refs):
+    bias_refs, refs = refs[:RING], refs[RING:]
+    qhi_ref, qlo_ref, key0_ref, key1_ref, val0_ref, val1_ref, gate_ref, wo_ref, os_ref = refs[:9]
+    out_ref, raw_ref, add_ref, q_ref, score_ref, att_ref, upd_ref = refs[9:]
     core = lax.axis_index("core")
     chip = lax.axis_index(CHIPS)
     columns, channels, half = gate_ref.shape
     parts = half // LANES
     length = 2 * half
-    sources = bias_ref.shape[0]
+    sources = RING * bias_refs[0].shape[0]
     rows = half // sources
     packed = 2 * rows * HEADS
     pairs = HEADS // 2
     count = jnp.sum(mask_ref[...])
+    my_x, my_y, my_z = lax.axis_index("x"), 2 * lax.axis_index("yhi") + lax.axis_index("ylo"), lax.axis_index("z")
+    back = lambda mine, turn: (mine + RING - turn) % RING
 
     for n in range(parts):
-        def widen(s, _):
-            at = pl.ds(pl.multiple_of(s * packed, 8), packed)
-            raw_ref[n % 2, at, :] = bias_ref[s, n * packed : (n + 1) * packed, :].astype(F32) * LOG2E
+        def widen(i, _):
+            z = back(my_z, i % RING)
+            for turn, bias_ref in enumerate(bias_refs):
+                x = back(my_x, jnp.where(core == 0, turn, i // RING))
+                y = back(my_y, jnp.where(core == 0, i // RING, turn))
+                s = (y % 2) * (2 * RING * RING) + z * (2 * RING) + x * 2 + y // 2
+                at = pl.ds(pl.multiple_of(s * packed, 8), packed)
+                raw_ref[n % 2, at, :] = bias_ref[i, n].astype(F32) * LOG2E
             return 0
 
-        lax.fori_loop(0, sources, widen, 0, unroll=4)
+        lax.fori_loop(0, RING * RING, widen, 0)
         place = lax.broadcasted_iota(jnp.int32, (half, LANES), 0)
         for side in range(2):
             real = core if side == 0 else 1 - core
@@ -326,8 +300,6 @@
         finish(t)
         return tops
 
-    for copy in copies:
-        copy.wait()
     real = (count - chip + sources - 1) // sources
     load_queries(0, 0)
 
@@ -362,14 +334,14 @@
 
 def attend_call(mask, bias, qhi, qlo, key0, key1, val0, val1, gate, wo, os):
     columns, channels, half = gate.shape
-    sources = bias.shape[0]
+    sources = RING * bias[0].shape[0]
     rows = half // sources
     parts = half // LANES
-    far = (qhi, qlo, key0, key1, val0, val1, gate, wo)
+    near = (*bias, qhi, qlo, key0, key1, val0, val1, gate)
     return pl.pallas_call(
         attend_kernel,
         out_shape=in_vmem((sources, rows * columns, channels)),
-        in_specs=[VM, VM] + [pl.BlockSpec(memory_space=pltpu.HBM)] * len(far) + [VM],
+        in_specs=[VM] * (3 + len(near)),
         out_specs=VM,
         scratch_shapes=[
             pltpu.VMEM((2, sources * 2 * rows * HEADS, LANES), F32),
@@ -378,12 +350,27 @@
             pltpu.VMEM((3, 2 * half, 2 * LANES), F32),
             pltpu.VMEM((channels, half), F32),
             pltpu.VMEM((columns * half, channels), F32),
-        ]
-        + [pltpu.VMEM(a.shape, a.dtype) for a in far]
-        + [pltpu.SemaphoreType.DMA((len(far),))],
+        ],
         compiler_params=room(30),
         name="attend",
-    )(mask, held(bias), *map(away, far), os)
+    )(mask, *map(held, near), wo, os)
+
+
+def ring(block, axes):
+    def moved(place, steps):
+        ylo, z, x, yhi, core = place
+        y = 2 * yhi + ylo
+        if axes[core] == "x":
+            x = (x + steps) % RING
+        else:
+            y = (y + steps) % RING
+        return y % 2, z, x, y // 2, core
+
+    sizes = (2, RING, RING, 2, 2)
+    places = list(itertools.product(*map(range, sizes)))
+    number = {place: i for i, place in enumerate(places)}
+    turns = [[(number[place], number[moved(place, steps)]) for place in places] for steps in range(1, RING)]
+    return [block] + [lax.ppermute(block, PLACES, turn) for turn in turns]
 
 
 def on_device(pair, residue_mask, ln_gain, ln_shift, w_query, w_key, w_value, w_gate, gate_shift,
@@ -398,7 +385,10 @@
 
     got = trade(pair.reshape(own_rows * columns, chips, channels).transpose(1, 0, 2))
     bias_own, bias_send = bias_call(pair, gain, shift, w_bias.T)
-    bias = trade(copies_call(bias_own, held(lax.ppermute(bias_send, "core", swap)), chips))
+    mixed = bias_own + lax.ppermute(bias_send, "core", swap)
+    near = jnp.stack([mixed] + [lax.ppermute(mixed, "z", [(i, (i + n) % RING) for i in range(RING)]) for n in range(1, RING)])
+    plane = jnp.concatenate(ring(near, ("y", "x")), axis=0)
+    bias = ring(plane, ("x", "y"))
 
     cols = columns_call(held(got), gain, shift, columns)
     other = lax.ppermute(cols, "core", swap)

time: 113 us -> 108 us (0.956)
  local copies, waits for them, and re-layouts: 11.8 us -> 4.52 us
  starting transfers between devices: 17 us -> 23.9 us
  waiting for transfers between devices: 31 us -> 26.9 us
    all_to_all x2 -> x1, waiting for transfers between devices: 29.8 us -> 0.01 us  [on_device(): lax.all_to_all(a, CHIPS, split_axis=0, concat_axis=0, tiled=True)]
    ppermute x1 -> x10, waiting for transfers between devices: 1.2 us -> 26.9 us  [the longest x6 14.9 us: ring(): return [block] + [lax.ppermute(block, PLACES, turn) for turn in turns]]
    ppermute x1 -> x10, starting transfers between devices: 0.08 us -> 11.1 us  [the longest x6 6.48 us: ring(): return [block] + [lax.ppermute(block, PLACES, turn) for turn in turns]]
    unnamed x36 -> x29, local copies, waits for them, and re-layouts: 7.46 us -> 0.14 us
    all_to_all x2 -> x1, starting transfers between devices: 16.9 us -> 11.6 us  [on_device(): lax.all_to_all(a, CHIPS, split_axis=0, concat_axis=0, tiled=True)]
    pallas_call x1, Pallas kernels: 17.9 us -> 19.6 us  [attend_call(): pl.pallas_call(attend_kernel, out_shape=in_vmem((sources, rows * columns,...]
    pallas_call x1 -> x0, Pallas kernels: 1.72 us -> none  [copies_call(): pl.pallas_call(copies_kernel, out_shape=jax.ShapeDtypeStruct((chips, thir...]
  transfers between devices with their start and end apart: 4 -> 12, of which waited for: 3 -> 7; matrix products, arithmetic and copies ran while one was open for 0% -> 0% of each run, Pallas kernels for 10% -> 9%
where the time goes in v4:
time: 108 us; the launch traced here: 107 us
  Pallas kernels  29.1 us (27%)
  waiting for transfers between devices  26.9 us (25%)
  starting transfers between devices  23.9 us (22%)
  blocking collectives  22.6 us (21%)
  local copies, waits for them, and re-layouts  4.52 us (4%)
    all_to_all x1, blocking collectives, on_device(): lax.all_to_all(a, CHIPS, split_axis=0, concat_axis=0, tiled=True)  22.6 us
    pallas_call x1, Pallas kernels, attend_call(): pl.pallas_call(attend_kernel, out_shape=in_vmem((sources, rows * columns,...  19.6 us
    ppermute x6, waiting for transfers between devices, ring(): return [block] + [lax.ppermute(block, PLACES, turn) for turn in turns]  14.9 us
    all_to_all x1, starting transfers between devices, on_device(): lax.all_to_all(a, CHIPS, split_axis=0, concat_axis=0, tiled=True)  11.6 us
    ppermute x3, waiting for transfers between devices, on_device(): lax.ppermute(mixed, 'z', [(i, (i + n) % RING) for i in range(RING)])  10.8 us
    ppermute x6, starting transfers between devices, ring(): return [block] + [lax.ppermute(block, PLACES, turn) for turn in turns]  6.48 us
    ppermute x3, starting transfers between devices, on_device(): lax.ppermute(mixed, 'z', [(i, (i + n) % RING) for i in range(RING)])  4.57 us
    pallas_call x1, Pallas kernels, columns_call(): pl.pallas_call(columns_kernel, out_shape=in_vmem((columns, half, channels...  3.46 us
  transfers between devices with their start and end apart: 12, of which 7 were waited for; matrix products, arithmetic and copies ran while one was open for 0% of the time, Pallas kernels for 9%

profile of v4, /device:TPU:0, one launch (start us, length us, event | category | flops | bytes accessed | tf_op | source)
XLA Modules:
  0.0 107.3 jit_solution(14784024861573728560)
XLA Ops:
  0.0 3.0 %copy.16 = bf16[72,64,128]{2,0,1:T(8,128)(2,1)} copy(bf16[72,64,128]{2,1,0:T(8,128)(2,1)} %bitcast.20) | data formatting | bytes 2359296 | tf_op jit(solution)/shard_map/reshape | solution.py:386
  3.1 11.6 %all-to-all-start = ((bf16[64,72,128]{2,1,0:T(8,128)(2,1)}), bf16[64,72,128]{2,1,0:T(8,128)(2,1)S(1)}, u32[]{:S(2)}, u32[]{:S(2)}) async-start(bf16[64,72,128]{2,1,0:T(8,128)(2,1)} %bitcast.19), calls=%async_computation | async-start | bytes 2359296 | tf_op jit(solution)/shard_map/all_to_all | solution.py:384
  14.7 2.4 %bias_rows.1 = (bf16[3,48,128]{2,1,0:T(8,128)(2,1)S(1)}, bf16[3,48,128]{2,1,0:T(8,128)(2,1)S(1)}) custom-call(bf16[6,768,128]{2,1,0:T(8,128)(2,1)S(1)} %copy-done, f32[1,128]{1,0:T(1,128)S(1)} %bitcast.22, f32[1,128]{1,0:T(1,128)S(1)} %bitcast.24, bf16[4,128]{1,0:T(4,128)(2,1)S(1)} %bitcast.26), custom_call_target="tpu_custom_call" | custom-call | tf_op jit(solution)/shard_map/bias_rows/pallas_call | solution.py:78
  17.3 1.2 %collective-permute-done = bf16[3,48,128]{2,1,0:T(8,128)(2,1)S(1)} collective-permute-done((bf16[3,48,128]{2,1,0:T(8,128)(2,1)S(1)}, bf16[3,48,128]{2,1,0:T(8,128)(2,1)S(1)}, u32[]{:S(2)}, u32[]{:S(2)}) %collective-permute-start) | collective-permute-done | bytes 36896 | tf_op jit(solution)/shard_map/ppermute | solution.py:388
  18.5 2.9 %collective-permute-start.3 = (bf16[3,48,128]{2,1,0:T(8,128)(2,1)S(1)}, bf16[3,48,128]{2,1,0:T(8,128)(2,1)S(1)}, u32[]{:S(2)}, u32[]{:S(2)}) collective-permute-start(bf16[3,48,128]{2,1,0:T(8,128)(2,1)S(1)} %get-tuple-element.24), channel_id=1, source_target_pairs={{0,48},{16,0},{32,16},{48,32},{1,49},{17,1},{33,17},{49,33},{2,50}... | collective-permute-start | bytes 110600 | tf_op jit(solution)/shard_map/ppermute | solution.py:389
  21.4 0.8 collective-permute-start.2
  22.2 0.9 collective-permute-start.1
  23.1 5.2 %collective-permute-done.3 = bf16[3,48,128]{2,1,0:T(8,128)(2,1)S(1)} collective-permute-done((bf16[3,48,128]{2,1,0:T(8,128)(2,1)S(1)}, bf16[3,48,128]{2,1,0:T(8,128)(2,1)S(1)}, u32[]{:S(2)}, u32[]{:S(2)}) %collective-permute-start.3) | collective-permute-done | bytes 36896 | tf_op jit(solution)/shard_map/ppermute | solution.py:389
  28.3 5.1 %collective-permute-done.2 = bf16[3,48,128]{2,1,0:T(8,128)(2,1)S(1)} collective-permute-done((bf16[3,48,128]{2,1,0:T(8,128)(2,1)S(1)}, bf16[3,48,128]{2,1,0:T(8,128)(2,1)S(1)}, u32[]{:S(2)}, u32[]{:S(2)}) %collective-permute-start.2) | collective-permute-done | bytes 36896 | tf_op jit(solution)/shard_map/ppermute | solution.py:389
  33.4 0.4 collective-permute-done.1
  33.9 1.0 collective-permute-start.6
  34.9 1.2 %collective-permute-start.5 = (bf16[4,3,48,128]{3,2,1,0:T(8,128)(2,1)S(1)}, bf16[4,3,48,128]{3,2,1,0:T(8,128)(2,1)S(1)}, u32[]{:S(2)}, u32[]{:S(2)}) collective-permute-start(bf16[4,3,48,128]{3,2,1,0:T(8,128)(2,1)S(1)} %pad_maximum_fusion), channel_id=1, source_target_pairs={{0,2},{1,9},{2,0},{3,11},{4,6},{5,13},{6,4},{7,15},{8,10},{9,1},{1... | collective-permute-start | bytes 442376 | tf_op jit(solution)/shard_map/ppermute | solution.py:373
  36.2 3.5 %columns.1.cols_ref = bf16[12,384,128]{2,1,0:T(8,128)(2,1)S(1)} custom-call(bf16[64,72,128]{2,1,0:T(8,128)(2,1)S(1)} %all-to-all-done.got_ref, f32[1,128]{1,0:T(1,128)S(1)} %bitcast.23, f32[1,128]{1,0:T(1,128)S(1)} %bitcast.25), custom_call_target="tpu_custom_call" | custom-call | tf_op jit(solution)/shard_map/columns/pallas_call | solution.py:117
  39.6 1.2 %collective-permute-start.10 = (bf16[12,384,128]{2,1,0:T(8,128)(2,1)S(1)}, bf16[12,384,128]{2,1,0:T(8,128)(2,1)S(1)}, u32[]{:S(2)}, u32[]{:S(2)}) collective-permute-start(bf16[12,384,128]{2,1,0:T(8,128)(2,1)S(1)} %columns.1.cols_ref), channel_id=1, source_target_pairs={{0,1},{1,0},{2,3},{3,2},{4,5},{5,4},{6,7},{7,6},{8,9},{9,8},{10,11... | collective-permute-start | bytes 3538952 | tf_op jit(solution)/shard_map/ppermute | solution.py:394
  40.8 2.3 %collective-permute-done.4 = bf16[4,3,48,128]{3,2,1,0:T(8,128)(2,1)S(1)} collective-permute-done((bf16[4,3,48,128]{3,2,1,0:T(8,128)(2,1)S(1)}, bf16[4,3,48,128]{3,2,1,0:T(8,128)(2,1)S(1)}, u32[]{:S(2)}, u32[]{:S(2)}) %collective-permute-start.4) | collective-permute-done | bytes 147488 | tf_op jit(solution)/shard_map/ppermute | solution.py:373
  43.2 2.8 %collective-permute-start.9 = (bf16[16,3,48,128]{3,2,1,0:T(8,128)(2,1)S(1)}, bf16[16,3,48,128]{3,2,1,0:T(8,128)(2,1)S(1)}, u32[]{:S(2)}, u32[]{:S(2)}) collective-permute-start(bf16[16,3,48,128]{3,2,1,0:T(8,128)(2,1)S(1)} %constant_dynamic-update-slice_fusion.refs_0_), channel_id=1, source_target_pairs={{0,12},{1,67},{2,14},{3,65},{4,0},{5,71},{6,2},{7,69},{8,4},{9,75}... | collective-permute-start | bytes 1769480 | tf_op jit(solution)/shard_map/ppermute | solution.py:373
  46.0 1.2 %collective-permute-start.8 = (bf16[16,3,48,128]{3,2,1,0:T(8,128)(2,1)S(1)}, bf16[16,3,48,128]{3,2,1,0:T(8,128)(2,1)S(1)}, u32[]{:S(2)}, u32[]{:S(2)}) collective-permute-start(bf16[16,3,48,128]{3,2,1,0:T(8,128)(2,1)S(1)} %constant_dynamic-update-slice_fusion.refs_0_), channel_id=1, source_target_pairs={{0,8},{1,3},{2,10},{3,1},{4,12},{5,7},{6,14},{7,5},{8,0},{9,11},{1... | collective-permute-start | bytes 1769480 | tf_op jit(solution)/shard_map/ppermute | solution.py:373
  47.6 2.3 %own.1 = (bf16[12,128,384]{2,1,0:T(8,128)(2,1)S(1)}, bf16[12,128,384]{2,1,0:T(8,128)(2,1)S(1)}, bf16[12,384,128]{2,1,0:T(8,128)(2,1)S(1)}, bf16[12,2,80,384]{3,2,1,0:T(8,128)(2,1)S(1)}, bf16[12,128,384]{2,1,0:T(8,128)(2,1)S(1)}) custom-call(bf16[12,384,128]{2,1,0:T(8,128)(2,1)S(1)} %columns.1.cols_ref, bf16[128,128]{1,0:T(8,128)(2,1)S(1)} %copy-done.4, ...), custom_call_target="tpu_custom_call" | custom-call | tf_op jit(solution)/shard_map/own/pallas_call | solution.py:173
  49.9 1.3 %other.1 = (bf16[12,384,128]{2,1,0:T(8,128)(2,1)S(1)}, bf16[12,2,80,384]{3,2,1,0:T(8,128)(2,1)S(1)}) custom-call(bf16[12,384,128]{2,1,0:T(8,128)(2,1)S(1)} %collective-permute-done.10.cols_ref, bf16[128,128]{1,0:T(8,128)(2,1)S(1)} %copy-done.1, bf16[128,128]{1,0:T(8,128)(2,1)S(1)} %copy-done.2), custom_call_target="tpu_custom_call" | custom-call | tf_op jit(solution)/shard_map/other/pallas_call | solution.py:196
  51.2 8.6 %collective-permute-done.9.refs_3_ = bf16[16,3,48,128]{3,2,1,0:T(8,128)(2,1)S(1)} collective-permute-done((bf16[16,3,48,128]{3,2,1,0:T(8,128)(2,1)S(1)}, bf16[16,3,48,128]{3,2,1,0:T(8,128)(2,1)S(1)}, u32[]{:S(2)}, u32[]{:S(2)}) %collective-permute-start.9) | collective-permute-done | bytes 589856 | tf_op jit(solution)/shard_map/ppermute | solution.py:373
  59.8 3.9 %collective-permute-done.7.refs_1_ = bf16[16,3,48,128]{3,2,1,0:T(8,128)(2,1)S(1)} collective-permute-done((bf16[16,3,48,128]{3,2,1,0:T(8,128)(2,1)S(1)}, bf16[16,3,48,128]{3,2,1,0:T(8,128)(2,1)S(1)}, u32[]{:S(2)}, u32[]{:S(2)}) %collective-permute-start.7) | collective-permute-done | bytes 589856 | tf_op jit(solution)/shard_map/ppermute | solution.py:373
  63.8 19.6 %attend.1 = bf16[64,72,128]{2,1,0:T(8,128)(2,1)S(1)} custom-call(s32[6,128]{1,0:T(8,128)S(1)} %bitcast.21, bf16[16,3,48,128]{3,2,1,0:T(8,128)(2,1)S(1)} %constant_dynamic-update-slice_fusion.refs_0_, bf16[16,3,48,128]{3,2,1,0:T(8,128)(2,1)S(1)} %collective-permute-done.7.refs_1_, bf16[16,3,48,128]{3,2,1,0:T(8,128)(2,1)S(1)} %collective-permute-done.8.refs_2_, ...), custom_call_target="tpu_custom_call" | custom-call | tf_op jit(solution)/shard_map/attend/pallas_call | solution.py:341
  83.4 22.6 %all_to_all.10 = bf16[64,72,128]{2,1,0:T(8,128)(2,1)S(1)} all-to-all(bf16[64,72,128]{2,1,0:T(8,128)(2,1)S(1)} %attend.1), channel_id=1, replica_groups=mesh['ylo'=2,'z'=4,'x'=4,'yhi'=2,'core'=2] {'ylo','z','x','yhi'}, dimensions={0} | all-to-all | bytes 2359296 | tf_op jit(solution)/shard_map/all_to_all | solution.py:384
  106.0 1.3 %copy.14 = bf16[72,64,128]{2,1,0:T(8,128)(2,1)} copy(bf16[72,64,128]{2,0,1:T(8,128)(2,1)S(1)} %bitcast.29) | data formatting | bytes 2359296 | tf_op jit(solution)/shard_map/transpose | solution.py:399
  (40 shorter events, 0.6 us)
Async XLA Ops:
  3.0 11.7 %copy-start = (bf16[6,768,128]{2,1,0:T(8,128)(2,1)S(1)}, bf16[6,768,128]{2,1,0:T(8,128)(2,1)}, u32[]{:S(2)}) copy-start(bf16[6,768,128]{2,1,0:T(8,128)(2,1)} %pair_ref.1) | copy-start | bytes 3538948
  3.0 11.7 %copy-start.7 = (f32[128]{0:T(128)S(1)}, f32[128]{0:T(128)}, u32[]{:S(2)}) copy-start(f32[128]{0:T(128)} %param.14) | copy-start | bytes 1540
  3.1 11.7 %copy-start.8 = (f32[128]{0:T(128)S(1)}, f32[128]{0:T(128)}, u32[]{:S(2)}) copy-start(f32[128]{0:T(128)} %param.15) | copy-start | bytes 1540
  3.1 11.7 %copy-start.9 = (bf16[128,4]{0,1:T(4,128)(2,1)S(1)}, bf16[128,4]{0,1:T(4,128)(2,1)}, u32[]{:S(2)}) copy-start(bf16[128,4]{0,1:T(4,128)(2,1)} %param.21) | copy-start | bytes 3076
  3.1 33.1 %all-to-all-start = ((bf16[64,72,128]{2,1,0:T(8,128)(2,1)}), bf16[64,72,128]{2,1,0:T(8,128)(2,1)S(1)}, u32[]{:S(2)}, u32[]{:S(2)}) async-start(bf16[64,72,128]{2,1,0:T(8,128)(2,1)} %bitcast.19), calls=%async_computation | async-start | bytes 2359296 | tf_op jit(solution)/shard_map/all_to_all | solution.py:384
  17.2 1.3 %collective-permute-start = (bf16[3,48,128]{2,1,0:T(8,128)(2,1)S(1)}, bf16[3,48,128]{2,1,0:T(8,128)(2,1)S(1)}, u32[]{:S(2)}, u32[]{:S(2)}) collective-permute-start(bf16[3,48,128]{2,1,0:T(8,128)(2,1)S(1)} %get-tuple-element.15), channel_id=1, source_target_pairs={{0,1},{1,0},{2,3},{3,2},{4,5},{5,4},{6,7},{7,6},{8,9},{9,8},{10,11... | collective-permute-start | bytes 110600 | tf_op jit(solution)/shard_map/ppermute | solution.py:388
  18.5 9.8 %collective-permute-start.3 = (bf16[3,48,128]{2,1,0:T(8,128)(2,1)S(1)}, bf16[3,48,128]{2,1,0:T(8,128)(2,1)S(1)}, u32[]{:S(2)}, u32[]{:S(2)}) collective-permute-start(bf16[3,48,128]{2,1,0:T(8,128)(2,1)S(1)} %get-tuple-element.24), channel_id=1, source_target_pairs={{0,48},{16,0},{32,16},{48,32},{1,49},{17,1},{33,17},{49,33},{2,50}... | collective-permute-start | bytes 110600 | tf_op jit(solution)/shard_map/ppermute | solution.py:389
  21.4 12.1 %collective-permute-start.2 = (bf16[3,48,128]{2,1,0:T(8,128)(2,1)S(1)}, bf16[3,48,128]{2,1,0:T(8,128)(2,1)S(1)}, u32[]{:S(2)}, u32[]{:S(2)}) collective-permute-start(bf16[3,48,128]{2,1,0:T(8,128)(2,1)S(1)} %get-tuple-element.24), channel_id=1, source_target_pairs={{0,32},{16,48},{32,0},{48,16},{1,33},{17,49},{33,1},{49,17},{2,34}... | collective-permute-start | bytes 110600 | tf_op jit(solution)/shard_map/ppermute | solution.py:389
  22.2 11.6 %collective-permute-start.1 = (bf16[3,48,128]{2,1,0:T(8,128)(2,1)S(1)}, bf16[3,48,128]{2,1,0:T(8,128)(2,1)S(1)}, u32[]{:S(2)}, u32[]{:S(2)}) collective-permute-start(bf16[3,48,128]{2,1,0:T(8,128)(2,1)S(1)} %get-tuple-element.24), channel_id=1, source_target_pairs={{0,16},{16,32},{32,48},{48,0},{1,17},{17,33},{33,49},{49,1},{2,18}... | collective-permute-start | bytes 110600 | tf_op jit(solution)/shard_map/ppermute | solution.py:389
  33.9 9.3 %collective-permute-start.6 = (bf16[4,3,48,128]{3,2,1,0:T(8,128)(2,1)S(1)}, bf16[4,3,48,128]{3,2,1,0:T(8,128)(2,1)S(1)}, u32[]{:S(2)}, u32[]{:S(2)}) collective-permute-start(bf16[4,3,48,128]{3,2,1,0:T(8,128)(2,1)S(1)} %pad_maximum_fusion), channel_id=1, source_target_pairs={{0,66},{1,13},{2,64},{3,15},{4,70},{5,1},{6,68},{7,3},{8,74},{9,5}... | collective-permute-start | bytes 442376 | tf_op jit(solution)/shard_map/ppermute | solution.py:373
  34.9 8.3 %collective-permute-start.5 = (bf16[4,3,48,128]{3,2,1,0:T(8,128)(2,1)S(1)}, bf16[4,3,48,128]{3,2,1,0:T(8,128)(2,1)S(1)}, u32[]{:S(2)}, u32[]{:S(2)}) collective-permute-start(bf16[4,3,48,128]{3,2,1,0:T(8,128)(2,1)S(1)} %pad_maximum_fusion), channel_id=1, source_target_pairs={{0,2},{1,9},{2,0},{3,11},{4,6},{5,13},{6,4},{7,15},{8,10},{9,1},{1... | collective-permute-start | bytes 442376 | tf_op jit(solution)/shard_map/ppermute | solution.py:373
  36.1 7.1 %collective-permute-start.4 = (bf16[4,3,48,128]{3,2,1,0:T(8,128)(2,1)S(1)}, bf16[4,3,48,128]{3,2,1,0:T(8,128)(2,1)S(1)}, u32[]{:S(2)}, u32[]{:S(2)}) collective-permute-start(bf16[4,3,48,128]{3,2,1,0:T(8,128)(2,1)S(1)} %pad_maximum_fusion), channel_id=1, source_target_pairs={{0,64},{1,5},{2,66},{3,7},{4,68},{5,9},{6,70},{7,11},{8,72},{9,13}... | collective-permute-start | bytes 442376 | tf_op jit(solution)/shard_map/ppermute | solution.py:373
  36.1 11.4 %copy-start.1 = (bf16[128,128]{1,0:T(8,128)(2,1)S(1)}, bf16[128,128]{1,0:T(8,128)(2,1)}, u32[]{:S(2)}) copy-start(bf16[128,128]{1,0:T(8,128)(2,1)} %wk_ref.3) | copy-start | bytes 98308
  36.1 11.4 %copy-start.2 = (bf16[128,128]{1,0:T(8,128)(2,1)S(1)}, bf16[128,128]{1,0:T(8,128)(2,1)}, u32[]{:S(2)}) copy-start(bf16[128,128]{1,0:T(8,128)(2,1)} %wv_ref.3) | copy-start | bytes 98308
  36.1 11.4 %copy-start.4 = (bf16[128,128]{1,0:T(8,128)(2,1)S(1)}, bf16[128,128]{1,0:T(8,128)(2,1)}, u32[]{:S(2)}) copy-start(bf16[128,128]{1,0:T(8,128)(2,1)} %wq_ref.1) | copy-start | bytes 98308
  36.1 11.4 %copy-start.5 = (bf16[128,128]{1,0:T(8,128)(2,1)S(1)}, bf16[128,128]{1,0:T(8,128)(2,1)}, u32[]{:S(2)}) copy-start(bf16[128,128]{1,0:T(8,128)(2,1)} %wg_ref.1) | copy-start | bytes 98308
  36.1 11.4 %copy-start.10 = (f32[128]{0:T(128)S(1)}, f32[128]{0:T(128)}, u32[]{:S(2)}) copy-start(f32[128]{0:T(128)} %param.20) | copy-start | bytes 1540
  39.6 10.3 %collective-permute-start.10 = (bf16[12,384,128]{2,1,0:T(8,128)(2,1)S(1)}, bf16[12,384,128]{2,1,0:T(8,128)(2,1)S(1)}, u32[]{:S(2)}, u32[]{:S(2)}) collective-permute-start(bf16[12,384,128]{2,1,0:T(8,128)(2,1)S(1)} %columns.1.cols_ref), channel_id=1, source_target_pairs={{0,1},{1,0},{2,3},{3,2},{4,5},{5,4},{6,7},{7,6},{8,9},{9,8},{10,11... | collective-permute-start | bytes 3538952 | tf_op jit(solution)/shard_map/ppermute | solution.py:394
  43.2 16.6 %collective-permute-start.9 = (bf16[16,3,48,128]{3,2,1,0:T(8,128)(2,1)S(1)}, bf16[16,3,48,128]{3,2,1,0:T(8,128)(2,1)S(1)}, u32[]{:S(2)}, u32[]{:S(2)}) collective-permute-start(bf16[16,3,48,128]{3,2,1,0:T(8,128)(2,1)S(1)} %constant_dynamic-update-slice_fusion.refs_0_), channel_id=1, source_target_pairs={{0,12},{1,67},{2,14},{3,65},{4,0},{5,71},{6,2},{7,69},{8,4},{9,75}... | collective-permute-start | bytes 1769480 | tf_op jit(solution)/shard_map/ppermute | solution.py:373
  46.0 13.8 %collective-permute-start.8 = (bf16[16,3,48,128]{3,2,1,0:T(8,128)(2,1)S(1)}, bf16[16,3,48,128]{3,2,1,0:T(8,128)(2,1)S(1)}, u32[]{:S(2)}, u32[]{:S(2)}) collective-permute-start(bf16[16,3,48,128]{3,2,1,0:T(8,128)(2,1)S(1)} %constant_dynamic-update-slice_fusion.refs_0_), channel_id=1, source_target_pairs={{0,8},{1,3},{2,10},{3,1},{4,12},{5,7},{6,14},{7,5},{8,0},{9,11},{1... | collective-permute-start | bytes 1769480 | tf_op jit(solution)/shard_map/ppermute | solution.py:373
  47.2 16.5 %collective-permute-start.7 = (bf16[16,3,48,128]{3,2,1,0:T(8,128)(2,1)S(1)}, bf16[16,3,48,128]{3,2,1,0:T(8,128)(2,1)S(1)}, u32[]{:S(2)}, u32[]{:S(2)}) collective-permute-start(bf16[16,3,48,128]{3,2,1,0:T(8,128)(2,1)S(1)} %constant_dynamic-update-slice_fusion.refs_0_), channel_id=1, source_target_pairs={{0,4},{1,65},{2,6},{3,67},{4,8},{5,69},{6,10},{7,71},{8,12},{9,73}... | collective-permute-start | bytes 1769480 | tf_op jit(solution)/shard_map/ppermute | solution.py:373
  47.5 16.2 %copy-start.3 = (bf16[128,128]{1,0:T(8,128)(2,1)S(1)}, bf16[128,128]{1,0:T(8,128)(2,1)}, u32[]{:S(2)}) copy-start(bf16[128,128]{1,0:T(8,128)(2,1)} %refs_11_.1) | copy-start | bytes 98308
  47.5 16.2 %copy-start.6 = (s32[768]{0:T(1024)S(1)}, s32[768]{0:T(1024)}, u32[]{:S(2)}) copy-start(s32[768]{0:T(1024)} %param.13) | copy-start | bytes 9220
  47.6 16.2 %copy-start.11 = (f32[128]{0:T(128)S(1)}, f32[128]{0:T(128)}, u32[]{:S(2)}) copy-start(f32[128]{0:T(128)} %param.23) | copy-start | bytes 1540

commit v5 on v4

--- a/solution.py
+++ b/solution.py
@@ -222,26 +222,29 @@
     pairs = HEADS // 2
     count = jnp.sum(mask_ref[...])
     my_x, my_y, my_z = lax.axis_index("x"), 2 * lax.axis_index("yhi") + lax.axis_index("ylo"), lax.axis_index("z")
-    back = lambda mine, turn: (mine + RING - turn) % RING
-
-    for n in range(parts):
-        def widen(i, _):
-            z = back(my_z, i % RING)
-            for turn, bias_ref in enumerate(bias_refs):
-                x = back(my_x, jnp.where(core == 0, turn, i // RING))
-                y = back(my_y, jnp.where(core == 0, i // RING, turn))
-                s = (y % 2) * (2 * RING * RING) + z * (2 * RING) + x * 2 + y // 2
-                at = pl.ds(pl.multiple_of(s * packed, 8), packed)
-                raw_ref[n % 2, at, :] = bias_ref[i, n].astype(F32) * LOG2E
-            return 0
-
-        lax.fori_loop(0, RING * RING, widen, 0)
-        place = lax.broadcasted_iota(jnp.int32, (half, LANES), 0)
-        for side in range(2):
-            real = core if side == 0 else 1 - core
-            valid = place + (place // rows) * rows + real * rows < count
+    back = lambda mine, turn: (mine + RING - turn) & (RING - 1)
+
+    def widen(i, _):
+        z = back(my_z, i & (RING - 1))
+        middle = i >> (RING.bit_length() - 1)
+        for turn, bias_ref in enumerate(bias_refs):
+            x = back(my_x, jnp.where(core == 0, turn, middle))
+            y = back(my_y, jnp.where(core == 0, middle, turn))
+            s = (y & 1) * (2 * RING * RING) + z * (2 * RING) + x * 2 + (y >> 1)
+            at = pl.ds(pl.multiple_of(s * packed, 8), packed)
+            for n in range(parts):
+                raw_ref[n, at, :] = bias_ref[i, n].astype(F32) * LOG2E
+        return 0
+
+    lax.fori_loop(0, RING * RING, widen, 0, unroll=2)
+    place = lax.broadcasted_iota(jnp.int32, (half, LANES), 0)
+    for side in range(2):
+        real = core if side == 0 else 1 - core
+        whole = count // (2 * rows)
+        valid = place < whole * rows + jnp.clip(count - whole * (2 * rows) - real * rows, 0, rows)
+        for n in range(parts):
             for h in range(HEADS):
-                got = raw_ref[n % 2, pl.ds(side * HEADS + h, half, stride=2 * HEADS), :]
+                got = raw_ref[n, pl.ds(side * HEADS + h, half, stride=2 * HEADS), :]
                 add_ref[n, h // 2, side * half : (side + 1) * half, (h % 2) * LANES : (h % 2 + 1) * LANES] = (
                     jnp.where(valid, got, -1e9)
                 )
@@ -286,7 +289,7 @@
         upd_ref[pl.ds(t, half, stride=columns), :] = update
 
     def column(take, t, tops):
-        slot = t % 2
+        slot = t & 1
         after = jnp.minimum(t + 1, columns - 1)
         load_queries(after, 1 - slot)
         for i in range(len(units)):
@@ -344,7 +347,7 @@
         in_specs=[VM] * (3 + len(near)),
         out_specs=VM,
         scratch_shapes=[
-            pltpu.VMEM((2, sources * 2 * rows * HEADS, LANES), F32),
+            pltpu.VMEM((parts, sources * 2 * rows * HEADS, LANES), F32),
             pltpu.VMEM((parts, HEADS // 2, 2 * half, 2 * LANES), F32),
             pltpu.VMEM((2, parts, HEADS // 2, 2 * channels, 2 * LANES), BF),
             pltpu.VMEM((3, 2 * half, 2 * LANES), F32),

time: 108 us -> 105 us (0.972); the launches traced: 107 us -> 106 us
  no operation moved by 1% of the time
where the time goes in v5:
time: 105 us; the launch traced here: 106 us
  Pallas kernels  28.1 us (27%)
  waiting for transfers between devices  26.9 us (26%)
  starting transfers between devices  23.9 us (23%)
  blocking collectives  22.6 us (22%)
  local copies, waits for them, and re-layouts  4.52 us (4%)
    all_to_all x1, blocking collectives, on_device(): lax.all_to_all(a, CHIPS, split_axis=0, concat_axis=0, tiled=True)  22.6 us
    pallas_call x1, Pallas kernels, attend_call(): pl.pallas_call(attend_kernel, out_shape=in_vmem((sources, rows * columns,...  18.6 us
    ppermute x6, waiting for transfers between devices, ring(): return [block] + [lax.ppermute(block, PLACES, turn) for turn in turns]  14.9 us
    all_to_all x1, starting transfers between devices, on_device(): lax.all_to_all(a, CHIPS, split_axis=0, concat_axis=0, tiled=True)  11.6 us
    ppermute x3, waiting for transfers between devices, on_device(): lax.ppermute(mixed, 'z', [(i, (i + n) % RING) for i in range(RING)])  10.8 us
    ppermute x6, starting transfers between devices, ring(): return [block] + [lax.ppermute(block, PLACES, turn) for turn in turns]  6.48 us
    ppermute x3, starting transfers between devices, on_device(): lax.ppermute(mixed, 'z', [(i, (i + n) % RING) for i in range(RING)])  4.57 us
    pallas_call x1, Pallas kernels, columns_call(): pl.pallas_call(columns_kernel, out_shape=in_vmem((columns, half, channels...  3.46 us
  transfers between devices with their start and end apart: 12, of which 7 were waited for; matrix products, arithmetic and copies ran while one was open for 0% of the time, Pallas kernels for 9%

profile of v5, /device:TPU:0, one launch (start us, length us, event | category | flops | bytes accessed | tf_op | source)
XLA Modules:
  0.0 106.3 jit_solution(17020001254403111900)
XLA Ops:
  0.0 3.0 %copy.16 = bf16[72,64,128]{2,0,1:T(8,128)(2,1)} copy(bf16[72,64,128]{2,1,0:T(8,128)(2,1)} %bitcast.20) | data formatting | bytes 2359296 | tf_op jit(solution)/shard_map/reshape | solution.py:389
  3.1 11.6 %all-to-all-start = ((bf16[64,72,128]{2,1,0:T(8,128)(2,1)}), bf16[64,72,128]{2,1,0:T(8,128)(2,1)S(1)}, u32[]{:S(2)}, u32[]{:S(2)}) async-start(bf16[64,72,128]{2,1,0:T(8,128)(2,1)} %bitcast.19), calls=%async_computation | async-start | bytes 2359296 | tf_op jit(solution)/shard_map/all_to_all | solution.py:387
  14.7 2.4 %bias_rows.1 = (bf16[3,48,128]{2,1,0:T(8,128)(2,1)S(1)}, bf16[3,48,128]{2,1,0:T(8,128)(2,1)S(1)}) custom-call(bf16[6,768,128]{2,1,0:T(8,128)(2,1)S(1)} %copy-done, f32[1,128]{1,0:T(1,128)S(1)} %bitcast.22, f32[1,128]{1,0:T(1,128)S(1)} %bitcast.24, bf16[4,128]{1,0:T(4,128)(2,1)S(1)} %bitcast.26), custom_call_target="tpu_custom_call" | custom-call | tf_op jit(solution)/shard_map/bias_rows/pallas_call | solution.py:78
  17.3 1.2 %collective-permute-done = bf16[3,48,128]{2,1,0:T(8,128)(2,1)S(1)} collective-permute-done((bf16[3,48,128]{2,1,0:T(8,128)(2,1)S(1)}, bf16[3,48,128]{2,1,0:T(8,128)(2,1)S(1)}, u32[]{:S(2)}, u32[]{:S(2)}) %collective-permute-start) | collective-permute-done | bytes 36896 | tf_op jit(solution)/shard_map/ppermute | solution.py:391
  18.5 2.9 %collective-permute-start.3 = (bf16[3,48,128]{2,1,0:T(8,128)(2,1)S(1)}, bf16[3,48,128]{2,1,0:T(8,128)(2,1)S(1)}, u32[]{:S(2)}, u32[]{:S(2)}) collective-permute-start(bf16[3,48,128]{2,1,0:T(8,128)(2,1)S(1)} %get-tuple-element.24), channel_id=1, source_target_pairs={{0,48},{16,0},{32,16},{48,32},{1,49},{17,1},{33,17},{49,33},{2,50}... | collective-permute-start | bytes 110600 | tf_op jit(solution)/shard_map/ppermute | solution.py:392
  21.4 0.8 collective-permute-start.2
  22.2 0.9 collective-permute-start.1
  23.1 5.2 %collective-permute-done.3 = bf16[3,48,128]{2,1,0:T(8,128)(2,1)S(1)} collective-permute-done((bf16[3,48,128]{2,1,0:T(8,128)(2,1)S(1)}, bf16[3,48,128]{2,1,0:T(8,128)(2,1)S(1)}, u32[]{:S(2)}, u32[]{:S(2)}) %collective-permute-start.3) | collective-permute-done | bytes 36896 | tf_op jit(solution)/shard_map/ppermute | solution.py:392
  28.3 5.1 %collective-permute-done.2 = bf16[3,48,128]{2,1,0:T(8,128)(2,1)S(1)} collective-permute-done((bf16[3,48,128]{2,1,0:T(8,128)(2,1)S(1)}, bf16[3,48,128]{2,1,0:T(8,128)(2,1)S(1)}, u32[]{:S(2)}, u32[]{:S(2)}) %collective-permute-start.2) | collective-permute-done | bytes 36896 | tf_op jit(solution)/shard_map/ppermute | solution.py:392
  33.4 0.4 collective-permute-done.1
  33.9 1.0 collective-permute-start.6
  34.9 1.2 %collective-permute-start.5 = (bf16[4,3,48,128]{3,2,1,0:T(8,128)(2,1)S(1)}, bf16[4,3,48,128]{3,2,1,0:T(8,128)(2,1)S(1)}, u32[]{:S(2)}, u32[]{:S(2)}) collective-permute-start(bf16[4,3,48,128]{3,2,1,0:T(8,128)(2,1)S(1)} %pad_maximum_fusion), channel_id=1, source_target_pairs={{0,2},{1,9},{2,0},{3,11},{4,6},{5,13},{6,4},{7,15},{8,10},{9,1},{1... | collective-permute-start | bytes 442376 | tf_op jit(solution)/shard_map/ppermute | solution.py:376
  36.2 3.5 %columns.1.cols_ref = bf16[12,384,128]{2,1,0:T(8,128)(2,1)S(1)} custom-call(bf16[64,72,128]{2,1,0:T(8,128)(2,1)S(1)} %all-to-all-done.got_ref, f32[1,128]{1,0:T(1,128)S(1)} %bitcast.23, f32[1,128]{1,0:T(1,128)S(1)} %bitcast.25), custom_call_target="tpu_custom_call" | custom-call | tf_op jit(solution)/shard_map/columns/pallas_call | solution.py:117
  39.6 1.2 %collective-permute-start.10 = (bf16[12,384,128]{2,1,0:T(8,128)(2,1)S(1)}, bf16[12,384,128]{2,1,0:T(8,128)(2,1)S(1)}, u32[]{:S(2)}, u32[]{:S(2)}) collective-permute-start(bf16[12,384,128]{2,1,0:T(8,128)(2,1)S(1)} %columns.1.cols_ref), channel_id=1, source_target_pairs={{0,1},{1,0},{2,3},{3,2},{4,5},{5,4},{6,7},{7,6},{8,9},{9,8},{10,11... | collective-permute-start | bytes 3538952 | tf_op jit(solution)/shard_map/ppermute | solution.py:397
  40.8 2.3 %collective-permute-done.4 = bf16[4,3,48,128]{3,2,1,0:T(8,128)(2,1)S(1)} collective-permute-done((bf16[4,3,48,128]{3,2,1,0:T(8,128)(2,1)S(1)}, bf16[4,3,48,128]{3,2,1,0:T(8,128)(2,1)S(1)}, u32[]{:S(2)}, u32[]{:S(2)}) %collective-permute-start.4) | collective-permute-done | bytes 147488 | tf_op jit(solution)/shard_map/ppermute | solution.py:376
  43.2 2.8 %collective-permute-start.9 = (bf16[16,3,48,128]{3,2,1,0:T(8,128)(2,1)S(1)}, bf16[16,3,48,128]{3,2,1,0:T(8,128)(2,1)S(1)}, u32[]{:S(2)}, u32[]{:S(2)}) collective-permute-start(bf16[16,3,48,128]{3,2,1,0:T(8,128)(2,1)S(1)} %constant_dynamic-update-slice_fusion.refs_0_), channel_id=1, source_target_pairs={{0,12},{1,67},{2,14},{3,65},{4,0},{5,71},{6,2},{7,69},{8,4},{9,75}... | collective-permute-start | bytes 1769480 | tf_op jit(solution)/shard_map/ppermute | solution.py:376
  46.0 1.2 %collective-permute-start.8 = (bf16[16,3,48,128]{3,2,1,0:T(8,128)(2,1)S(1)}, bf16[16,3,48,128]{3,2,1,0:T(8,128)(2,1)S(1)}, u32[]{:S(2)}, u32[]{:S(2)}) collective-permute-start(bf16[16,3,48,128]{3,2,1,0:T(8,128)(2,1)S(1)} %constant_dynamic-update-slice_fusion.refs_0_), channel_id=1, source_target_pairs={{0,8},{1,3},{2,10},{3,1},{4,12},{5,7},{6,14},{7,5},{8,0},{9,11},{1... | collective-permute-start | bytes 1769480 | tf_op jit(solution)/shard_map/ppermute | solution.py:376
  47.6 2.3 %own.1 = (bf16[12,128,384]{2,1,0:T(8,128)(2,1)S(1)}, bf16[12,128,384]{2,1,0:T(8,128)(2,1)S(1)}, bf16[12,384,128]{2,1,0:T(8,128)(2,1)S(1)}, bf16[12,2,80,384]{3,2,1,0:T(8,128)(2,1)S(1)}, bf16[12,128,384]{2,1,0:T(8,128)(2,1)S(1)}) custom-call(bf16[12,384,128]{2,1,0:T(8,128)(2,1)S(1)} %columns.1.cols_ref, bf16[128,128]{1,0:T(8,128)(2,1)S(1)} %copy-done.4, ...), custom_call_target="tpu_custom_call" | custom-call | tf_op jit(solution)/shard_map/own/pallas_call | solution.py:173
  49.9 1.3 %other.1 = (bf16[12,384,128]{2,1,0:T(8,128)(2,1)S(1)}, bf16[12,2,80,384]{3,2,1,0:T(8,128)(2,1)S(1)}) custom-call(bf16[12,384,128]{2,1,0:T(8,128)(2,1)S(1)} %collective-permute-done.10.cols_ref, bf16[128,128]{1,0:T(8,128)(2,1)S(1)} %copy-done.1, bf16[128,128]{1,0:T(8,128)(2,1)S(1)} %copy-done.2), custom_call_target="tpu_custom_call" | custom-call | tf_op jit(solution)/shard_map/other/pallas_call | solution.py:196
  51.2 8.6 %collective-permute-done.9.refs_3_ = bf16[16,3,48,128]{3,2,1,0:T(8,128)(2,1)S(1)} collective-permute-done((bf16[16,3,48,128]{3,2,1,0:T(8,128)(2,1)S(1)}, bf16[16,3,48,128]{3,2,1,0:T(8,128)(2,1)S(1)}, u32[]{:S(2)}, u32[]{:S(2)}) %collective-permute-start.9) | collective-permute-done | bytes 589856 | tf_op jit(solution)/shard_map/ppermute | solution.py:376
  59.8 3.9 %collective-permute-done.7.refs_1_ = bf16[16,3,48,128]{3,2,1,0:T(8,128)(2,1)S(1)} collective-permute-done((bf16[16,3,48,128]{3,2,1,0:T(8,128)(2,1)S(1)}, bf16[16,3,48,128]{3,2,1,0:T(8,128)(2,1)S(1)}, u32[]{:S(2)}, u32[]{:S(2)}) %collective-permute-start.7) | collective-permute-done | bytes 589856 | tf_op jit(solution)/shard_map/ppermute | solution.py:376
  63.8 18.6 %attend.1 = bf16[64,72,128]{2,1,0:T(8,128)(2,1)S(1)} custom-call(s32[6,128]{1,0:T(8,128)S(1)} %bitcast.21, bf16[16,3,48,128]{3,2,1,0:T(8,128)(2,1)S(1)} %constant_dynamic-update-slice_fusion.refs_0_, bf16[16,3,48,128]{3,2,1,0:T(8,128)(2,1)S(1)} %collective-permute-done.7.refs_1_, bf16[16,3,48,128]{3,2,1,0:T(8,128)(2,1)S(1)} %collective-permute-done.8.refs_2_, ...), custom_call_target="tpu_custom_call" | custom-call | tf_op jit(solution)/shard_map/attend/pallas_call | solution.py:344
  82.4 22.6 %all_to_all.10 = bf16[64,72,128]{2,1,0:T(8,128)(2,1)S(1)} all-to-all(bf16[64,72,128]{2,1,0:T(8,128)(2,1)S(1)} %attend.1), channel_id=1, replica_groups=mesh['ylo'=2,'z'=4,'x'=4,'yhi'=2,'core'=2] {'ylo','z','x','yhi'}, dimensions={0} | all-to-all | bytes 2359296 | tf_op jit(solution)/shard_map/all_to_all | solution.py:387
  105.0 1.3 %copy.14 = bf16[72,64,128]{2,1,0:T(8,128)(2,1)} copy(bf16[72,64,128]{2,0,1:T(8,128)(2,1)S(1)} %bitcast.29) | data formatting | bytes 2359296 | tf_op jit(solution)/shard_map/transpose | solution.py:402
  (40 shorter events, 0.6 us)
Async XLA Ops:
  3.0 11.7 %copy-start = (bf16[6,768,128]{2,1,0:T(8,128)(2,1)S(1)}, bf16[6,768,128]{2,1,0:T(8,128)(2,1)}, u32[]{:S(2)}) copy-start(bf16[6,768,128]{2,1,0:T(8,128)(2,1)} %pair_ref.1) | copy-start | bytes 3538948
  3.0 11.7 %copy-start.7 = (f32[128]{0:T(128)S(1)}, f32[128]{0:T(128)}, u32[]{:S(2)}) copy-start(f32[128]{0:T(128)} %param.14) | copy-start | bytes 1540
  3.1 11.7 %copy-start.8 = (f32[128]{0:T(128)S(1)}, f32[128]{0:T(128)}, u32[]{:S(2)}) copy-start(f32[128]{0:T(128)} %param.15) | copy-start | bytes 1540
  3.1 11.7 %copy-start.9 = (bf16[128,4]{0,1:T(4,128)(2,1)S(1)}, bf16[128,4]{0,1:T(4,128)(2,1)}, u32[]{:S(2)}) copy-start(bf16[128,4]{0,1:T(4,128)(2,1)} %param.21) | copy-start | bytes 3076
  3.1 33.1 %all-to-all-start = ((bf16[64,72,128]{2,1,0:T(8,128)(2,1)}), bf16[64,72,128]{2,1,0:T(8,128)(2,1)S(1)}, u32[]{:S(2)}, u32[]{:S(2)}) async-start(bf16[64,72,128]{2,1,0:T(8,128)(2,1)} %bitcast.19), calls=%async_computation | async-start | bytes 2359296 | tf_op jit(solution)/shard_map/all_to_all | solution.py:387
  17.2 1.3 %collective-permute-start = (bf16[3,48,128]{2,1,0:T(8,128)(2,1)S(1)}, bf16[3,48,128]{2,1,0:T(8,128)(2,1)S(1)}, u32[]{:S(2)}, u32[]{:S(2)}) collective-permute-start(bf16[3,48,128]{2,1,0:T(8,128)(2,1)S(1)} %get-tuple-element.15), channel_id=1, source_target_pairs={{0,1},{1,0},{2,3},{3,2},{4,5},{5,4},{6,7},{7,6},{8,9},{9,8},{10,11... | collective-permute-start | bytes 110600 | tf_op jit(solution)/shard_map/ppermute | solution.py:391
  18.5 9.8 %collective-permute-start.3 = (bf16[3,48,128]{2,1,0:T(8,128)(2,1)S(1)}, bf16[3,48,128]{2,1,0:T(8,128)(2,1)S(1)}, u32[]{:S(2)}, u32[]{:S(2)}) collective-permute-start(bf16[3,48,128]{2,1,0:T(8,128)(2,1)S(1)} %get-tuple-element.24), channel_id=1, source_target_pairs={{0,48},{16,0},{32,16},{48,32},{1,49},{17,1},{33,17},{49,33},{2,50}... | collective-permute-start | bytes 110600 | tf_op jit(solution)/shard_map/ppermute | solution.py:392
  21.4 12.1 %collective-permute-start.2 = (bf16[3,48,128]{2,1,0:T(8,128)(2,1)S(1)}, bf16[3,48,128]{2,1,0:T(8,128)(2,1)S(1)}, u32[]{:S(2)}, u32[]{:S(2)}) collective-permute-start(bf16[3,48,128]{2,1,0:T(8,128)(2,1)S(1)} %get-tuple-element.24), channel_id=1, source_target_pairs={{0,32},{16,48},{32,0},{48,16},{1,33},{17,49},{33,1},{49,17},{2,34}... | collective-permute-start | bytes 110600 | tf_op jit(solution)/shard_map/ppermute | solution.py:392
  22.2 11.6 %collective-permute-start.1 = (bf16[3,48,128]{2,1,0:T(8,128)(2,1)S(1)}, bf16[3,48,128]{2,1,0:T(8,128)(2,1)S(1)}, u32[]{:S(2)}, u32[]{:S(2)}) collective-permute-start(bf16[3,48,128]{2,1,0:T(8,128)(2,1)S(1)} %get-tuple-element.24), channel_id=1, source_target_pairs={{0,16},{16,32},{32,48},{48,0},{1,17},{17,33},{33,49},{49,1},{2,18}... | collective-permute-start | bytes 110600 | tf_op jit(solution)/shard_map/ppermute | solution.py:392
  33.9 9.3 %collective-permute-start.6 = (bf16[4,3,48,128]{3,2,1,0:T(8,128)(2,1)S(1)}, bf16[4,3,48,128]{3,2,1,0:T(8,128)(2,1)S(1)}, u32[]{:S(2)}, u32[]{:S(2)}) collective-permute-start(bf16[4,3,48,128]{3,2,1,0:T(8,128)(2,1)S(1)} %pad_maximum_fusion), channel_id=1, source_target_pairs={{0,66},{1,13},{2,64},{3,15},{4,70},{5,1},{6,68},{7,3},{8,74},{9,5}... | collective-permute-start | bytes 442376 | tf_op jit(solution)/shard_map/ppermute | solution.py:376
  34.9 8.3 %collective-permute-start.5 = (bf16[4,3,48,128]{3,2,1,0:T(8,128)(2,1)S(1)}, bf16[4,3,48,128]{3,2,1,0:T(8,128)(2,1)S(1)}, u32[]{:S(2)}, u32[]{:S(2)}) collective-permute-start(bf16[4,3,48,128]{3,2,1,0:T(8,128)(2,1)S(1)} %pad_maximum_fusion), channel_id=1, source_target_pairs={{0,2},{1,9},{2,0},{3,11},{4,6},{5,13},{6,4},{7,15},{8,10},{9,1},{1... | collective-permute-start | bytes 442376 | tf_op jit(solution)/shard_map/ppermute | solution.py:376
  36.1 7.1 %collective-permute-start.4 = (bf16[4,3,48,128]{3,2,1,0:T(8,128)(2,1)S(1)}, bf16[4,3,48,128]{3,2,1,0:T(8,128)(2,1)S(1)}, u32[]{:S(2)}, u32[]{:S(2)}) collective-permute-start(bf16[4,3,48,128]{3,2,1,0:T(8,128)(2,1)S(1)} %pad_maximum_fusion), channel_id=1, source_target_pairs={{0,64},{1,5},{2,66},{3,7},{4,68},{5,9},{6,70},{7,11},{8,72},{9,13}... | collective-permute-start | bytes 442376 | tf_op jit(solution)/shard_map/ppermute | solution.py:376
  36.1 11.4 %copy-start.1 = (bf16[128,128]{1,0:T(8,128)(2,1)S(1)}, bf16[128,128]{1,0:T(8,128)(2,1)}, u32[]{:S(2)}) copy-start(bf16[128,128]{1,0:T(8,128)(2,1)} %wk_ref.3) | copy-start | bytes 98308
  36.1 11.4 %copy-start.2 = (bf16[128,128]{1,0:T(8,128)(2,1)S(1)}, bf16[128,128]{1,0:T(8,128)(2,1)}, u32[]{:S(2)}) copy-start(bf16[128,128]{1,0:T(8,128)(2,1)} %wv_ref.3) | copy-start | bytes 98308
  36.1 11.4 %copy-start.4 = (bf16[128,128]{1,0:T(8,128)(2,1)S(1)}, bf16[128,128]{1,0:T(8,128)(2,1)}, u32[]{:S(2)}) copy-start(bf16[128,128]{1,0:T(8,128)(2,1)} %wq_ref.1) | copy-start | bytes 98308
  36.1 11.4 %copy-start.5 = (bf16[128,128]{1,0:T(8,128)(2,1)S(1)}, bf16[128,128]{1,0:T(8,128)(2,1)}, u32[]{:S(2)}) copy-start(bf16[128,128]{1,0:T(8,128)(2,1)} %wg_ref.1) | copy-start | bytes 98308
  36.1 11.4 %copy-start.10 = (f32[128]{0:T(128)S(1)}, f32[128]{0:T(128)}, u32[]{:S(2)}) copy-start(f32[128]{0:T(128)} %param.20) | copy-start | bytes 1540
  39.6 10.3 %collective-permute-start.10 = (bf16[12,384,128]{2,1,0:T(8,128)(2,1)S(1)}, bf16[12,384,128]{2,1,0:T(8,128)(2,1)S(1)}, u32[]{:S(2)}, u32[]{:S(2)}) collective-permute-start(bf16[12,384,128]{2,1,0:T(8,128)(2,1)S(1)} %columns.1.cols_ref), channel_id=1, source_target_pairs={{0,1},{1,0},{2,3},{3,2},{4,5},{5,4},{6,7},{7,6},{8,9},{9,8},{10,11... | collective-permute-start | bytes 3538952 | tf_op jit(solution)/shard_map/ppermute | solution.py:397
  43.2 16.6 %collective-permute-start.9 = (bf16[16,3,48,128]{3,2,1,0:T(8,128)(2,1)S(1)}, bf16[16,3,48,128]{3,2,1,0:T(8,128)(2,1)S(1)}, u32[]{:S(2)}, u32[]{:S(2)}) collective-permute-start(bf16[16,3,48,128]{3,2,1,0:T(8,128)(2,1)S(1)} %constant_dynamic-update-slice_fusion.refs_0_), channel_id=1, source_target_pairs={{0,12},{1,67},{2,14},{3,65},{4,0},{5,71},{6,2},{7,69},{8,4},{9,75}... | collective-permute-start | bytes 1769480 | tf_op jit(solution)/shard_map/ppermute | solution.py:376
  46.0 13.8 %collective-permute-start.8 = (bf16[16,3,48,128]{3,2,1,0:T(8,128)(2,1)S(1)}, bf16[16,3,48,128]{3,2,1,0:T(8,128)(2,1)S(1)}, u32[]{:S(2)}, u32[]{:S(2)}) collective-permute-start(bf16[16,3,48,128]{3,2,1,0:T(8,128)(2,1)S(1)} %constant_dynamic-update-slice_fusion.refs_0_), channel_id=1, source_target_pairs={{0,8},{1,3},{2,10},{3,1},{4,12},{5,7},{6,14},{7,5},{8,0},{9,11},{1... | collective-permute-start | bytes 1769480 | tf_op jit(solution)/shard_map/ppermute | solution.py:376
  47.2 16.5 %collective-permute-start.7 = (bf16[16,3,48,128]{3,2,1,0:T(8,128)(2,1)S(1)}, bf16[16,3,48,128]{3,2,1,0:T(8,128)(2,1)S(1)}, u32[]{:S(2)}, u32[]{:S(2)}) collective-permute-start(bf16[16,3,48,128]{3,2,1,0:T(8,128)(2,1)S(1)} %constant_dynamic-update-slice_fusion.refs_0_), channel_id=1, source_target_pairs={{0,4},{1,65},{2,6},{3,67},{4,8},{5,69},{6,10},{7,71},{8,12},{9,73}... | collective-permute-start | bytes 1769480 | tf_op jit(solution)/shard_map/ppermute | solution.py:376
  47.5 16.2 %copy-start.3 = (bf16[128,128]{1,0:T(8,128)(2,1)S(1)}, bf16[128,128]{1,0:T(8,128)(2,1)}, u32[]{:S(2)}) copy-start(bf16[128,128]{1,0:T(8,128)(2,1)} %refs_11_.1) | copy-start | bytes 98308
  47.5 16.2 %copy-start.6 = (s32[768]{0:T(1024)S(1)}, s32[768]{0:T(1024)}, u32[]{:S(2)}) copy-start(s32[768]{0:T(1024)} %param.13) | copy-start | bytes 9220
  47.6 16.2 %copy-start.11 = (f32[128]{0:T(128)S(1)}, f32[128]{0:T(128)}, u32[]{:S(2)}) copy-start(f32[128]{0:T(128)} %param.23) | copy-start | bytes 1540

commit v6 on v5

--- a/solution.py
+++ b/solution.py
@@ -260,22 +260,27 @@
                 q_ref[slot, n, h // 2, mine, to] = qhi_ref[t, mine, at]
                 q_ref[slot, n, h // 2, channels + h * DIM : channels + (h + 1) * DIM, to] = qlo_ref[t, mine, at]
 
-    def score(t, slot, i, take):
+    key_refs, val_refs = (key0_ref, key1_ref), (val0_ref, val1_ref)
+
+    def score(t, slot, i, side, take):
         n, p = units[i]
-        key = jnp.concatenate([key0_ref[t, :take], key1_ref[t, :take]], axis=0)
+        key = key_refs[side][t, :take]
         key = jnp.concatenate([key, key], axis=1)
         scores = jnp.dot(key, q_ref[slot, n, p], preferred_element_type=F32)
-        own = scores[:take] + add_ref[n, p, :take]
-        other = scores[take:] + add_ref[n, p, half : half + take]
-        score_ref[i % 3, :take] = own
-        score_ref[i % 3, take : 2 * take] = other
-        return jnp.maximum(jnp.max(own, axis=0, keepdims=True), jnp.max(other, axis=0, keepdims=True))
-
-    def combine(t, i, take, top):
+        scores += add_ref[n, p, side * half : side * half + take]
+        score_ref[i % 3, side * take : (side + 1) * take] = scores
+        return jnp.max(scores.reshape(take // 16, 16, 2 * LANES), axis=0)
+
+    def highest(parts):
+        return jnp.max(jnp.maximum(*parts), axis=0, keepdims=True)
+
+    def combine(t, i, side, take, top):
+        _, p = units[i]
+        weights = jnp.exp2(score_ref[i % 3, side * take : (side + 1) * take] - top).astype(BF)
+        return jnp.dot(val_refs[side][t, p, :, :take], weights, preferred_element_type=F32)
+
+    def divide(i, got):
         n, p = units[i]
-        weights = jnp.exp2(score_ref[i % 3, : 2 * take] - top).astype(BF)
-        got = jnp.dot(val0_ref[t, p, :, :take], weights[:take], preferred_element_type=F32)
-        got += jnp.dot(val1_ref[t, p, :, :take], weights[take:], preferred_element_type=F32)
         for k in range(2):
             to = slice(k * LANES, (k + 1) * LANES)
             h = 2 * p + k
@@ -293,13 +298,13 @@
         after = jnp.minimum(t + 1, columns - 1)
         load_queries(after, 1 - slot)
         for i in range(len(units)):
-            ahead = i + 2
-            if ahead < len(units):
-                later = score(t, slot, ahead, take)
-            else:
-                later = score(after, 1 - slot, ahead - len(units), take)
-            combine(t, i, take, tops[0])
-            tops = (tops[1], later)
+            ahead = (t, slot, i + 2) if i + 2 < len(units) else (after, 1 - slot, i + 2 - len(units))
+            parts, got = [], []
+            for side in range(2):
+                parts.append(score(*ahead, side, take))
+                got.append(combine(t, i, side, take, tops[0]))
+            divide(i, got[0] + got[1])
+            tops = (tops[1], highest(parts))
         finish(t)
         return tops
 
@@ -307,7 +312,7 @@
     load_queries(0, 0)
 
     def valid_columns(take):
-        tops = (score(0, 0, 0, take), score(0, 0, 1, take))
+        tops = tuple(highest([score(0, 0, i, side, take) for side in range(2)]) for i in range(2))
         lax.fori_loop(0, real, functools.partial(column, take), tops)
 
     need = (count + 2 * rows - 1) // (2 * rows) * rows

time: 105 us -> 106 us (level); the launches traced: 106 us -> 106 us
  no operation moved by 1% of the time
where the time goes in v6:
time: 106 us
  Pallas kernels  28.6 us (27%)
  waiting for transfers between devices  26.9 us (25%)
  starting transfers between devices  23.9 us (23%)
  blocking collectives  21.8 us (21%)
  local copies, waits for them, and re-layouts  4.52 us (4%)
    all_to_all x1, blocking collectives, on_device(): lax.all_to_all(a, CHIPS, split_axis=0, concat_axis=0, tiled=True)  21.8 us
    pallas_call x1, Pallas kernels, attend_call(): pl.pallas_call(attend_kernel, out_shape=in_vmem((sources, rows * columns,...  19.1 us
    ppermute x6, waiting for transfers between devices, ring(): return [block] + [lax.ppermute(block, PLACES, turn) for turn in turns]  14.9 us
    all_to_all x1, starting transfers between devices, on_device(): lax.all_to_all(a, CHIPS, split_axis=0, concat_axis=0, tiled=True)  11.6 us
    ppermute x3, waiting for transfers between devices, on_device(): lax.ppermute(mixed, 'z', [(i, (i + n) % RING) for i in range(RING)])  10.8 us
    ppermute x6, starting transfers between devices, ring(): return [block] + [lax.ppermute(block, PLACES, turn) for turn in turns]  6.48 us
    ppermute x3, starting transfers between devices, on_device(): lax.ppermute(mixed, 'z', [(i, (i + n) % RING) for i in range(RING)])  4.57 us
    pallas_call x1, Pallas kernels, columns_call(): pl.pallas_call(columns_kernel, out_shape=in_vmem((columns, half, channels...  3.46 us
  transfers between devices with their start and end apart: 12, of which 7 were waited for; matrix products, arithmetic and copies ran while one was open for 0% of the time, Pallas kernels for 9%

profile of v6, /device:TPU:0, one launch (start us, length us, event | category | flops | bytes accessed | tf_op | source)
XLA Modules:
  0.0 106.0 jit_solution(13559946290031480549)
XLA Ops:
  0.0 3.0 %copy.16 = bf16[72,64,128]{2,0,1:T(8,128)(2,1)} copy(bf16[72,64,128]{2,1,0:T(8,128)(2,1)} %bitcast.20) | data formatting | bytes 2359296 | tf_op jit(solution)/shard_map/reshape | solution.py:394
  3.1 11.6 %all-to-all-start = ((bf16[64,72,128]{2,1,0:T(8,128)(2,1)}), bf16[64,72,128]{2,1,0:T(8,128)(2,1)S(1)}, u32[]{:S(2)}, u32[]{:S(2)}) async-start(bf16[64,72,128]{2,1,0:T(8,128)(2,1)} %bitcast.19), calls=%async_computation | async-start | bytes 2359296 | tf_op jit(solution)/shard_map/all_to_all | solution.py:392
  14.7 2.4 %bias_rows.1 = (bf16[3,48,128]{2,1,0:T(8,128)(2,1)S(1)}, bf16[3,48,128]{2,1,0:T(8,128)(2,1)S(1)}) custom-call(bf16[6,768,128]{2,1,0:T(8,128)(2,1)S(1)} %copy-done, f32[1,128]{1,0:T(1,128)S(1)} %bitcast.22, f32[1,128]{1,0:T(1,128)S(1)} %bitcast.24, bf16[4,128]{1,0:T(4,128)(2,1)S(1)} %bitcast.26), custom_call_target="tpu_custom_call" | custom-call | tf_op jit(solution)/shard_map/bias_rows/pallas_call | solution.py:78
  17.3 1.2 %collective-permute-done = bf16[3,48,128]{2,1,0:T(8,128)(2,1)S(1)} collective-permute-done((bf16[3,48,128]{2,1,0:T(8,128)(2,1)S(1)}, bf16[3,48,128]{2,1,0:T(8,128)(2,1)S(1)}, u32[]{:S(2)}, u32[]{:S(2)}) %collective-permute-start) | collective-permute-done | bytes 36896 | tf_op jit(solution)/shard_map/ppermute | solution.py:396
  18.5 2.9 %collective-permute-start.3 = (bf16[3,48,128]{2,1,0:T(8,128)(2,1)S(1)}, bf16[3,48,128]{2,1,0:T(8,128)(2,1)S(1)}, u32[]{:S(2)}, u32[]{:S(2)}) collective-permute-start(bf16[3,48,128]{2,1,0:T(8,128)(2,1)S(1)} %get-tuple-element.24), channel_id=1, source_target_pairs={{0,48},{16,0},{32,16},{48,32},{1,49},{17,1},{33,17},{49,33},{2,50}... | collective-permute-start | bytes 110600 | tf_op jit(solution)/shard_map/ppermute | solution.py:397
  21.4 0.8 collective-permute-start.2
  22.2 0.9 collective-permute-start.1
  23.1 5.2 %collective-permute-done.3 = bf16[3,48,128]{2,1,0:T(8,128)(2,1)S(1)} collective-permute-done((bf16[3,48,128]{2,1,0:T(8,128)(2,1)S(1)}, bf16[3,48,128]{2,1,0:T(8,128)(2,1)S(1)}, u32[]{:S(2)}, u32[]{:S(2)}) %collective-permute-start.3) | collective-permute-done | bytes 36896 | tf_op jit(solution)/shard_map/ppermute | solution.py:397
  28.3 5.1 %collective-permute-done.2 = bf16[3,48,128]{2,1,0:T(8,128)(2,1)S(1)} collective-permute-done((bf16[3,48,128]{2,1,0:T(8,128)(2,1)S(1)}, bf16[3,48,128]{2,1,0:T(8,128)(2,1)S(1)}, u32[]{:S(2)}, u32[]{:S(2)}) %collective-permute-start.2) | collective-permute-done | bytes 36896 | tf_op jit(solution)/shard_map/ppermute | solution.py:397
  33.4 0.4 collective-permute-done.1
  33.9 1.0 collective-permute-start.6
  34.9 1.2 %collective-permute-start.5 = (bf16[4,3,48,128]{3,2,1,0:T(8,128)(2,1)S(1)}, bf16[4,3,48,128]{3,2,1,0:T(8,128)(2,1)S(1)}, u32[]{:S(2)}, u32[]{:S(2)}) collective-permute-start(bf16[4,3,48,128]{3,2,1,0:T(8,128)(2,1)S(1)} %pad_maximum_fusion), channel_id=1, source_target_pairs={{0,2},{1,9},{2,0},{3,11},{4,6},{5,13},{6,4},{7,15},{8,10},{9,1},{1... | collective-permute-start | bytes 442376 | tf_op jit(solution)/shard_map/ppermute | solution.py:381
  36.2 3.5 %columns.1.cols_ref = bf16[12,384,128]{2,1,0:T(8,128)(2,1)S(1)} custom-call(bf16[64,72,128]{2,1,0:T(8,128)(2,1)S(1)} %all-to-all-done.got_ref, f32[1,128]{1,0:T(1,128)S(1)} %bitcast.23, f32[1,128]{1,0:T(1,128)S(1)} %bitcast.25), custom_call_target="tpu_custom_call" | custom-call | tf_op jit(solution)/shard_map/columns/pallas_call | solution.py:117
  39.6 1.2 %collective-permute-start.10 = (bf16[12,384,128]{2,1,0:T(8,128)(2,1)S(1)}, bf16[12,384,128]{2,1,0:T(8,128)(2,1)S(1)}, u32[]{:S(2)}, u32[]{:S(2)}) collective-permute-start(bf16[12,384,128]{2,1,0:T(8,128)(2,1)S(1)} %columns.1.cols_ref), channel_id=1, source_target_pairs={{0,1},{1,0},{2,3},{3,2},{4,5},{5,4},{6,7},{7,6},{8,9},{9,8},{10,11... | collective-permute-start | bytes 3538952 | tf_op jit(solution)/shard_map/ppermute | solution.py:402
  40.8 2.3 %collective-permute-done.4 = bf16[4,3,48,128]{3,2,1,0:T(8,128)(2,1)S(1)} collective-permute-done((bf16[4,3,48,128]{3,2,1,0:T(8,128)(2,1)S(1)}, bf16[4,3,48,128]{3,2,1,0:T(8,128)(2,1)S(1)}, u32[]{:S(2)}, u32[]{:S(2)}) %collective-permute-start.4) | collective-permute-done | bytes 147488 | tf_op jit(solution)/shard_map/ppermute | solution.py:381
  43.2 2.8 %collective-permute-start.9 = (bf16[16,3,48,128]{3,2,1,0:T(8,128)(2,1)S(1)}, bf16[16,3,48,128]{3,2,1,0:T(8,128)(2,1)S(1)}, u32[]{:S(2)}, u32[]{:S(2)}) collective-permute-start(bf16[16,3,48,128]{3,2,1,0:T(8,128)(2,1)S(1)} %constant_dynamic-update-slice_fusion.refs_0_), channel_id=1, source_target_pairs={{0,12},{1,67},{2,14},{3,65},{4,0},{5,71},{6,2},{7,69},{8,4},{9,75}... | collective-permute-start | bytes 1769480 | tf_op jit(solution)/shard_map/ppermute | solution.py:381
  46.0 1.2 %collective-permute-start.8 = (bf16[16,3,48,128]{3,2,1,0:T(8,128)(2,1)S(1)}, bf16[16,3,48,128]{3,2,1,0:T(8,128)(2,1)S(1)}, u32[]{:S(2)}, u32[]{:S(2)}) collective-permute-start(bf16[16,3,48,128]{3,2,1,0:T(8,128)(2,1)S(1)} %constant_dynamic-update-slice_fusion.refs_0_), channel_id=1, source_target_pairs={{0,8},{1,3},{2,10},{3,1},{4,12},{5,7},{6,14},{7,5},{8,0},{9,11},{1... | collective-permute-start | bytes 1769480 | tf_op jit(solution)/shard_map/ppermute | solution.py:381
  47.6 2.3 %own.1 = (bf16[12,128,384]{2,1,0:T(8,128)(2,1)S(1)}, bf16[12,128,384]{2,1,0:T(8,128)(2,1)S(1)}, bf16[12,384,128]{2,1,0:T(8,128)(2,1)S(1)}, bf16[12,2,80,384]{3,2,1,0:T(8,128)(2,1)S(1)}, bf16[12,128,384]{2,1,0:T(8,128)(2,1)S(1)}) custom-call(bf16[12,384,128]{2,1,0:T(8,128)(2,1)S(1)} %columns.1.cols_ref, bf16[128,128]{1,0:T(8,128)(2,1)S(1)} %copy-done.4, ...), custom_call_target="tpu_custom_call" | custom-call | tf_op jit(solution)/shard_map/own/pallas_call | solution.py:173
  49.9 1.3 %other.1 = (bf16[12,384,128]{2,1,0:T(8,128)(2,1)S(1)}, bf16[12,2,80,384]{3,2,1,0:T(8,128)(2,1)S(1)}) custom-call(bf16[12,384,128]{2,1,0:T(8,128)(2,1)S(1)} %collective-permute-done.10.cols_ref, bf16[128,128]{1,0:T(8,128)(2,1)S(1)} %copy-done.1, bf16[128,128]{1,0:T(8,128)(2,1)S(1)} %copy-done.2), custom_call_target="tpu_custom_call" | custom-call | tf_op jit(solution)/shard_map/other/pallas_call | solution.py:196
  51.2 8.6 %collective-permute-done.9.refs_3_ = bf16[16,3,48,128]{3,2,1,0:T(8,128)(2,1)S(1)} collective-permute-done((bf16[16,3,48,128]{3,2,1,0:T(8,128)(2,1)S(1)}, bf16[16,3,48,128]{3,2,1,0:T(8,128)(2,1)S(1)}, u32[]{:S(2)}, u32[]{:S(2)}) %collective-permute-start.9) | collective-permute-done | bytes 589856 | tf_op jit(solution)/shard_map/ppermute | solution.py:381
  59.8 3.9 %collective-permute-done.7.refs_1_ = bf16[16,3,48,128]{3,2,1,0:T(8,128)(2,1)S(1)} collective-permute-done((bf16[16,3,48,128]{3,2,1,0:T(8,128)(2,1)S(1)}, bf16[16,3,48,128]{3,2,1,0:T(8,128)(2,1)S(1)}, u32[]{:S(2)}, u32[]{:S(2)}) %collective-permute-start.7) | collective-permute-done | bytes 589856 | tf_op jit(solution)/shard_map/ppermute | solution.py:381
  63.8 19.1 %attend.1 = bf16[64,72,128]{2,1,0:T(8,128)(2,1)S(1)} custom-call(s32[6,128]{1,0:T(8,128)S(1)} %bitcast.21, bf16[16,3,48,128]{3,2,1,0:T(8,128)(2,1)S(1)} %constant_dynamic-update-slice_fusion.refs_0_, bf16[16,3,48,128]{3,2,1,0:T(8,128)(2,1)S(1)} %collective-permute-done.7.refs_1_, bf16[16,3,48,128]{3,2,1,0:T(8,128)(2,1)S(1)} %collective-permute-done.8.refs_2_, ...), custom_call_target="tpu_custom_call" | custom-call | tf_op jit(solution)/shard_map/attend/pallas_call | solution.py:349
  82.9 21.8 %all_to_all.10 = bf16[64,72,128]{2,1,0:T(8,128)(2,1)S(1)} all-to-all(bf16[64,72,128]{2,1,0:T(8,128)(2,1)S(1)} %attend.1), channel_id=1, replica_groups=mesh['ylo'=2,'z'=4,'x'=4,'yhi'=2,'core'=2] {'ylo','z','x','yhi'}, dimensions={0} | all-to-all | bytes 2359296 | tf_op jit(solution)/shard_map/all_to_all | solution.py:392
  104.7 1.3 %copy.14 = bf16[72,64,128]{2,1,0:T(8,128)(2,1)} copy(bf16[72,64,128]{2,0,1:T(8,128)(2,1)S(1)} %bitcast.29) | data formatting | bytes 2359296 | tf_op jit(solution)/shard_map/transpose | solution.py:407
  (40 shorter events, 0.6 us)
Async XLA Ops:
  3.0 11.7 %copy-start = (bf16[6,768,128]{2,1,0:T(8,128)(2,1)S(1)}, bf16[6,768,128]{2,1,0:T(8,128)(2,1)}, u32[]{:S(2)}) copy-start(bf16[6,768,128]{2,1,0:T(8,128)(2,1)} %pair_ref.1) | copy-start | bytes 3538948
  3.0 11.7 %copy-start.7 = (f32[128]{0:T(128)S(1)}, f32[128]{0:T(128)}, u32[]{:S(2)}) copy-start(f32[128]{0:T(128)} %param.14) | copy-start | bytes 1540
  3.1 11.7 %copy-start.8 = (f32[128]{0:T(128)S(1)}, f32[128]{0:T(128)}, u32[]{:S(2)}) copy-start(f32[128]{0:T(128)} %param.15) | copy-start | bytes 1540
  3.1 11.7 %copy-start.9 = (bf16[128,4]{0,1:T(4,128)(2,1)S(1)}, bf16[128,4]{0,1:T(4,128)(2,1)}, u32[]{:S(2)}) copy-start(bf16[128,4]{0,1:T(4,128)(2,1)} %param.21) | copy-start | bytes 3076
  3.1 33.1 %all-to-all-start = ((bf16[64,72,128]{2,1,0:T(8,128)(2,1)}), bf16[64,72,128]{2,1,0:T(8,128)(2,1)S(1)}, u32[]{:S(2)}, u32[]{:S(2)}) async-start(bf16[64,72,128]{2,1,0:T(8,128)(2,1)} %bitcast.19), calls=%async_computation | async-start | bytes 2359296 | tf_op jit(solution)/shard_map/all_to_all | solution.py:392
  17.2 1.3 %collective-permute-start = (bf16[3,48,128]{2,1,0:T(8,128)(2,1)S(1)}, bf16[3,48,128]{2,1,0:T(8,128)(2,1)S(1)}, u32[]{:S(2)}, u32[]{:S(2)}) collective-permute-start(bf16[3,48,128]{2,1,0:T(8,128)(2,1)S(1)} %get-tuple-element.15), channel_id=1, source_target_pairs={{0,1},{1,0},{2,3},{3,2},{4,5},{5,4},{6,7},{7,6},{8,9},{9,8},{10,11... | collective-permute-start | bytes 110600 | tf_op jit(solution)/shard_map/ppermute | solution.py:396
  18.5 9.8 %collective-permute-start.3 = (bf16[3,48,128]{2,1,0:T(8,128)(2,1)S(1)}, bf16[3,48,128]{2,1,0:T(8,128)(2,1)S(1)}, u32[]{:S(2)}, u32[]{:S(2)}) collective-permute-start(bf16[3,48,128]{2,1,0:T(8,128)(2,1)S(1)} %get-tuple-element.24), channel_id=1, source_target_pairs={{0,48},{16,0},{32,16},{48,32},{1,49},{17,1},{33,17},{49,33},{2,50}... | collective-permute-start | bytes 110600 | tf_op jit(solution)/shard_map/ppermute | solution.py:397
  21.4 12.1 %collective-permute-start.2 = (bf16[3,48,128]{2,1,0:T(8,128)(2,1)S(1)}, bf16[3,48,128]{2,1,0:T(8,128)(2,1)S(1)}, u32[]{:S(2)}, u32[]{:S(2)}) collective-permute-start(bf16[3,48,128]{2,1,0:T(8,128)(2,1)S(1)} %get-tuple-element.24), channel_id=1, source_target_pairs={{0,32},{16,48},{32,0},{48,16},{1,33},{17,49},{33,1},{49,17},{2,34}... | collective-permute-start | bytes 110600 | tf_op jit(solution)/shard_map/ppermute | solution.py:397
  22.2 11.6 %collective-permute-start.1 = (bf16[3,48,128]{2,1,0:T(8,128)(2,1)S(1)}, bf16[3,48,128]{2,1,0:T(8,128)(2,1)S(1)}, u32[]{:S(2)}, u32[]{:S(2)}) collective-permute-start(bf16[3,48,128]{2,1,0:T(8,128)(2,1)S(1)} %get-tuple-element.24), channel_id=1, source_target_pairs={{0,16},{16,32},{32,48},{48,0},{1,17},{17,33},{33,49},{49,1},{2,18}... | collective-permute-start | bytes 110600 | tf_op jit(solution)/shard_map/ppermute | solution.py:397
  33.9 9.3 %collective-permute-start.6 = (bf16[4,3,48,128]{3,2,1,0:T(8,128)(2,1)S(1)}, bf16[4,3,48,128]{3,2,1,0:T(8,128)(2,1)S(1)}, u32[]{:S(2)}, u32[]{:S(2)}) collective-permute-start(bf16[4,3,48,128]{3,2,1,0:T(8,128)(2,1)S(1)} %pad_maximum_fusion), channel_id=1, source_target_pairs={{0,66},{1,13},{2,64},{3,15},{4,70},{5,1},{6,68},{7,3},{8,74},{9,5}... | collective-permute-start | bytes 442376 | tf_op jit(solution)/shard_map/ppermute | solution.py:381
  34.9 8.3 %collective-permute-start.5 = (bf16[4,3,48,128]{3,2,1,0:T(8,128)(2,1)S(1)}, bf16[4,3,48,128]{3,2,1,0:T(8,128)(2,1)S(1)}, u32[]{:S(2)}, u32[]{:S(2)}) collective-permute-start(bf16[4,3,48,128]{3,2,1,0:T(8,128)(2,1)S(1)} %pad_maximum_fusion), channel_id=1, source_target_pairs={{0,2},{1,9},{2,0},{3,11},{4,6},{5,13},{6,4},{7,15},{8,10},{9,1},{1... | collective-permute-start | bytes 442376 | tf_op jit(solution)/shard_map/ppermute | solution.py:381
  36.1 7.1 %collective-permute-start.4 = (bf16[4,3,48,128]{3,2,1,0:T(8,128)(2,1)S(1)}, bf16[4,3,48,128]{3,2,1,0:T(8,128)(2,1)S(1)}, u32[]{:S(2)}, u32[]{:S(2)}) collective-permute-start(bf16[4,3,48,128]{3,2,1,0:T(8,128)(2,1)S(1)} %pad_maximum_fusion), channel_id=1, source_target_pairs={{0,64},{1,5},{2,66},{3,7},{4,68},{5,9},{6,70},{7,11},{8,72},{9,13}... | collective-permute-start | bytes 442376 | tf_op jit(solution)/shard_map/ppermute | solution.py:381
  36.1 11.4 %copy-start.1 = (bf16[128,128]{1,0:T(8,128)(2,1)S(1)}, bf16[128,128]{1,0:T(8,128)(2,1)}, u32[]{:S(2)}) copy-start(bf16[128,128]{1,0:T(8,128)(2,1)} %wk_ref.3) | copy-start | bytes 98308
  36.1 11.4 %copy-start.2 = (bf16[128,128]{1,0:T(8,128)(2,1)S(1)}, bf16[128,128]{1,0:T(8,128)(2,1)}, u32[]{:S(2)}) copy-start(bf16[128,128]{1,0:T(8,128)(2,1)} %wv_ref.3) | copy-start | bytes 98308
  36.1 11.4 %copy-start.4 = (bf16[128,128]{1,0:T(8,128)(2,1)S(1)}, bf16[128,128]{1,0:T(8,128)(2,1)}, u32[]{:S(2)}) copy-start(bf16[128,128]{1,0:T(8,128)(2,1)} %wq_ref.1) | copy-start | bytes 98308
  36.1 11.4 %copy-start.5 = (bf16[128,128]{1,0:T(8,128)(2,1)S(1)}, bf16[128,128]{1,0:T(8,128)(2,1)}, u32[]{:S(2)}) copy-start(bf16[128,128]{1,0:T(8,128)(2,1)} %wg_ref.1) | copy-start | bytes 98308
  36.1 11.4 %copy-start.10 = (f32[128]{0:T(128)S(1)}, f32[128]{0:T(128)}, u32[]{:S(2)}) copy-start(f32[128]{0:T(128)} %param.20) | copy-start | bytes 1540
  39.6 10.3 %collective-permute-start.10 = (bf16[12,384,128]{2,1,0:T(8,128)(2,1)S(1)}, bf16[12,384,128]{2,1,0:T(8,128)(2,1)S(1)}, u32[]{:S(2)}, u32[]{:S(2)}) collective-permute-start(bf16[12,384,128]{2,1,0:T(8,128)(2,1)S(1)} %columns.1.cols_ref), channel_id=1, source_target_pairs={{0,1},{1,0},{2,3},{3,2},{4,5},{5,4},{6,7},{7,6},{8,9},{9,8},{10,11... | collective-permute-start | bytes 3538952 | tf_op jit(solution)/shard_map/ppermute | solution.py:402
  43.2 16.6 %collective-permute-start.9 = (bf16[16,3,48,128]{3,2,1,0:T(8,128)(2,1)S(1)}, bf16[16,3,48,128]{3,2,1,0:T(8,128)(2,1)S(1)}, u32[]{:S(2)}, u32[]{:S(2)}) collective-permute-start(bf16[16,3,48,128]{3,2,1,0:T(8,128)(2,1)S(1)} %constant_dynamic-update-slice_fusion.refs_0_), channel_id=1, source_target_pairs={{0,12},{1,67},{2,14},{3,65},{4,0},{5,71},{6,2},{7,69},{8,4},{9,75}... | collective-permute-start | bytes 1769480 | tf_op jit(solution)/shard_map/ppermute | solution.py:381
  46.0 13.8 %collective-permute-start.8 = (bf16[16,3,48,128]{3,2,1,0:T(8,128)(2,1)S(1)}, bf16[16,3,48,128]{3,2,1,0:T(8,128)(2,1)S(1)}, u32[]{:S(2)}, u32[]{:S(2)}) collective-permute-start(bf16[16,3,48,128]{3,2,1,0:T(8,128)(2,1)S(1)} %constant_dynamic-update-slice_fusion.refs_0_), channel_id=1, source_target_pairs={{0,8},{1,3},{2,10},{3,1},{4,12},{5,7},{6,14},{7,5},{8,0},{9,11},{1... | collective-permute-start | bytes 1769480 | tf_op jit(solution)/shard_map/ppermute | solution.py:381
  47.2 16.5 %collective-permute-start.7 = (bf16[16,3,48,128]{3,2,1,0:T(8,128)(2,1)S(1)}, bf16[16,3,48,128]{3,2,1,0:T(8,128)(2,1)S(1)}, u32[]{:S(2)}, u32[]{:S(2)}) collective-permute-start(bf16[16,3,48,128]{3,2,1,0:T(8,128)(2,1)S(1)} %constant_dynamic-update-slice_fusion.refs_0_), channel_id=1, source_target_pairs={{0,4},{1,65},{2,6},{3,67},{4,8},{5,69},{6,10},{7,71},{8,12},{9,73}... | collective-permute-start | bytes 1769480 | tf_op jit(solution)/shard_map/ppermute | solution.py:381
  47.5 16.2 %copy-start.3 = (bf16[128,128]{1,0:T(8,128)(2,1)S(1)}, bf16[128,128]{1,0:T(8,128)(2,1)}, u32[]{:S(2)}) copy-start(bf16[128,128]{1,0:T(8,128)(2,1)} %refs_11_.1) | copy-start | bytes 98308
  47.5 16.2 %copy-start.6 = (s32[768]{0:T(1024)S(1)}, s32[768]{0:T(1024)}, u32[]{:S(2)}) copy-start(s32[768]{0:T(1024)} %param.13) | copy-start | bytes 9220
  47.6 16.2 %copy-start.11 = (f32[128]{0:T(128)S(1)}, f32[128]{0:T(128)}, u32[]{:S(2)}) copy-start(f32[128]{0:T(128)} %param.23) | copy-start | bytes 1540

commit v7 on v6

--- a/solution.py
+++ b/solution.py
@@ -249,6 +249,7 @@
                     jnp.where(valid, got, -1e9)
                 )
     q_ref[...] = jnp.zeros_like(q_ref)
+    att_ref[...] = jnp.zeros_like(att_ref)
     units = [(n, p) for n in range(parts) for p in range(pairs)]
 
     def load_queries(t, slot):
@@ -285,7 +286,7 @@
             to = slice(k * LANES, (k + 1) * LANES)
             h = 2 * p + k
             att_ref[h * DIM : (h + 1) * DIM, n * LANES : (n + 1) * LANES] = (
-                got[k * DIM : (k + 1) * DIM, to] / got[2 * DIM : 2 * DIM + 1, to]
+                got[k * DIM : (k + 1) * DIM, to] * (1.0 / got[2 * DIM : 2 * DIM + 1, to])
             )
 
     def finish(t):
@@ -296,6 +297,7 @@
     def column(take, t, tops):
         slot = t & 1
         after = jnp.minimum(t + 1, columns - 1)
+        finish(jnp.maximum(t - 1, 0))
         load_queries(after, 1 - slot)
         for i in range(len(units)):
             ahead = (t, slot, i + 2) if i + 2 < len(units) else (after, 1 - slot, i + 2 - len(units))
@@ -305,7 +307,6 @@
                 got.append(combine(t, i, side, take, tops[0]))
             divide(i, got[0] + got[1])
             tops = (tops[1], highest(parts))
-        finish(t)
         return tops
 
     real = (count - chip + sources - 1) // sources
@@ -314,6 +315,7 @@
     def valid_columns(take):
         tops = tuple(highest([score(0, 0, i, side, take) for side in range(2)]) for i in range(2))
         lax.fori_loop(0, real, functools.partial(column, take), tops)
+        finish(jnp.maximum(real - 1, 0))
 
     need = (count + 2 * rows - 1) // (2 * rows) * rows
     below = -1

time: 106 us -> 102 us (0.962)
  Pallas kernels: 28.6 us -> 24.2 us
    pallas_call x1, Pallas kernels: 19.1 us -> 14.7 us  [attend_call(): pl.pallas_call(attend_kernel, out_shape=in_vmem((sources, rows * columns,...]
where the time goes in v7:
time: 102 us
  waiting for transfers between devices  26.9 us (26%)
  Pallas kernels  24.2 us (24%)
  starting transfers between devices  23.9 us (23%)
  blocking collectives  22.1 us (22%)
  local copies, waits for them, and re-layouts  4.52 us (4%)
    all_to_all x1, blocking collectives, on_device(): lax.all_to_all(a, CHIPS, split_axis=0, concat_axis=0, tiled=True)  22.1 us
    ppermute x6, waiting for transfers between devices, ring(): return [block] + [lax.ppermute(block, PLACES, turn) for turn in turns]  14.9 us
    pallas_call x1, Pallas kernels, attend_call(): pl.pallas_call(attend_kernel, out_shape=in_vmem((sources, rows * columns,...  14.7 us
    all_to_all x1, starting transfers between devices, on_device(): lax.all_to_all(a, CHIPS, split_axis=0, concat_axis=0, tiled=True)  11.6 us
    ppermute x3, waiting for transfers between devices, on_device(): lax.ppermute(mixed, 'z', [(i, (i + n) % RING) for i in range(RING)])  10.8 us
    ppermute x6, starting transfers between devices, ring(): return [block] + [lax.ppermute(block, PLACES, turn) for turn in turns]  6.48 us
    ppermute x3, starting transfers between devices, on_device(): lax.ppermute(mixed, 'z', [(i, (i + n) % RING) for i in range(RING)])  4.57 us
    pallas_call x1, Pallas kernels, columns_call(): pl.pallas_call(columns_kernel, out_shape=in_vmem((columns, half, channels...  3.46 us
  transfers between devices with their start and end apart: 12, of which 7 were waited for; matrix products, arithmetic and copies ran while one was open for 0% of the time, Pallas kernels for 9%

profile of v7, /device:TPU:0, one launch (start us, length us, event | category | flops | bytes accessed | tf_op | source)
XLA Modules:
  0.0 101.9 jit_solution(10480515142590141989)
XLA Ops:
  0.0 3.0 %copy.16 = bf16[72,64,128]{2,0,1:T(8,128)(2,1)} copy(bf16[72,64,128]{2,1,0:T(8,128)(2,1)} %bitcast.20) | data formatting | bytes 2359296 | tf_op jit(solution)/shard_map/reshape | solution.py:396
  3.1 11.6 %all-to-all-start = ((bf16[64,72,128]{2,1,0:T(8,128)(2,1)}), bf16[64,72,128]{2,1,0:T(8,128)(2,1)S(1)}, u32[]{:S(2)}, u32[]{:S(2)}) async-start(bf16[64,72,128]{2,1,0:T(8,128)(2,1)} %bitcast.19), calls=%async_computation | async-start | bytes 2359296 | tf_op jit(solution)/shard_map/all_to_all | solution.py:394
  14.7 2.4 %bias_rows.1 = (bf16[3,48,128]{2,1,0:T(8,128)(2,1)S(1)}, bf16[3,48,128]{2,1,0:T(8,128)(2,1)S(1)}) custom-call(bf16[6,768,128]{2,1,0:T(8,128)(2,1)S(1)} %copy-done, f32[1,128]{1,0:T(1,128)S(1)} %bitcast.22, f32[1,128]{1,0:T(1,128)S(1)} %bitcast.24, bf16[4,128]{1,0:T(4,128)(2,1)S(1)} %bitcast.26), custom_call_target="tpu_custom_call" | custom-call | tf_op jit(solution)/shard_map/bias_rows/pallas_call | solution.py:78
  17.3 1.2 %collective-permute-done = bf16[3,48,128]{2,1,0:T(8,128)(2,1)S(1)} collective-permute-done((bf16[3,48,128]{2,1,0:T(8,128)(2,1)S(1)}, bf16[3,48,128]{2,1,0:T(8,128)(2,1)S(1)}, u32[]{:S(2)}, u32[]{:S(2)}) %collective-permute-start) | collective-permute-done | bytes 36896 | tf_op jit(solution)/shard_map/ppermute | solution.py:398
  18.5 2.9 %collective-permute-start.3 = (bf16[3,48,128]{2,1,0:T(8,128)(2,1)S(1)}, bf16[3,48,128]{2,1,0:T(8,128)(2,1)S(1)}, u32[]{:S(2)}, u32[]{:S(2)}) collective-permute-start(bf16[3,48,128]{2,1,0:T(8,128)(2,1)S(1)} %get-tuple-element.24), channel_id=1, source_target_pairs={{0,48},{16,0},{32,16},{48,32},{1,49},{17,1},{33,17},{49,33},{2,50}... | collective-permute-start | bytes 110600 | tf_op jit(solution)/shard_map/ppermute | solution.py:399
  21.4 0.8 collective-permute-start.2
  22.2 0.9 collective-permute-start.1
  23.1 5.2 %collective-permute-done.3 = bf16[3,48,128]{2,1,0:T(8,128)(2,1)S(1)} collective-permute-done((bf16[3,48,128]{2,1,0:T(8,128)(2,1)S(1)}, bf16[3,48,128]{2,1,0:T(8,128)(2,1)S(1)}, u32[]{:S(2)}, u32[]{:S(2)}) %collective-permute-start.3) | collective-permute-done | bytes 36896 | tf_op jit(solution)/shard_map/ppermute | solution.py:399
  28.3 5.1 %collective-permute-done.2 = bf16[3,48,128]{2,1,0:T(8,128)(2,1)S(1)} collective-permute-done((bf16[3,48,128]{2,1,0:T(8,128)(2,1)S(1)}, bf16[3,48,128]{2,1,0:T(8,128)(2,1)S(1)}, u32[]{:S(2)}, u32[]{:S(2)}) %collective-permute-start.2) | collective-permute-done | bytes 36896 | tf_op jit(solution)/shard_map/ppermute | solution.py:399
  33.4 0.4 collective-permute-done.1
  33.9 1.0 %collective-permute-start.6 = (bf16[4,3,48,128]{3,2,1,0:T(8,128)(2,1)S(1)}, bf16[4,3,48,128]{3,2,1,0:T(8,128)(2,1)S(1)}, u32[]{:S(2)}, u32[]{:S(2)}) collective-permute-start(bf16[4,3,48,128]{3,2,1,0:T(8,128)(2,1)S(1)} %pad_maximum_fusion), channel_id=1, source_target_pairs={{0,66},{1,13},{2,64},{3,15},{4,70},{5,1},{6,68},{7,3},{8,74},{9,5}... | collective-permute-start | bytes 442376 | tf_op jit(solution)/shard_map/ppermute | solution.py:383
  34.9 1.2 %collective-permute-start.5 = (bf16[4,3,48,128]{3,2,1,0:T(8,128)(2,1)S(1)}, bf16[4,3,48,128]{3,2,1,0:T(8,128)(2,1)S(1)}, u32[]{:S(2)}, u32[]{:S(2)}) collective-permute-start(bf16[4,3,48,128]{3,2,1,0:T(8,128)(2,1)S(1)} %pad_maximum_fusion), channel_id=1, source_target_pairs={{0,2},{1,9},{2,0},{3,11},{4,6},{5,13},{6,4},{7,15},{8,10},{9,1},{1... | collective-permute-start | bytes 442376 | tf_op jit(solution)/shard_map/ppermute | solution.py:383
  36.2 3.5 %columns.1.cols_ref = bf16[12,384,128]{2,1,0:T(8,128)(2,1)S(1)} custom-call(bf16[64,72,128]{2,1,0:T(8,128)(2,1)S(1)} %all-to-all-done.got_ref, f32[1,128]{1,0:T(1,128)S(1)} %bitcast.23, f32[1,128]{1,0:T(1,128)S(1)} %bitcast.25), custom_call_target="tpu_custom_call" | custom-call | tf_op jit(solution)/shard_map/columns/pallas_call | solution.py:117
  39.6 1.2 %collective-permute-start.10 = (bf16[12,384,128]{2,1,0:T(8,128)(2,1)S(1)}, bf16[12,384,128]{2,1,0:T(8,128)(2,1)S(1)}, u32[]{:S(2)}, u32[]{:S(2)}) collective-permute-start(bf16[12,384,128]{2,1,0:T(8,128)(2,1)S(1)} %columns.1.cols_ref), channel_id=1, source_target_pairs={{0,1},{1,0},{2,3},{3,2},{4,5},{5,4},{6,7},{7,6},{8,9},{9,8},{10,11... | collective-permute-start | bytes 3538952 | tf_op jit(solution)/shard_map/ppermute | solution.py:404
  40.8 2.3 %collective-permute-done.4 = bf16[4,3,48,128]{3,2,1,0:T(8,128)(2,1)S(1)} collective-permute-done((bf16[4,3,48,128]{3,2,1,0:T(8,128)(2,1)S(1)}, bf16[4,3,48,128]{3,2,1,0:T(8,128)(2,1)S(1)}, u32[]{:S(2)}, u32[]{:S(2)}) %collective-permute-start.4) | collective-permute-done | bytes 147488 | tf_op jit(solution)/shard_map/ppermute | solution.py:383
  43.2 2.8 %collective-permute-start.9 = (bf16[16,3,48,128]{3,2,1,0:T(8,128)(2,1)S(1)}, bf16[16,3,48,128]{3,2,1,0:T(8,128)(2,1)S(1)}, u32[]{:S(2)}, u32[]{:S(2)}) collective-permute-start(bf16[16,3,48,128]{3,2,1,0:T(8,128)(2,1)S(1)} %constant_dynamic-update-slice_fusion.refs_0_), channel_id=1, source_target_pairs={{0,12},{1,67},{2,14},{3,65},{4,0},{5,71},{6,2},{7,69},{8,4},{9,75}... | collective-permute-start | bytes 1769480 | tf_op jit(solution)/shard_map/ppermute | solution.py:383
  46.0 1.2 %collective-permute-start.8 = (bf16[16,3,48,128]{3,2,1,0:T(8,128)(2,1)S(1)}, bf16[16,3,48,128]{3,2,1,0:T(8,128)(2,1)S(1)}, u32[]{:S(2)}, u32[]{:S(2)}) collective-permute-start(bf16[16,3,48,128]{3,2,1,0:T(8,128)(2,1)S(1)} %constant_dynamic-update-slice_fusion.refs_0_), channel_id=1, source_target_pairs={{0,8},{1,3},{2,10},{3,1},{4,12},{5,7},{6,14},{7,5},{8,0},{9,11},{1... | collective-permute-start | bytes 1769480 | tf_op jit(solution)/shard_map/ppermute | solution.py:383
  47.6 2.3 %own.1 = (bf16[12,128,384]{2,1,0:T(8,128)(2,1)S(1)}, bf16[12,128,384]{2,1,0:T(8,128)(2,1)S(1)}, bf16[12,384,128]{2,1,0:T(8,128)(2,1)S(1)}, bf16[12,2,80,384]{3,2,1,0:T(8,128)(2,1)S(1)}, bf16[12,128,384]{2,1,0:T(8,128)(2,1)S(1)}) custom-call(bf16[12,384,128]{2,1,0:T(8,128)(2,1)S(1)} %columns.1.cols_ref, bf16[128,128]{1,0:T(8,128)(2,1)S(1)} %copy-done.4, ...), custom_call_target="tpu_custom_call" | custom-call | tf_op jit(solution)/shard_map/own/pallas_call | solution.py:173
  49.9 1.3 %other.1 = (bf16[12,384,128]{2,1,0:T(8,128)(2,1)S(1)}, bf16[12,2,80,384]{3,2,1,0:T(8,128)(2,1)S(1)}) custom-call(bf16[12,384,128]{2,1,0:T(8,128)(2,1)S(1)} %collective-permute-done.10.cols_ref, bf16[128,128]{1,0:T(8,128)(2,1)S(1)} %copy-done.1, bf16[128,128]{1,0:T(8,128)(2,1)S(1)} %copy-done.2), custom_call_target="tpu_custom_call" | custom-call | tf_op jit(solution)/shard_map/other/pallas_call | solution.py:196
  51.2 8.6 %collective-permute-done.9.refs_3_ = bf16[16,3,48,128]{3,2,1,0:T(8,128)(2,1)S(1)} collective-permute-done((bf16[16,3,48,128]{3,2,1,0:T(8,128)(2,1)S(1)}, bf16[16,3,48,128]{3,2,1,0:T(8,128)(2,1)S(1)}, u32[]{:S(2)}, u32[]{:S(2)}) %collective-permute-start.9) | collective-permute-done | bytes 589856 | tf_op jit(solution)/shard_map/ppermute | solution.py:383
  59.8 3.9 %collective-permute-done.7.refs_1_ = bf16[16,3,48,128]{3,2,1,0:T(8,128)(2,1)S(1)} collective-permute-done((bf16[16,3,48,128]{3,2,1,0:T(8,128)(2,1)S(1)}, bf16[16,3,48,128]{3,2,1,0:T(8,128)(2,1)S(1)}, u32[]{:S(2)}, u32[]{:S(2)}) %collective-permute-start.7) | collective-permute-done | bytes 589856 | tf_op jit(solution)/shard_map/ppermute | solution.py:383
  63.8 14.7 %attend.1 = bf16[64,72,128]{2,1,0:T(8,128)(2,1)S(1)} custom-call(s32[6,128]{1,0:T(8,128)S(1)} %bitcast.21, bf16[16,3,48,128]{3,2,1,0:T(8,128)(2,1)S(1)} %constant_dynamic-update-slice_fusion.refs_0_, bf16[16,3,48,128]{3,2,1,0:T(8,128)(2,1)S(1)} %collective-permute-done.7.refs_1_, bf16[16,3,48,128]{3,2,1,0:T(8,128)(2,1)S(1)} %collective-permute-done.8.refs_2_, ...), custom_call_target="tpu_custom_call" | custom-call | tf_op jit(solution)/shard_map/attend/pallas_call | solution.py:351
  78.5 22.1 %all_to_all.10 = bf16[64,72,128]{2,1,0:T(8,128)(2,1)S(1)} all-to-all(bf16[64,72,128]{2,1,0:T(8,128)(2,1)S(1)} %attend.1), channel_id=1, replica_groups=mesh['ylo'=2,'z'=4,'x'=4,'yhi'=2,'core'=2] {'ylo','z','x','yhi'}, dimensions={0} | all-to-all | bytes 2359296 | tf_op jit(solution)/shard_map/all_to_all | solution.py:394
  100.6 1.3 %copy.14 = bf16[72,64,128]{2,1,0:T(8,128)(2,1)} copy(bf16[72,64,128]{2,0,1:T(8,128)(2,1)S(1)} %bitcast.29) | data formatting | bytes 2359296 | tf_op jit(solution)/shard_map/transpose | solution.py:409
  (40 shorter events, 0.6 us)
Async XLA Ops:
  3.0 11.7 %copy-start = (bf16[6,768,128]{2,1,0:T(8,128)(2,1)S(1)}, bf16[6,768,128]{2,1,0:T(8,128)(2,1)}, u32[]{:S(2)}) copy-start(bf16[6,768,128]{2,1,0:T(8,128)(2,1)} %pair_ref.1) | copy-start | bytes 3538948
  3.0 11.7 %copy-start.7 = (f32[128]{0:T(128)S(1)}, f32[128]{0:T(128)}, u32[]{:S(2)}) copy-start(f32[128]{0:T(128)} %param.14) | copy-start | bytes 1540
  3.1 11.7 %copy-start.8 = (f32[128]{0:T(128)S(1)}, f32[128]{0:T(128)}, u32[]{:S(2)}) copy-start(f32[128]{0:T(128)} %param.15) | copy-start | bytes 1540
  3.1 11.7 %copy-start.9 = (bf16[128,4]{0,1:T(4,128)(2,1)S(1)}, bf16[128,4]{0,1:T(4,128)(2,1)}, u32[]{:S(2)}) copy-start(bf16[128,4]{0,1:T(4,128)(2,1)} %param.21) | copy-start | bytes 3076
  3.1 33.1 %all-to-all-start = ((bf16[64,72,128]{2,1,0:T(8,128)(2,1)}), bf16[64,72,128]{2,1,0:T(8,128)(2,1)S(1)}, u32[]{:S(2)}, u32[]{:S(2)}) async-start(bf16[64,72,128]{2,1,0:T(8,128)(2,1)} %bitcast.19), calls=%async_computation | async-start | bytes 2359296 | tf_op jit(solution)/shard_map/all_to_all | solution.py:394
  17.2 1.3 %collective-permute-start = (bf16[3,48,128]{2,1,0:T(8,128)(2,1)S(1)}, bf16[3,48,128]{2,1,0:T(8,128)(2,1)S(1)}, u32[]{:S(2)}, u32[]{:S(2)}) collective-permute-start(bf16[3,48,128]{2,1,0:T(8,128)(2,1)S(1)} %get-tuple-element.15), channel_id=1, source_target_pairs={{0,1},{1,0},{2,3},{3,2},{4,5},{5,4},{6,7},{7,6},{8,9},{9,8},{10,11... | collective-permute-start | bytes 110600 | tf_op jit(solution)/shard_map/ppermute | solution.py:398
  18.5 9.8 %collective-permute-start.3 = (bf16[3,48,128]{2,1,0:T(8,128)(2,1)S(1)}, bf16[3,48,128]{2,1,0:T(8,128)(2,1)S(1)}, u32[]{:S(2)}, u32[]{:S(2)}) collective-permute-start(bf16[3,48,128]{2,1,0:T(8,128)(2,1)S(1)} %get-tuple-element.24), channel_id=1, source_target_pairs={{0,48},{16,0},{32,16},{48,32},{1,49},{17,1},{33,17},{49,33},{2,50}... | collective-permute-start | bytes 110600 | tf_op jit(solution)/shard_map/ppermute | solution.py:399
  21.4 12.1 %collective-permute-start.2 = (bf16[3,48,128]{2,1,0:T(8,128)(2,1)S(1)}, bf16[3,48,128]{2,1,0:T(8,128)(2,1)S(1)}, u32[]{:S(2)}, u32[]{:S(2)}) collective-permute-start(bf16[3,48,128]{2,1,0:T(8,128)(2,1)S(1)} %get-tuple-element.24), channel_id=1, source_target_pairs={{0,32},{16,48},{32,0},{48,16},{1,33},{17,49},{33,1},{49,17},{2,34}... | collective-permute-start | bytes 110600 | tf_op jit(solution)/shard_map/ppermute | solution.py:399
  22.2 11.6 %collective-permute-start.1 = (bf16[3,48,128]{2,1,0:T(8,128)(2,1)S(1)}, bf16[3,48,128]{2,1,0:T(8,128)(2,1)S(1)}, u32[]{:S(2)}, u32[]{:S(2)}) collective-permute-start(bf16[3,48,128]{2,1,0:T(8,128)(2,1)S(1)} %get-tuple-element.24), channel_id=1, source_target_pairs={{0,16},{16,32},{32,48},{48,0},{1,17},{17,33},{33,49},{49,1},{2,18}... | collective-permute-start | bytes 110600 | tf_op jit(solution)/shard_map/ppermute | solution.py:399
  33.9 9.3 %collective-permute-start.6 = (bf16[4,3,48,128]{3,2,1,0:T(8,128)(2,1)S(1)}, bf16[4,3,48,128]{3,2,1,0:T(8,128)(2,1)S(1)}, u32[]{:S(2)}, u32[]{:S(2)}) collective-permute-start(bf16[4,3,48,128]{3,2,1,0:T(8,128)(2,1)S(1)} %pad_maximum_fusion), channel_id=1, source_target_pairs={{0,66},{1,13},{2,64},{3,15},{4,70},{5,1},{6,68},{7,3},{8,74},{9,5}... | collective-permute-start | bytes 442376 | tf_op jit(solution)/shard_map/ppermute | solution.py:383
  34.9 8.3 %collective-permute-start.5 = (bf16[4,3,48,128]{3,2,1,0:T(8,128)(2,1)S(1)}, bf16[4,3,48,128]{3,2,1,0:T(8,128)(2,1)S(1)}, u32[]{:S(2)}, u32[]{:S(2)}) collective-permute-start(bf16[4,3,48,128]{3,2,1,0:T(8,128)(2,1)S(1)} %pad_maximum_fusion), channel_id=1, source_target_pairs={{0,2},{1,9},{2,0},{3,11},{4,6},{5,13},{6,4},{7,15},{8,10},{9,1},{1... | collective-permute-start | bytes 442376 | tf_op jit(solution)/shard_map/ppermute | solution.py:383
  36.1 7.1 %collective-permute-start.4 = (bf16[4,3,48,128]{3,2,1,0:T(8,128)(2,1)S(1)}, bf16[4,3,48,128]{3,2,1,0:T(8,128)(2,1)S(1)}, u32[]{:S(2)}, u32[]{:S(2)}) collective-permute-start(bf16[4,3,48,128]{3,2,1,0:T(8,128)(2,1)S(1)} %pad_maximum_fusion), channel_id=1, source_target_pairs={{0,64},{1,5},{2,66},{3,7},{4,68},{5,9},{6,70},{7,11},{8,72},{9,13}... | collective-permute-start | bytes 442376 | tf_op jit(solution)/shard_map/ppermute | solution.py:383
  36.1 11.4 %copy-start.1 = (bf16[128,128]{1,0:T(8,128)(2,1)S(1)}, bf16[128,128]{1,0:T(8,128)(2,1)}, u32[]{:S(2)}) copy-start(bf16[128,128]{1,0:T(8,128)(2,1)} %wk_ref.3) | copy-start | bytes 98308
  36.1 11.4 %copy-start.2 = (bf16[128,128]{1,0:T(8,128)(2,1)S(1)}, bf16[128,128]{1,0:T(8,128)(2,1)}, u32[]{:S(2)}) copy-start(bf16[128,128]{1,0:T(8,128)(2,1)} %wv_ref.3) | copy-start | bytes 98308
  36.1 11.4 %copy-start.4 = (bf16[128,128]{1,0:T(8,128)(2,1)S(1)}, bf16[128,128]{1,0:T(8,128)(2,1)}, u32[]{:S(2)}) copy-start(bf16[128,128]{1,0:T(8,128)(2,1)} %wq_ref.1) | copy-start | bytes 98308
  36.1 11.4 %copy-start.5 = (bf16[128,128]{1,0:T(8,128)(2,1)S(1)}, bf16[128,128]{1,0:T(8,128)(2,1)}, u32[]{:S(2)}) copy-start(bf16[128,128]{1,0:T(8,128)(2,1)} %wg_ref.1) | copy-start | bytes 98308
  36.1 11.4 %copy-start.10 = (f32[128]{0:T(128)S(1)}, f32[128]{0:T(128)}, u32[]{:S(2)}) copy-start(f32[128]{0:T(128)} %param.20) | copy-start | bytes 1540
  39.6 10.3 %collective-permute-start.10 = (bf16[12,384,128]{2,1,0:T(8,128)(2,1)S(1)}, bf16[12,384,128]{2,1,0:T(8,128)(2,1)S(1)}, u32[]{:S(2)}, u32[]{:S(2)}) collective-permute-start(bf16[12,384,128]{2,1,0:T(8,128)(2,1)S(1)} %columns.1.cols_ref), channel_id=1, source_target_pairs={{0,1},{1,0},{2,3},{3,2},{4,5},{5,4},{6,7},{7,6},{8,9},{9,8},{10,11... | collective-permute-start | bytes 3538952 | tf_op jit(solution)/shard_map/ppermute | solution.py:404
  43.2 16.6 %collective-permute-start.9 = (bf16[16,3,48,128]{3,2,1,0:T(8,128)(2,1)S(1)}, bf16[16,3,48,128]{3,2,1,0:T(8,128)(2,1)S(1)}, u32[]{:S(2)}, u32[]{:S(2)}) collective-permute-start(bf16[16,3,48,128]{3,2,1,0:T(8,128)(2,1)S(1)} %constant_dynamic-update-slice_fusion.refs_0_), channel_id=1, source_target_pairs={{0,12},{1,67},{2,14},{3,65},{4,0},{5,71},{6,2},{7,69},{8,4},{9,75}... | collective-permute-start | bytes 1769480 | tf_op jit(solution)/shard_map/ppermute | solution.py:383
  46.0 13.8 %collective-permute-start.8 = (bf16[16,3,48,128]{3,2,1,0:T(8,128)(2,1)S(1)}, bf16[16,3,48,128]{3,2,1,0:T(8,128)(2,1)S(1)}, u32[]{:S(2)}, u32[]{:S(2)}) collective-permute-start(bf16[16,3,48,128]{3,2,1,0:T(8,128)(2,1)S(1)} %constant_dynamic-update-slice_fusion.refs_0_), channel_id=1, source_target_pairs={{0,8},{1,3},{2,10},{3,1},{4,12},{5,7},{6,14},{7,5},{8,0},{9,11},{1... | collective-permute-start | bytes 1769480 | tf_op jit(solution)/shard_map/ppermute | solution.py:383
  47.2 16.5 %collective-permute-start.7 = (bf16[16,3,48,128]{3,2,1,0:T(8,128)(2,1)S(1)}, bf16[16,3,48,128]{3,2,1,0:T(8,128)(2,1)S(1)}, u32[]{:S(2)}, u32[]{:S(2)}) collective-permute-start(bf16[16,3,48,128]{3,2,1,0:T(8,128)(2,1)S(1)} %constant_dynamic-update-slice_fusion.refs_0_), channel_id=1, source_target_pairs={{0,4},{1,65},{2,6},{3,67},{4,8},{5,69},{6,10},{7,71},{8,12},{9,73}... | collective-permute-start | bytes 1769480 | tf_op jit(solution)/shard_map/ppermute | solution.py:383
  47.5 16.2 %copy-start.3 = (bf16[128,128]{1,0:T(8,128)(2,1)S(1)}, bf16[128,128]{1,0:T(8,128)(2,1)}, u32[]{:S(2)}) copy-start(bf16[128,128]{1,0:T(8,128)(2,1)} %refs_11_.1) | copy-start | bytes 98308
  47.5 16.2 %copy-start.6 = (s32[768]{0:T(1024)S(1)}, s32[768]{0:T(1024)}, u32[]{:S(2)}) copy-start(s32[768]{0:T(1024)} %param.13) | copy-start | bytes 9220
  47.6 16.2 %copy-start.11 = (f32[128]{0:T(128)S(1)}, f32[128]{0:T(128)}, u32[]{:S(2)}) copy-start(f32[128]{0:T(128)} %param.23) | copy-start | bytes 1540

commit v8 on v7

--- a/solution.py
+++ b/solution.py
@@ -204,7 +204,7 @@
 
 
 def takes(half):
-    return (half * 19 // 24, half * 21 // 24, half * 23 // 24)
+    return tuple(half * n // 24 for n in range(19, 24))
 
 
 def attend_kernel(mask_ref, *refs):

time: 102 us -> 104 us (1.020)
  no operation moved by 1% of the time
where the time goes in v8:
time: 104 us; the launch traced here: 103 us
  waiting for transfers between devices  26.9 us (26%)
  Pallas kernels  24.7 us (24%)
  starting transfers between devices  23.9 us (23%)
  blocking collectives  22.6 us (22%)
  local copies, waits for them, and re-layouts  4.52 us (4%)
    all_to_all x1, blocking collectives, on_device(): lax.all_to_all(a, CHIPS, split_axis=0, concat_axis=0, tiled=True)  22.6 us
    pallas_call x1, Pallas kernels, attend_call(): pl.pallas_call(attend_kernel, out_shape=in_vmem((sources, rows * columns,...  15.3 us
    ppermute x6, waiting for transfers between devices, ring(): return [block] + [lax.ppermute(block, PLACES, turn) for turn in turns]  14.9 us
    all_to_all x1, starting transfers between devices, on_device(): lax.all_to_all(a, CHIPS, split_axis=0, concat_axis=0, tiled=True)  11.6 us
    ppermute x3, waiting for transfers between devices, on_device(): lax.ppermute(mixed, 'z', [(i, (i + n) % RING) for i in range(RING)])  10.8 us
    ppermute x6, starting transfers between devices, ring(): return [block] + [lax.ppermute(block, PLACES, turn) for turn in turns]  6.48 us
    ppermute x3, starting transfers between devices, on_device(): lax.ppermute(mixed, 'z', [(i, (i + n) % RING) for i in range(RING)])  4.57 us
    pallas_call x1, Pallas kernels, columns_call(): pl.pallas_call(columns_kernel, out_shape=in_vmem((columns, half, channels...  3.46 us
  transfers between devices with their start and end apart: 12, of which 7 were waited for; matrix products, arithmetic and copies ran while one was open for 0% of the time, Pallas kernels for 9%

profile of v8, /device:TPU:0, one launch (start us, length us, event | category | flops | bytes accessed | tf_op | source)
XLA Modules:
  0.0 102.9 jit_solution(16026567585262953325)
XLA Ops:
  0.0 3.0 %copy.16 = bf16[72,64,128]{2,0,1:T(8,128)(2,1)} copy(bf16[72,64,128]{2,1,0:T(8,128)(2,1)} %bitcast.20) | data formatting | bytes 2359296 | tf_op jit(solution)/shard_map/reshape | solution.py:396
  3.1 11.6 %all-to-all-start = ((bf16[64,72,128]{2,1,0:T(8,128)(2,1)}), bf16[64,72,128]{2,1,0:T(8,128)(2,1)S(1)}, u32[]{:S(2)}, u32[]{:S(2)}) async-start(bf16[64,72,128]{2,1,0:T(8,128)(2,1)} %bitcast.19), calls=%async_computation | async-start | bytes 2359296 | tf_op jit(solution)/shard_map/all_to_all | solution.py:394
  14.7 2.4 %bias_rows.1 = (bf16[3,48,128]{2,1,0:T(8,128)(2,1)S(1)}, bf16[3,48,128]{2,1,0:T(8,128)(2,1)S(1)}) custom-call(bf16[6,768,128]{2,1,0:T(8,128)(2,1)S(1)} %copy-done, f32[1,128]{1,0:T(1,128)S(1)} %bitcast.22, f32[1,128]{1,0:T(1,128)S(1)} %bitcast.24, bf16[4,128]{1,0:T(4,128)(2,1)S(1)} %bitcast.26), custom_call_target="tpu_custom_call" | custom-call | tf_op jit(solution)/shard_map/bias_rows/pallas_call | solution.py:78
  17.3 1.2 %collective-permute-done = bf16[3,48,128]{2,1,0:T(8,128)(2,1)S(1)} collective-permute-done((bf16[3,48,128]{2,1,0:T(8,128)(2,1)S(1)}, bf16[3,48,128]{2,1,0:T(8,128)(2,1)S(1)}, u32[]{:S(2)}, u32[]{:S(2)}) %collective-permute-start) | collective-permute-done | bytes 36896 | tf_op jit(solution)/shard_map/ppermute | solution.py:398
  18.5 2.9 %collective-permute-start.3 = (bf16[3,48,128]{2,1,0:T(8,128)(2,1)S(1)}, bf16[3,48,128]{2,1,0:T(8,128)(2,1)S(1)}, u32[]{:S(2)}, u32[]{:S(2)}) collective-permute-start(bf16[3,48,128]{2,1,0:T(8,128)(2,1)S(1)} %get-tuple-element.24), channel_id=1, source_target_pairs={{0,48},{16,0},{32,16},{48,32},{1,49},{17,1},{33,17},{49,33},{2,50}... | collective-permute-start | bytes 110600 | tf_op jit(solution)/shard_map/ppermute | solution.py:399
  21.4 0.8 collective-permute-start.2
  22.2 0.9 collective-permute-start.1
  23.1 5.2 %collective-permute-done.3 = bf16[3,48,128]{2,1,0:T(8,128)(2,1)S(1)} collective-permute-done((bf16[3,48,128]{2,1,0:T(8,128)(2,1)S(1)}, bf16[3,48,128]{2,1,0:T(8,128)(2,1)S(1)}, u32[]{:S(2)}, u32[]{:S(2)}) %collective-permute-start.3) | collective-permute-done | bytes 36896 | tf_op jit(solution)/shard_map/ppermute | solution.py:399
  28.3 5.1 %collective-permute-done.2 = bf16[3,48,128]{2,1,0:T(8,128)(2,1)S(1)} collective-permute-done((bf16[3,48,128]{2,1,0:T(8,128)(2,1)S(1)}, bf16[3,48,128]{2,1,0:T(8,128)(2,1)S(1)}, u32[]{:S(2)}, u32[]{:S(2)}) %collective-permute-start.2) | collective-permute-done | bytes 36896 | tf_op jit(solution)/shard_map/ppermute | solution.py:399
  33.4 0.4 collective-permute-done.1
  33.9 1.0 %collective-permute-start.6 = (bf16[4,3,48,128]{3,2,1,0:T(8,128)(2,1)S(1)}, bf16[4,3,48,128]{3,2,1,0:T(8,128)(2,1)S(1)}, u32[]{:S(2)}, u32[]{:S(2)}) collective-permute-start(bf16[4,3,48,128]{3,2,1,0:T(8,128)(2,1)S(1)} %pad_maximum_fusion), channel_id=1, source_target_pairs={{0,66},{1,13},{2,64},{3,15},{4,70},{5,1},{6,68},{7,3},{8,74},{9,5}... | collective-permute-start | bytes 442376 | tf_op jit(solution)/shard_map/ppermute | solution.py:383
  34.9 1.2 %collective-permute-start.5 = (bf16[4,3,48,128]{3,2,1,0:T(8,128)(2,1)S(1)}, bf16[4,3,48,128]{3,2,1,0:T(8,128)(2,1)S(1)}, u32[]{:S(2)}, u32[]{:S(2)}) collective-permute-start(bf16[4,3,48,128]{3,2,1,0:T(8,128)(2,1)S(1)} %pad_maximum_fusion), channel_id=1, source_target_pairs={{0,2},{1,9},{2,0},{3,11},{4,6},{5,13},{6,4},{7,15},{8,10},{9,1},{1... | collective-permute-start | bytes 442376 | tf_op jit(solution)/shard_map/ppermute | solution.py:383
  36.2 3.5 %columns.1.cols_ref = bf16[12,384,128]{2,1,0:T(8,128)(2,1)S(1)} custom-call(bf16[64,72,128]{2,1,0:T(8,128)(2,1)S(1)} %all-to-all-done.got_ref, f32[1,128]{1,0:T(1,128)S(1)} %bitcast.23, f32[1,128]{1,0:T(1,128)S(1)} %bitcast.25), custom_call_target="tpu_custom_call" | custom-call | tf_op jit(solution)/shard_map/columns/pallas_call | solution.py:117
  39.6 1.2 %collective-permute-start.10 = (bf16[12,384,128]{2,1,0:T(8,128)(2,1)S(1)}, bf16[12,384,128]{2,1,0:T(8,128)(2,1)S(1)}, u32[]{:S(2)}, u32[]{:S(2)}) collective-permute-start(bf16[12,384,128]{2,1,0:T(8,128)(2,1)S(1)} %columns.1.cols_ref), channel_id=1, source_target_pairs={{0,1},{1,0},{2,3},{3,2},{4,5},{5,4},{6,7},{7,6},{8,9},{9,8},{10,11... | collective-permute-start | bytes 3538952 | tf_op jit(solution)/shard_map/ppermute | solution.py:404
  40.8 2.3 %collective-permute-done.4 = bf16[4,3,48,128]{3,2,1,0:T(8,128)(2,1)S(1)} collective-permute-done((bf16[4,3,48,128]{3,2,1,0:T(8,128)(2,1)S(1)}, bf16[4,3,48,128]{3,2,1,0:T(8,128)(2,1)S(1)}, u32[]{:S(2)}, u32[]{:S(2)}) %collective-permute-start.4) | collective-permute-done | bytes 147488 | tf_op jit(solution)/shard_map/ppermute | solution.py:383
  43.2 2.8 %collective-permute-start.9 = (bf16[16,3,48,128]{3,2,1,0:T(8,128)(2,1)S(1)}, bf16[16,3,48,128]{3,2,1,0:T(8,128)(2,1)S(1)}, u32[]{:S(2)}, u32[]{:S(2)}) collective-permute-start(bf16[16,3,48,128]{3,2,1,0:T(8,128)(2,1)S(1)} %constant_dynamic-update-slice_fusion.refs_0_), channel_id=1, source_target_pairs={{0,12},{1,67},{2,14},{3,65},{4,0},{5,71},{6,2},{7,69},{8,4},{9,75}... | collective-permute-start | bytes 1769480 | tf_op jit(solution)/shard_map/ppermute | solution.py:383
  46.0 1.2 %collective-permute-start.8 = (bf16[16,3,48,128]{3,2,1,0:T(8,128)(2,1)S(1)}, bf16[16,3,48,128]{3,2,1,0:T(8,128)(2,1)S(1)}, u32[]{:S(2)}, u32[]{:S(2)}) collective-permute-start(bf16[16,3,48,128]{3,2,1,0:T(8,128)(2,1)S(1)} %constant_dynamic-update-slice_fusion.refs_0_), channel_id=1, source_target_pairs={{0,8},{1,3},{2,10},{3,1},{4,12},{5,7},{6,14},{7,5},{8,0},{9,11},{1... | collective-permute-start | bytes 1769480 | tf_op jit(solution)/shard_map/ppermute | solution.py:383
  47.6 2.3 %own.1 = (bf16[12,128,384]{2,1,0:T(8,128)(2,1)S(1)}, bf16[12,128,384]{2,1,0:T(8,128)(2,1)S(1)}, bf16[12,384,128]{2,1,0:T(8,128)(2,1)S(1)}, bf16[12,2,80,384]{3,2,1,0:T(8,128)(2,1)S(1)}, bf16[12,128,384]{2,1,0:T(8,128)(2,1)S(1)}) custom-call(bf16[12,384,128]{2,1,0:T(8,128)(2,1)S(1)} %columns.1.cols_ref, bf16[128,128]{1,0:T(8,128)(2,1)S(1)} %copy-done.4, ...), custom_call_target="tpu_custom_call" | custom-call | tf_op jit(solution)/shard_map/own/pallas_call | solution.py:173
  49.9 1.3 %other.1 = (bf16[12,384,128]{2,1,0:T(8,128)(2,1)S(1)}, bf16[12,2,80,384]{3,2,1,0:T(8,128)(2,1)S(1)}) custom-call(bf16[12,384,128]{2,1,0:T(8,128)(2,1)S(1)} %collective-permute-done.10.cols_ref, bf16[128,128]{1,0:T(8,128)(2,1)S(1)} %copy-done.1, bf16[128,128]{1,0:T(8,128)(2,1)S(1)} %copy-done.2), custom_call_target="tpu_custom_call" | custom-call | tf_op jit(solution)/shard_map/other/pallas_call | solution.py:196
  51.2 8.6 %collective-permute-done.9.refs_3_ = bf16[16,3,48,128]{3,2,1,0:T(8,128)(2,1)S(1)} collective-permute-done((bf16[16,3,48,128]{3,2,1,0:T(8,128)(2,1)S(1)}, bf16[16,3,48,128]{3,2,1,0:T(8,128)(2,1)S(1)}, u32[]{:S(2)}, u32[]{:S(2)}) %collective-permute-start.9) | collective-permute-done | bytes 589856 | tf_op jit(solution)/shard_map/ppermute | solution.py:383
  59.8 3.9 %collective-permute-done.7.refs_1_ = bf16[16,3,48,128]{3,2,1,0:T(8,128)(2,1)S(1)} collective-permute-done((bf16[16,3,48,128]{3,2,1,0:T(8,128)(2,1)S(1)}, bf16[16,3,48,128]{3,2,1,0:T(8,128)(2,1)S(1)}, u32[]{:S(2)}, u32[]{:S(2)}) %collective-permute-start.7) | collective-permute-done | bytes 589856 | tf_op jit(solution)/shard_map/ppermute | solution.py:383
  63.8 15.3 %attend.1 = bf16[64,72,128]{2,1,0:T(8,128)(2,1)S(1)} custom-call(s32[6,128]{1,0:T(8,128)S(1)} %bitcast.21, bf16[16,3,48,128]{3,2,1,0:T(8,128)(2,1)S(1)} %constant_dynamic-update-slice_fusion.refs_0_, bf16[16,3,48,128]{3,2,1,0:T(8,128)(2,1)S(1)} %collective-permute-done.7.refs_1_, bf16[16,3,48,128]{3,2,1,0:T(8,128)(2,1)S(1)} %collective-permute-done.8.refs_2_, ...), custom_call_target="tpu_custom_call" | custom-call | tf_op jit(solution)/shard_map/attend/pallas_call | solution.py:351
  79.0 22.6 %all_to_all.10 = bf16[64,72,128]{2,1,0:T(8,128)(2,1)S(1)} all-to-all(bf16[64,72,128]{2,1,0:T(8,128)(2,1)S(1)} %attend.1), channel_id=1, replica_groups=mesh['ylo'=2,'z'=4,'x'=4,'yhi'=2,'core'=2] {'ylo','z','x','yhi'}, dimensions={0} | all-to-all | bytes 2359296 | tf_op jit(solution)/shard_map/all_to_all | solution.py:394
  101.6 1.3 %copy.14 = bf16[72,64,128]{2,1,0:T(8,128)(2,1)} copy(bf16[72,64,128]{2,0,1:T(8,128)(2,1)S(1)} %bitcast.29) | data formatting | bytes 2359296 | tf_op jit(solution)/shard_map/transpose | solution.py:409
  (40 shorter events, 0.6 us)
Async XLA Ops:
  3.0 11.7 %copy-start = (bf16[6,768,128]{2,1,0:T(8,128)(2,1)S(1)}, bf16[6,768,128]{2,1,0:T(8,128)(2,1)}, u32[]{:S(2)}) copy-start(bf16[6,768,128]{2,1,0:T(8,128)(2,1)} %pair_ref.1) | copy-start | bytes 3538948
  3.0 11.7 %copy-start.7 = (f32[128]{0:T(128)S(1)}, f32[128]{0:T(128)}, u32[]{:S(2)}) copy-start(f32[128]{0:T(128)} %param.14) | copy-start | bytes 1540
  3.1 11.7 %copy-start.8 = (f32[128]{0:T(128)S(1)}, f32[128]{0:T(128)}, u32[]{:S(2)}) copy-start(f32[128]{0:T(128)} %param.15) | copy-start | bytes 1540
  3.1 11.7 %copy-start.9 = (bf16[128,4]{0,1:T(4,128)(2,1)S(1)}, bf16[128,4]{0,1:T(4,128)(2,1)}, u32[]{:S(2)}) copy-start(bf16[128,4]{0,1:T(4,128)(2,1)} %param.21) | copy-start | bytes 3076
  3.1 33.1 %all-to-all-start = ((bf16[64,72,128]{2,1,0:T(8,128)(2,1)}), bf16[64,72,128]{2,1,0:T(8,128)(2,1)S(1)}, u32[]{:S(2)}, u32[]{:S(2)}) async-start(bf16[64,72,128]{2,1,0:T(8,128)(2,1)} %bitcast.19), calls=%async_computation | async-start | bytes 2359296 | tf_op jit(solution)/shard_map/all_to_all | solution.py:394
  17.2 1.3 %collective-permute-start = (bf16[3,48,128]{2,1,0:T(8,128)(2,1)S(1)}, bf16[3,48,128]{2,1,0:T(8,128)(2,1)S(1)}, u32[]{:S(2)}, u32[]{:S(2)}) collective-permute-start(bf16[3,48,128]{2,1,0:T(8,128)(2,1)S(1)} %get-tuple-element.15), channel_id=1, source_target_pairs={{0,1},{1,0},{2,3},{3,2},{4,5},{5,4},{6,7},{7,6},{8,9},{9,8},{10,11... | collective-permute-start | bytes 110600 | tf_op jit(solution)/shard_map/ppermute | solution.py:398
  18.5 9.8 %collective-permute-start.3 = (bf16[3,48,128]{2,1,0:T(8,128)(2,1)S(1)}, bf16[3,48,128]{2,1,0:T(8,128)(2,1)S(1)}, u32[]{:S(2)}, u32[]{:S(2)}) collective-permute-start(bf16[3,48,128]{2,1,0:T(8,128)(2,1)S(1)} %get-tuple-element.24), channel_id=1, source_target_pairs={{0,48},{16,0},{32,16},{48,32},{1,49},{17,1},{33,17},{49,33},{2,50}... | collective-permute-start | bytes 110600 | tf_op jit(solution)/shard_map/ppermute | solution.py:399
  21.4 12.1 %collective-permute-start.2 = (bf16[3,48,128]{2,1,0:T(8,128)(2,1)S(1)}, bf16[3,48,128]{2,1,0:T(8,128)(2,1)S(1)}, u32[]{:S(2)}, u32[]{:S(2)}) collective-permute-start(bf16[3,48,128]{2,1,0:T(8,128)(2,1)S(1)} %get-tuple-element.24), channel_id=1, source_target_pairs={{0,32},{16,48},{32,0},{48,16},{1,33},{17,49},{33,1},{49,17},{2,34}... | collective-permute-start | bytes 110600 | tf_op jit(solution)/shard_map/ppermute | solution.py:399
  22.2 11.6 %collective-permute-start.1 = (bf16[3,48,128]{2,1,0:T(8,128)(2,1)S(1)}, bf16[3,48,128]{2,1,0:T(8,128)(2,1)S(1)}, u32[]{:S(2)}, u32[]{:S(2)}) collective-permute-start(bf16[3,48,128]{2,1,0:T(8,128)(2,1)S(1)} %get-tuple-element.24), channel_id=1, source_target_pairs={{0,16},{16,32},{32,48},{48,0},{1,17},{17,33},{33,49},{49,1},{2,18}... | collective-permute-start | bytes 110600 | tf_op jit(solution)/shard_map/ppermute | solution.py:399
  33.9 9.3 %collective-permute-start.6 = (bf16[4,3,48,128]{3,2,1,0:T(8,128)(2,1)S(1)}, bf16[4,3,48,128]{3,2,1,0:T(8,128)(2,1)S(1)}, u32[]{:S(2)}, u32[]{:S(2)}) collective-permute-start(bf16[4,3,48,128]{3,2,1,0:T(8,128)(2,1)S(1)} %pad_maximum_fusion), channel_id=1, source_target_pairs={{0,66},{1,13},{2,64},{3,15},{4,70},{5,1},{6,68},{7,3},{8,74},{9,5}... | collective-permute-start | bytes 442376 | tf_op jit(solution)/shard_map/ppermute | solution.py:383
  34.9 8.3 %collective-permute-start.5 = (bf16[4,3,48,128]{3,2,1,0:T(8,128)(2,1)S(1)}, bf16[4,3,48,128]{3,2,1,0:T(8,128)(2,1)S(1)}, u32[]{:S(2)}, u32[]{:S(2)}) collective-permute-start(bf16[4,3,48,128]{3,2,1,0:T(8,128)(2,1)S(1)} %pad_maximum_fusion), channel_id=1, source_target_pairs={{0,2},{1,9},{2,0},{3,11},{4,6},{5,13},{6,4},{7,15},{8,10},{9,1},{1... | collective-permute-start | bytes 442376 | tf_op jit(solution)/shard_map/ppermute | solution.py:383
  36.1 7.1 %collective-permute-start.4 = (bf16[4,3,48,128]{3,2,1,0:T(8,128)(2,1)S(1)}, bf16[4,3,48,128]{3,2,1,0:T(8,128)(2,1)S(1)}, u32[]{:S(2)}, u32[]{:S(2)}) collective-permute-start(bf16[4,3,48,128]{3,2,1,0:T(8,128)(2,1)S(1)} %pad_maximum_fusion), channel_id=1, source_target_pairs={{0,64},{1,5},{2,66},{3,7},{4,68},{5,9},{6,70},{7,11},{8,72},{9,13}... | collective-permute-start | bytes 442376 | tf_op jit(solution)/shard_map/ppermute | solution.py:383
  36.1 11.4 %copy-start.1 = (bf16[128,128]{1,0:T(8,128)(2,1)S(1)}, bf16[128,128]{1,0:T(8,128)(2,1)}, u32[]{:S(2)}) copy-start(bf16[128,128]{1,0:T(8,128)(2,1)} %wk_ref.3) | copy-start | bytes 98308
  36.1 11.4 %copy-start.2 = (bf16[128,128]{1,0:T(8,128)(2,1)S(1)}, bf16[128,128]{1,0:T(8,128)(2,1)}, u32[]{:S(2)}) copy-start(bf16[128,128]{1,0:T(8,128)(2,1)} %wv_ref.3) | copy-start | bytes 98308
  36.1 11.4 %copy-start.4 = (bf16[128,128]{1,0:T(8,128)(2,1)S(1)}, bf16[128,128]{1,0:T(8,128)(2,1)}, u32[]{:S(2)}) copy-start(bf16[128,128]{1,0:T(8,128)(2,1)} %wq_ref.1) | copy-start | bytes 98308
  36.1 11.4 %copy-start.5 = (bf16[128,128]{1,0:T(8,128)(2,1)S(1)}, bf16[128,128]{1,0:T(8,128)(2,1)}, u32[]{:S(2)}) copy-start(bf16[128,128]{1,0:T(8,128)(2,1)} %wg_ref.1) | copy-start | bytes 98308
  36.1 11.4 %copy-start.10 = (f32[128]{0:T(128)S(1)}, f32[128]{0:T(128)}, u32[]{:S(2)}) copy-start(f32[128]{0:T(128)} %param.20) | copy-start | bytes 1540
  39.6 10.3 %collective-permute-start.10 = (bf16[12,384,128]{2,1,0:T(8,128)(2,1)S(1)}, bf16[12,384,128]{2,1,0:T(8,128)(2,1)S(1)}, u32[]{:S(2)}, u32[]{:S(2)}) collective-permute-start(bf16[12,384,128]{2,1,0:T(8,128)(2,1)S(1)} %columns.1.cols_ref), channel_id=1, source_target_pairs={{0,1},{1,0},{2,3},{3,2},{4,5},{5,4},{6,7},{7,6},{8,9},{9,8},{10,11... | collective-permute-start | bytes 3538952 | tf_op jit(solution)/shard_map/ppermute | solution.py:404
  43.2 16.6 %collective-permute-start.9 = (bf16[16,3,48,128]{3,2,1,0:T(8,128)(2,1)S(1)}, bf16[16,3,48,128]{3,2,1,0:T(8,128)(2,1)S(1)}, u32[]{:S(2)}, u32[]{:S(2)}) collective-permute-start(bf16[16,3,48,128]{3,2,1,0:T(8,128)(2,1)S(1)} %constant_dynamic-update-slice_fusion.refs_0_), channel_id=1, source_target_pairs={{0,12},{1,67},{2,14},{3,65},{4,0},{5,71},{6,2},{7,69},{8,4},{9,75}... | collective-permute-start | bytes 1769480 | tf_op jit(solution)/shard_map/ppermute | solution.py:383
  46.0 13.8 %collective-permute-start.8 = (bf16[16,3,48,128]{3,2,1,0:T(8,128)(2,1)S(1)}, bf16[16,3,48,128]{3,2,1,0:T(8,128)(2,1)S(1)}, u32[]{:S(2)}, u32[]{:S(2)}) collective-permute-start(bf16[16,3,48,128]{3,2,1,0:T(8,128)(2,1)S(1)} %constant_dynamic-update-slice_fusion.refs_0_), channel_id=1, source_target_pairs={{0,8},{1,3},{2,10},{3,1},{4,12},{5,7},{6,14},{7,5},{8,0},{9,11},{1... | collective-permute-start | bytes 1769480 | tf_op jit(solution)/shard_map/ppermute | solution.py:383
  47.2 16.5 %collective-permute-start.7 = (bf16[16,3,48,128]{3,2,1,0:T(8,128)(2,1)S(1)}, bf16[16,3,48,128]{3,2,1,0:T(8,128)(2,1)S(1)}, u32[]{:S(2)}, u32[]{:S(2)}) collective-permute-start(bf16[16,3,48,128]{3,2,1,0:T(8,128)(2,1)S(1)} %constant_dynamic-update-slice_fusion.refs_0_), channel_id=1, source_target_pairs={{0,4},{1,65},{2,6},{3,67},{4,8},{5,69},{6,10},{7,71},{8,12},{9,73}... | collective-permute-start | bytes 1769480 | tf_op jit(solution)/shard_map/ppermute | solution.py:383
  47.5 16.2 %copy-start.3 = (bf16[128,128]{1,0:T(8,128)(2,1)S(1)}, bf16[128,128]{1,0:T(8,128)(2,1)}, u32[]{:S(2)}) copy-start(bf16[128,128]{1,0:T(8,128)(2,1)} %refs_11_.1) | copy-start | bytes 98308
  47.5 16.2 %copy-start.6 = (s32[768]{0:T(1024)S(1)}, s32[768]{0:T(1024)}, u32[]{:S(2)}) copy-start(s32[768]{0:T(1024)} %param.13) | copy-start | bytes 9220
  47.6 16.2 %copy-start.11 = (f32[128]{0:T(128)S(1)}, f32[128]{0:T(128)}, u32[]{:S(2)}) copy-start(f32[128]{0:T(128)} %param.23) | copy-start | bytes 1540

commit v9 on v8

--- a/solution.py
+++ b/solution.py
@@ -324,11 +324,12 @@
         below = take
 
     def padding(t, _):
-        weight = F32(1.0 / length).astype(BF).astype(F32)
+        weights = jnp.full((half, LANES), 1.0 / length, BF)
         for p in range(pairs):
-            part = jnp.sum(val0_ref[t, p, : 2 * DIM, :].astype(F32), axis=1, keepdims=True)
-            part += jnp.sum(val1_ref[t, p, : 2 * DIM, :].astype(F32), axis=1, keepdims=True)
-            att_ref[p * 2 * DIM : (p + 1) * 2 * DIM, :] = jnp.broadcast_to(part * weight, (2 * DIM, half))
+            part = jnp.dot(val0_ref[t, p, : 2 * DIM, :], weights, preferred_element_type=F32)
+            part += jnp.dot(val1_ref[t, p, : 2 * DIM, :], weights, preferred_element_type=F32)
+            for n in range(parts):
+                att_ref[p * 2 * DIM : (p + 1) * 2 * DIM, n * LANES : (n + 1) * LANES] = part
         finish(t)
         return 0
 

time: 104 us -> 104 us (level)
  no operation moved by 1% of the time
where the time goes in v9:
time: 104 us; the launch traced here: 103 us
  waiting for transfers between devices  26.9 us (26%)
  Pallas kernels  24.6 us (24%)
  starting transfers between devices  23.9 us (23%)
  blocking collectives  22.6 us (22%)
  local copies, waits for them, and re-layouts  4.52 us (4%)
    all_to_all x1, blocking collectives, on_device(): lax.all_to_all(a, CHIPS, split_axis=0, concat_axis=0, tiled=True)  22.6 us
    pallas_call x1, Pallas kernels, attend_call(): pl.pallas_call(attend_kernel, out_shape=in_vmem((sources, rows * columns,...  15.2 us
    ppermute x6, waiting for transfers between devices, ring(): return [block] + [lax.ppermute(block, PLACES, turn) for turn in turns]  14.9 us
    all_to_all x1, starting transfers between devices, on_device(): lax.all_to_all(a, CHIPS, split_axis=0, concat_axis=0, tiled=True)  11.6 us
    ppermute x3, waiting for transfers between devices, on_device(): lax.ppermute(mixed, 'z', [(i, (i + n) % RING) for i in range(RING)])  10.8 us
    ppermute x6, starting transfers between devices, ring(): return [block] + [lax.ppermute(block, PLACES, turn) for turn in turns]  6.48 us
    ppermute x3, starting transfers between devices, on_device(): lax.ppermute(mixed, 'z', [(i, (i + n) % RING) for i in range(RING)])  4.57 us
    pallas_call x1, Pallas kernels, columns_call(): pl.pallas_call(columns_kernel, out_shape=in_vmem((columns, half, channels...  3.46 us
  transfers between devices with their start and end apart: 12, of which 7 were waited for; matrix products, arithmetic and copies ran while one was open for 0% of the time, Pallas kernels for 9%

profile of v9, /device:TPU:0, one launch (start us, length us, event | category | flops | bytes accessed | tf_op | source)
XLA Modules:
  0.0 102.9 jit_solution(17376297095406335361)
XLA Ops:
  0.0 3.0 %copy.16 = bf16[72,64,128]{2,0,1:T(8,128)(2,1)} copy(bf16[72,64,128]{2,1,0:T(8,128)(2,1)} %bitcast.20) | data formatting | bytes 2359296 | tf_op jit(solution)/shard_map/reshape | solution.py:397
  3.1 11.6 %all-to-all-start = ((bf16[64,72,128]{2,1,0:T(8,128)(2,1)}), bf16[64,72,128]{2,1,0:T(8,128)(2,1)S(1)}, u32[]{:S(2)}, u32[]{:S(2)}) async-start(bf16[64,72,128]{2,1,0:T(8,128)(2,1)} %bitcast.19), calls=%async_computation | async-start | bytes 2359296 | tf_op jit(solution)/shard_map/all_to_all | solution.py:395
  14.7 2.4 %bias_rows.1 = (bf16[3,48,128]{2,1,0:T(8,128)(2,1)S(1)}, bf16[3,48,128]{2,1,0:T(8,128)(2,1)S(1)}) custom-call(bf16[6,768,128]{2,1,0:T(8,128)(2,1)S(1)} %copy-done, f32[1,128]{1,0:T(1,128)S(1)} %bitcast.22, f32[1,128]{1,0:T(1,128)S(1)} %bitcast.24, bf16[4,128]{1,0:T(4,128)(2,1)S(1)} %bitcast.26), custom_call_target="tpu_custom_call" | custom-call | tf_op jit(solution)/shard_map/bias_rows/pallas_call | solution.py:78
  17.3 1.2 %collective-permute-done = bf16[3,48,128]{2,1,0:T(8,128)(2,1)S(1)} collective-permute-done((bf16[3,48,128]{2,1,0:T(8,128)(2,1)S(1)}, bf16[3,48,128]{2,1,0:T(8,128)(2,1)S(1)}, u32[]{:S(2)}, u32[]{:S(2)}) %collective-permute-start) | collective-permute-done | bytes 36896 | tf_op jit(solution)/shard_map/ppermute | solution.py:399
  18.5 2.9 %collective-permute-start.3 = (bf16[3,48,128]{2,1,0:T(8,128)(2,1)S(1)}, bf16[3,48,128]{2,1,0:T(8,128)(2,1)S(1)}, u32[]{:S(2)}, u32[]{:S(2)}) collective-permute-start(bf16[3,48,128]{2,1,0:T(8,128)(2,1)S(1)} %get-tuple-element.24), channel_id=1, source_target_pairs={{0,48},{16,0},{32,16},{48,32},{1,49},{17,1},{33,17},{49,33},{2,50}... | collective-permute-start | bytes 110600 | tf_op jit(solution)/shard_map/ppermute | solution.py:400
  21.4 0.8 collective-permute-start.2
  22.2 0.9 collective-permute-start.1
  23.1 5.2 %collective-permute-done.3 = bf16[3,48,128]{2,1,0:T(8,128)(2,1)S(1)} collective-permute-done((bf16[3,48,128]{2,1,0:T(8,128)(2,1)S(1)}, bf16[3,48,128]{2,1,0:T(8,128)(2,1)S(1)}, u32[]{:S(2)}, u32[]{:S(2)}) %collective-permute-start.3) | collective-permute-done | bytes 36896 | tf_op jit(solution)/shard_map/ppermute | solution.py:400
  28.3 5.1 %collective-permute-done.2 = bf16[3,48,128]{2,1,0:T(8,128)(2,1)S(1)} collective-permute-done((bf16[3,48,128]{2,1,0:T(8,128)(2,1)S(1)}, bf16[3,48,128]{2,1,0:T(8,128)(2,1)S(1)}, u32[]{:S(2)}, u32[]{:S(2)}) %collective-permute-start.2) | collective-permute-done | bytes 36896 | tf_op jit(solution)/shard_map/ppermute | solution.py:400
  33.4 0.4 collective-permute-done.1
  33.9 1.0 %collective-permute-start.6 = (bf16[4,3,48,128]{3,2,1,0:T(8,128)(2,1)S(1)}, bf16[4,3,48,128]{3,2,1,0:T(8,128)(2,1)S(1)}, u32[]{:S(2)}, u32[]{:S(2)}) collective-permute-start(bf16[4,3,48,128]{3,2,1,0:T(8,128)(2,1)S(1)} %pad_maximum_fusion), channel_id=1, source_target_pairs={{0,66},{1,13},{2,64},{3,15},{4,70},{5,1},{6,68},{7,3},{8,74},{9,5}... | collective-permute-start | bytes 442376 | tf_op jit(solution)/shard_map/ppermute | solution.py:384
  34.9 1.2 %collective-permute-start.5 = (bf16[4,3,48,128]{3,2,1,0:T(8,128)(2,1)S(1)}, bf16[4,3,48,128]{3,2,1,0:T(8,128)(2,1)S(1)}, u32[]{:S(2)}, u32[]{:S(2)}) collective-permute-start(bf16[4,3,48,128]{3,2,1,0:T(8,128)(2,1)S(1)} %pad_maximum_fusion), channel_id=1, source_target_pairs={{0,2},{1,9},{2,0},{3,11},{4,6},{5,13},{6,4},{7,15},{8,10},{9,1},{1... | collective-permute-start | bytes 442376 | tf_op jit(solution)/shard_map/ppermute | solution.py:384
  36.2 3.5 %columns.1.cols_ref = bf16[12,384,128]{2,1,0:T(8,128)(2,1)S(1)} custom-call(bf16[64,72,128]{2,1,0:T(8,128)(2,1)S(1)} %all-to-all-done.got_ref, f32[1,128]{1,0:T(1,128)S(1)} %bitcast.23, f32[1,128]{1,0:T(1,128)S(1)} %bitcast.25), custom_call_target="tpu_custom_call" | custom-call | tf_op jit(solution)/shard_map/columns/pallas_call | solution.py:117
  39.6 1.2 %collective-permute-start.10 = (bf16[12,384,128]{2,1,0:T(8,128)(2,1)S(1)}, bf16[12,384,128]{2,1,0:T(8,128)(2,1)S(1)}, u32[]{:S(2)}, u32[]{:S(2)}) collective-permute-start(bf16[12,384,128]{2,1,0:T(8,128)(2,1)S(1)} %columns.1.cols_ref), channel_id=1, source_target_pairs={{0,1},{1,0},{2,3},{3,2},{4,5},{5,4},{6,7},{7,6},{8,9},{9,8},{10,11... | collective-permute-start | bytes 3538952 | tf_op jit(solution)/shard_map/ppermute | solution.py:405
  40.8 2.3 %collective-permute-done.4 = bf16[4,3,48,128]{3,2,1,0:T(8,128)(2,1)S(1)} collective-permute-done((bf16[4,3,48,128]{3,2,1,0:T(8,128)(2,1)S(1)}, bf16[4,3,48,128]{3,2,1,0:T(8,128)(2,1)S(1)}, u32[]{:S(2)}, u32[]{:S(2)}) %collective-permute-start.4) | collective-permute-done | bytes 147488 | tf_op jit(solution)/shard_map/ppermute | solution.py:384
  43.2 2.8 %collective-permute-start.9 = (bf16[16,3,48,128]{3,2,1,0:T(8,128)(2,1)S(1)}, bf16[16,3,48,128]{3,2,1,0:T(8,128)(2,1)S(1)}, u32[]{:S(2)}, u32[]{:S(2)}) collective-permute-start(bf16[16,3,48,128]{3,2,1,0:T(8,128)(2,1)S(1)} %constant_dynamic-update-slice_fusion.refs_0_), channel_id=1, source_target_pairs={{0,12},{1,67},{2,14},{3,65},{4,0},{5,71},{6,2},{7,69},{8,4},{9,75}... | collective-permute-start | bytes 1769480 | tf_op jit(solution)/shard_map/ppermute | solution.py:384
  46.0 1.2 %collective-permute-start.8 = (bf16[16,3,48,128]{3,2,1,0:T(8,128)(2,1)S(1)}, bf16[16,3,48,128]{3,2,1,0:T(8,128)(2,1)S(1)}, u32[]{:S(2)}, u32[]{:S(2)}) collective-permute-start(bf16[16,3,48,128]{3,2,1,0:T(8,128)(2,1)S(1)} %constant_dynamic-update-slice_fusion.refs_0_), channel_id=1, source_target_pairs={{0,8},{1,3},{2,10},{3,1},{4,12},{5,7},{6,14},{7,5},{8,0},{9,11},{1... | collective-permute-start | bytes 1769480 | tf_op jit(solution)/shard_map/ppermute | solution.py:384
  47.6 2.3 %own.1 = (bf16[12,128,384]{2,1,0:T(8,128)(2,1)S(1)}, bf16[12,128,384]{2,1,0:T(8,128)(2,1)S(1)}, bf16[12,384,128]{2,1,0:T(8,128)(2,1)S(1)}, bf16[12,2,80,384]{3,2,1,0:T(8,128)(2,1)S(1)}, bf16[12,128,384]{2,1,0:T(8,128)(2,1)S(1)}) custom-call(bf16[12,384,128]{2,1,0:T(8,128)(2,1)S(1)} %columns.1.cols_ref, bf16[128,128]{1,0:T(8,128)(2,1)S(1)} %copy-done.4, ...), custom_call_target="tpu_custom_call" | custom-call | tf_op jit(solution)/shard_map/own/pallas_call | solution.py:173
  49.9 1.3 %other.1 = (bf16[12,384,128]{2,1,0:T(8,128)(2,1)S(1)}, bf16[12,2,80,384]{3,2,1,0:T(8,128)(2,1)S(1)}) custom-call(bf16[12,384,128]{2,1,0:T(8,128)(2,1)S(1)} %collective-permute-done.10.cols_ref, bf16[128,128]{1,0:T(8,128)(2,1)S(1)} %copy-done.1, bf16[128,128]{1,0:T(8,128)(2,1)S(1)} %copy-done.2), custom_call_target="tpu_custom_call" | custom-call | tf_op jit(solution)/shard_map/other/pallas_call | solution.py:196
  51.2 8.6 %collective-permute-done.9.refs_3_ = bf16[16,3,48,128]{3,2,1,0:T(8,128)(2,1)S(1)} collective-permute-done((bf16[16,3,48,128]{3,2,1,0:T(8,128)(2,1)S(1)}, bf16[16,3,48,128]{3,2,1,0:T(8,128)(2,1)S(1)}, u32[]{:S(2)}, u32[]{:S(2)}) %collective-permute-start.9) | collective-permute-done | bytes 589856 | tf_op jit(solution)/shard_map/ppermute | solution.py:384
  59.8 3.9 %collective-permute-done.7.refs_1_ = bf16[16,3,48,128]{3,2,1,0:T(8,128)(2,1)S(1)} collective-permute-done((bf16[16,3,48,128]{3,2,1,0:T(8,128)(2,1)S(1)}, bf16[16,3,48,128]{3,2,1,0:T(8,128)(2,1)S(1)}, u32[]{:S(2)}, u32[]{:S(2)}) %collective-permute-start.7) | collective-permute-done | bytes 589856 | tf_op jit(solution)/shard_map/ppermute | solution.py:384
  63.8 15.2 %attend.1 = bf16[64,72,128]{2,1,0:T(8,128)(2,1)S(1)} custom-call(s32[6,128]{1,0:T(8,128)S(1)} %bitcast.21, bf16[16,3,48,128]{3,2,1,0:T(8,128)(2,1)S(1)} %constant_dynamic-update-slice_fusion.refs_0_, bf16[16,3,48,128]{3,2,1,0:T(8,128)(2,1)S(1)} %collective-permute-done.7.refs_1_, bf16[16,3,48,128]{3,2,1,0:T(8,128)(2,1)S(1)} %collective-permute-done.8.refs_2_, ...), custom_call_target="tpu_custom_call" | custom-call | tf_op jit(solution)/shard_map/attend/pallas_call | solution.py:352
  78.9 22.6 %all_to_all.10 = bf16[64,72,128]{2,1,0:T(8,128)(2,1)S(1)} all-to-all(bf16[64,72,128]{2,1,0:T(8,128)(2,1)S(1)} %attend.1), channel_id=1, replica_groups=mesh['ylo'=2,'z'=4,'x'=4,'yhi'=2,'core'=2] {'ylo','z','x','yhi'}, dimensions={0} | all-to-all | bytes 2359296 | tf_op jit(solution)/shard_map/all_to_all | solution.py:395
  101.5 1.3 %copy.14 = bf16[72,64,128]{2,1,0:T(8,128)(2,1)} copy(bf16[72,64,128]{2,0,1:T(8,128)(2,1)S(1)} %bitcast.29) | data formatting | bytes 2359296 | tf_op jit(solution)/shard_map/transpose | solution.py:410
  (40 shorter events, 0.6 us)
Async XLA Ops:
  3.0 11.7 %copy-start = (bf16[6,768,128]{2,1,0:T(8,128)(2,1)S(1)}, bf16[6,768,128]{2,1,0:T(8,128)(2,1)}, u32[]{:S(2)}) copy-start(bf16[6,768,128]{2,1,0:T(8,128)(2,1)} %pair_ref.1) | copy-start | bytes 3538948
  3.0 11.7 %copy-start.7 = (f32[128]{0:T(128)S(1)}, f32[128]{0:T(128)}, u32[]{:S(2)}) copy-start(f32[128]{0:T(128)} %param.14) | copy-start | bytes 1540
  3.1 11.7 %copy-start.8 = (f32[128]{0:T(128)S(1)}, f32[128]{0:T(128)}, u32[]{:S(2)}) copy-start(f32[128]{0:T(128)} %param.15) | copy-start | bytes 1540
  3.1 11.7 %copy-start.9 = (bf16[128,4]{0,1:T(4,128)(2,1)S(1)}, bf16[128,4]{0,1:T(4,128)(2,1)}, u32[]{:S(2)}) copy-start(bf16[128,4]{0,1:T(4,128)(2,1)} %param.21) | copy-start | bytes 3076
  3.1 33.1 %all-to-all-start = ((bf16[64,72,128]{2,1,0:T(8,128)(2,1)}), bf16[64,72,128]{2,1,0:T(8,128)(2,1)S(1)}, u32[]{:S(2)}, u32[]{:S(2)}) async-start(bf16[64,72,128]{2,1,0:T(8,128)(2,1)} %bitcast.19), calls=%async_computation | async-start | bytes 2359296 | tf_op jit(solution)/shard_map/all_to_all | solution.py:395
  17.2 1.3 %collective-permute-start = (bf16[3,48,128]{2,1,0:T(8,128)(2,1)S(1)}, bf16[3,48,128]{2,1,0:T(8,128)(2,1)S(1)}, u32[]{:S(2)}, u32[]{:S(2)}) collective-permute-start(bf16[3,48,128]{2,1,0:T(8,128)(2,1)S(1)} %get-tuple-element.15), channel_id=1, source_target_pairs={{0,1},{1,0},{2,3},{3,2},{4,5},{5,4},{6,7},{7,6},{8,9},{9,8},{10,11... | collective-permute-start | bytes 110600 | tf_op jit(solution)/shard_map/ppermute | solution.py:399
  18.5 9.8 %collective-permute-start.3 = (bf16[3,48,128]{2,1,0:T(8,128)(2,1)S(1)}, bf16[3,48,128]{2,1,0:T(8,128)(2,1)S(1)}, u32[]{:S(2)}, u32[]{:S(2)}) collective-permute-start(bf16[3,48,128]{2,1,0:T(8,128)(2,1)S(1)} %get-tuple-element.24), channel_id=1, source_target_pairs={{0,48},{16,0},{32,16},{48,32},{1,49},{17,1},{33,17},{49,33},{2,50}... | collective-permute-start | bytes 110600 | tf_op jit(solution)/shard_map/ppermute | solution.py:400
  21.4 12.1 %collective-permute-start.2 = (bf16[3,48,128]{2,1,0:T(8,128)(2,1)S(1)}, bf16[3,48,128]{2,1,0:T(8,128)(2,1)S(1)}, u32[]{:S(2)}, u32[]{:S(2)}) collective-permute-start(bf16[3,48,128]{2,1,0:T(8,128)(2,1)S(1)} %get-tuple-element.24), channel_id=1, source_target_pairs={{0,32},{16,48},{32,0},{48,16},{1,33},{17,49},{33,1},{49,17},{2,34}... | collective-permute-start | bytes 110600 | tf_op jit(solution)/shard_map/ppermute | solution.py:400
  22.2 11.6 %collective-permute-start.1 = (bf16[3,48,128]{2,1,0:T(8,128)(2,1)S(1)}, bf16[3,48,128]{2,1,0:T(8,128)(2,1)S(1)}, u32[]{:S(2)}, u32[]{:S(2)}) collective-permute-start(bf16[3,48,128]{2,1,0:T(8,128)(2,1)S(1)} %get-tuple-element.24), channel_id=1, source_target_pairs={{0,16},{16,32},{32,48},{48,0},{1,17},{17,33},{33,49},{49,1},{2,18}... | collective-permute-start | bytes 110600 | tf_op jit(solution)/shard_map/ppermute | solution.py:400
  33.9 9.3 %collective-permute-start.6 = (bf16[4,3,48,128]{3,2,1,0:T(8,128)(2,1)S(1)}, bf16[4,3,48,128]{3,2,1,0:T(8,128)(2,1)S(1)}, u32[]{:S(2)}, u32[]{:S(2)}) collective-permute-start(bf16[4,3,48,128]{3,2,1,0:T(8,128)(2,1)S(1)} %pad_maximum_fusion), channel_id=1, source_target_pairs={{0,66},{1,13},{2,64},{3,15},{4,70},{5,1},{6,68},{7,3},{8,74},{9,5}... | collective-permute-start | bytes 442376 | tf_op jit(solution)/shard_map/ppermute | solution.py:384
  34.9 8.3 %collective-permute-start.5 = (bf16[4,3,48,128]{3,2,1,0:T(8,128)(2,1)S(1)}, bf16[4,3,48,128]{3,2,1,0:T(8,128)(2,1)S(1)}, u32[]{:S(2)}, u32[]{:S(2)}) collective-permute-start(bf16[4,3,48,128]{3,2,1,0:T(8,128)(2,1)S(1)} %pad_maximum_fusion), channel_id=1, source_target_pairs={{0,2},{1,9},{2,0},{3,11},{4,6},{5,13},{6,4},{7,15},{8,10},{9,1},{1... | collective-permute-start | bytes 442376 | tf_op jit(solution)/shard_map/ppermute | solution.py:384
  36.1 7.1 %collective-permute-start.4 = (bf16[4,3,48,128]{3,2,1,0:T(8,128)(2,1)S(1)}, bf16[4,3,48,128]{3,2,1,0:T(8,128)(2,1)S(1)}, u32[]{:S(2)}, u32[]{:S(2)}) collective-permute-start(bf16[4,3,48,128]{3,2,1,0:T(8,128)(2,1)S(1)} %pad_maximum_fusion), channel_id=1, source_target_pairs={{0,64},{1,5},{2,66},{3,7},{4,68},{5,9},{6,70},{7,11},{8,72},{9,13}... | collective-permute-start | bytes 442376 | tf_op jit(solution)/shard_map/ppermute | solution.py:384
  36.1 11.4 %copy-start.1 = (bf16[128,128]{1,0:T(8,128)(2,1)S(1)}, bf16[128,128]{1,0:T(8,128)(2,1)}, u32[]{:S(2)}) copy-start(bf16[128,128]{1,0:T(8,128)(2,1)} %wk_ref.3) | copy-start | bytes 98308
  36.1 11.4 %copy-start.2 = (bf16[128,128]{1,0:T(8,128)(2,1)S(1)}, bf16[128,128]{1,0:T(8,128)(2,1)}, u32[]{:S(2)}) copy-start(bf16[128,128]{1,0:T(8,128)(2,1)} %wv_ref.3) | copy-start | bytes 98308
  36.1 11.4 %copy-start.4 = (bf16[128,128]{1,0:T(8,128)(2,1)S(1)}, bf16[128,128]{1,0:T(8,128)(2,1)}, u32[]{:S(2)}) copy-start(bf16[128,128]{1,0:T(8,128)(2,1)} %wq_ref.1) | copy-start | bytes 98308
  36.1 11.4 %copy-start.5 = (bf16[128,128]{1,0:T(8,128)(2,1)S(1)}, bf16[128,128]{1,0:T(8,128)(2,1)}, u32[]{:S(2)}) copy-start(bf16[128,128]{1,0:T(8,128)(2,1)} %wg_ref.1) | copy-start | bytes 98308
  36.1 11.4 %copy-start.10 = (f32[128]{0:T(128)S(1)}, f32[128]{0:T(128)}, u32[]{:S(2)}) copy-start(f32[128]{0:T(128)} %param.20) | copy-start | bytes 1540
  39.6 10.3 %collective-permute-start.10 = (bf16[12,384,128]{2,1,0:T(8,128)(2,1)S(1)}, bf16[12,384,128]{2,1,0:T(8,128)(2,1)S(1)}, u32[]{:S(2)}, u32[]{:S(2)}) collective-permute-start(bf16[12,384,128]{2,1,0:T(8,128)(2,1)S(1)} %columns.1.cols_ref), channel_id=1, source_target_pairs={{0,1},{1,0},{2,3},{3,2},{4,5},{5,4},{6,7},{7,6},{8,9},{9,8},{10,11... | collective-permute-start | bytes 3538952 | tf_op jit(solution)/shard_map/ppermute | solution.py:405
  43.2 16.6 %collective-permute-start.9 = (bf16[16,3,48,128]{3,2,1,0:T(8,128)(2,1)S(1)}, bf16[16,3,48,128]{3,2,1,0:T(8,128)(2,1)S(1)}, u32[]{:S(2)}, u32[]{:S(2)}) collective-permute-start(bf16[16,3,48,128]{3,2,1,0:T(8,128)(2,1)S(1)} %constant_dynamic-update-slice_fusion.refs_0_), channel_id=1, source_target_pairs={{0,12},{1,67},{2,14},{3,65},{4,0},{5,71},{6,2},{7,69},{8,4},{9,75}... | collective-permute-start | bytes 1769480 | tf_op jit(solution)/shard_map/ppermute | solution.py:384
  46.0 13.8 %collective-permute-start.8 = (bf16[16,3,48,128]{3,2,1,0:T(8,128)(2,1)S(1)}, bf16[16,3,48,128]{3,2,1,0:T(8,128)(2,1)S(1)}, u32[]{:S(2)}, u32[]{:S(2)}) collective-permute-start(bf16[16,3,48,128]{3,2,1,0:T(8,128)(2,1)S(1)} %constant_dynamic-update-slice_fusion.refs_0_), channel_id=1, source_target_pairs={{0,8},{1,3},{2,10},{3,1},{4,12},{5,7},{6,14},{7,5},{8,0},{9,11},{1... | collective-permute-start | bytes 1769480 | tf_op jit(solution)/shard_map/ppermute | solution.py:384
  47.2 16.5 %collective-permute-start.7 = (bf16[16,3,48,128]{3,2,1,0:T(8,128)(2,1)S(1)}, bf16[16,3,48,128]{3,2,1,0:T(8,128)(2,1)S(1)}, u32[]{:S(2)}, u32[]{:S(2)}) collective-permute-start(bf16[16,3,48,128]{3,2,1,0:T(8,128)(2,1)S(1)} %constant_dynamic-update-slice_fusion.refs_0_), channel_id=1, source_target_pairs={{0,4},{1,65},{2,6},{3,67},{4,8},{5,69},{6,10},{7,71},{8,12},{9,73}... | collective-permute-start | bytes 1769480 | tf_op jit(solution)/shard_map/ppermute | solution.py:384
  47.5 16.2 %copy-start.3 = (bf16[128,128]{1,0:T(8,128)(2,1)S(1)}, bf16[128,128]{1,0:T(8,128)(2,1)}, u32[]{:S(2)}) copy-start(bf16[128,128]{1,0:T(8,128)(2,1)} %refs_11_.1) | copy-start | bytes 98308
  47.5 16.2 %copy-start.6 = (s32[768]{0:T(1024)S(1)}, s32[768]{0:T(1024)}, u32[]{:S(2)}) copy-start(s32[768]{0:T(1024)} %param.13) | copy-start | bytes 9220
  47.6 16.2 %copy-start.11 = (f32[128]{0:T(128)S(1)}, f32[128]{0:T(128)}, u32[]{:S(2)}) copy-start(f32[128]{0:T(128)} %param.23) | copy-start | bytes 1540
